TPU v7x, 128 devices: a whole 4x4x4 slice. The times are simulated.
128 devices in a mesh: gx: 16 (over x, y), gy: 8 (over z, core).
Axes of the slice: x: 4, y: 4, z: 4, core: 2. Of those that a mesh axis runs over, the one named last changes fastest.
Arguments:
- rhs_loads: float32 [3, 128, 256, 768], P(None, 'gx', 'gy'), may hold values from -16 to 16
- flags: int32 [16, 32, 96], P('gx', 'gy'), may hold values from 0 to 1
- fixed: int32 [128, 256], P('gx', 'gy'), may hold values from 0 to 1, as said below
Outputs:
- adjoint: float32 [3, 128, 256, 768], P(None, 'gx', 'gy')
- residual: float32 [3, 128, 256, 768], P(None, 'gx', 'gy')
Inputs may be any that keep to these rules, and one draw needn't show every extreme that they name: `fixed`: every copy of a shared node holds the same value.
All inputs are finite; a program needn't handle non-finite values.
Results may differ from a plain program's by a relative error of at most 0.0027.
Values sent between devices are 32-bit elements; how exact they have to be, the bound alone decides.
No kernel may reach another device: no remote copies, remote signals or barrier semaphores. Data moves between devices by JAX's collectives and lax.ppermute only.
A program may use at most 64 MiB of HBM per device.

v0:
```python
import math

import jax
import jax.numpy as jnp
import numpy as np
from jax import lax
from jax.sharding import PartitionSpec as P

ORDER = 7
ITERS = 2


POISSON = 0.3
LAME_FIRST = POISSON / ((1.0 + POISSON) * (1.0 - 2.0 * POISSON))
LAME_SHEAR = 1.0 / (2.0 * (1.0 + POISSON))
SOLID_MODULUS = 0.1
VOID_MODULUS = 0.001
HIGHEST = lax.Precision.HIGHEST
INTERIOR_POINTS = (
    -0.8717401485096066,
    -0.5917001814331423,
    -0.2092992179024789,
    0.2092992179024789,
    0.5917001814331423,
    0.8717401485096066,
)


def with_halo(block, sides, width):
    for axis, dim in sides:
        count = lax.axis_size(axis)
        forward = [(i, i + 1) for i in range(count - 1)]
        backward = [(target, source) for source, target in forward]
        low = lax.ppermute(
            lax.slice_in_dim(block, block.shape[dim] - width, None, axis=dim), axis, forward
        )
        high = lax.ppermute(lax.slice_in_dim(block, 0, width, axis=dim), axis, backward)
        block = jnp.concatenate([low, block, high], axis=dim)
    return block


def legendre_value(poly_order, point):
    previous = 1.0
    current = point
    for degree in range(1, poly_order):
        following = ((2.0 * degree + 1.0) * point * current - degree * previous) / (degree + 1.0)
        previous = current
        current = following
    return current


def gll_tables(poly_order):
    points = np.array([-1.0] + list(INTERIOR_POINTS) + [1.0])
    values = np.array([legendre_value(poly_order, float(point)) for point in points])
    weights = 2.0 / (poly_order * (poly_order + 1) * values**2)
    node_count = poly_order + 1
    derivative = np.zeros((node_count, node_count))
    for row_index in range(node_count):
        for col_index in range(node_count):
            if row_index != col_index:
                derivative[row_index, col_index] = values[row_index] / (
                    values[col_index] * (points[row_index] - points[col_index])
                )
    derivative[0, 0] = -poly_order * (poly_order + 1) / 4.0
    derivative[poly_order, poly_order] = poly_order * (poly_order + 1) / 4.0
    return (derivative, weights)


def shared_halves(local_len, offset, global_len, node_count):
    position = jnp.arange(local_len, dtype=jnp.int32)
    node_index = position % node_count
    global_pos = position + offset
    shared = (node_index == 0) & (global_pos > 0) | (node_index == node_count - 1) & (
        global_pos < global_len - 1
    )
    return jnp.where(shared, 0.5, 1.0).astype(jnp.float32)


def pair_core(padded, which_dim, node_count):
    inner_len = padded.shape[which_dim] - 2
    middle = lax.slice_in_dim(padded, 1, inner_len + 1, axis=which_dim)
    ahead = lax.slice_in_dim(padded, 2, inner_len + 2, axis=which_dim)
    behind = lax.slice_in_dim(padded, 0, inner_len, axis=which_dim)
    node_index = jnp.arange(inner_len) % node_count
    view_shape = tuple(
        (inner_len if dim_index == which_dim else 1 for dim_index in range(padded.ndim))
    )
    upper_node = (node_index == node_count - 1).reshape(view_shape)
    lower_node = (node_index == 0).reshape(view_shape)
    return middle + jnp.where(upper_node, ahead, 0.0) + jnp.where(lower_node, behind, 0.0)


def local(rhs_loads, flags, fixed):
    node_count = ORDER + 1
    size_x = rhs_loads.shape[1]
    size_y = rhs_loads.shape[2]
    size_z = rhs_loads.shape[3]
    derivative_np, weights_np = gll_tables(ORDER)
    derivative = jnp.asarray(derivative_np, jnp.float32)
    tile_len = math.gcd(size_z, 128)
    z_matrix = jnp.asarray(np.kron(np.eye(tile_len // node_count), derivative_np.T), jnp.float32)
    weight_x = jnp.asarray(np.tile(weights_np, size_x // node_count), jnp.float32)
    weight_y = jnp.asarray(np.tile(weights_np, size_y // node_count), jnp.float32)
    weight_z = jnp.asarray(np.tile(weights_np, size_z // node_count), jnp.float32)
    weight_nodes = weight_x[:, None, None] * weight_y[None, :, None] * weight_z[None, None, :]
    modulus = jnp.where(flags == 1, SOLID_MODULUS, VOID_MODULUS).astype(jnp.float32)
    modulus = jnp.repeat(
        jnp.repeat(jnp.repeat(modulus, node_count, axis=0), node_count, axis=1), node_count, axis=2
    )
    shear_nodes = modulus * LAME_SHEAR * weight_nodes
    lame_nodes = modulus * LAME_FIRST * weight_nodes
    free = (
        1.0
        - fixed.astype(jnp.float32)[:, :, None]
        * (jnp.arange(size_z) == 0).astype(jnp.float32)[None, None, :]
    )
    inverse_mult = (
        shared_halves(
            size_x, lax.axis_index("gx") * size_x, size_x * lax.axis_size("gx"), node_count
        )[:, None, None]
        * shared_halves(
            size_y, lax.axis_index("gy") * size_y, size_y * lax.axis_size("gy"), node_count
        )[None, :, None]
        * shared_halves(size_z, 0, size_z, node_count)[None, None, :]
    )

    def derive(values_in, which_dim):
        if which_dim == 0:
            split = values_in.reshape(3, size_x // node_count, node_count, size_y, size_z)
            result = jnp.einsum("ai,xeiyz->xeayz", derivative, split, precision=HIGHEST)
        elif which_dim == 1:
            split = values_in.reshape(3, size_x, size_y // node_count, node_count, size_z)
            result = jnp.einsum("bj,xpfjz->xpfbz", derivative, split, precision=HIGHEST)
        else:
            split = values_in.reshape(3, size_x, size_y, size_z // tile_len, tile_len)
            result = jnp.einsum("xpqsk,kc->xpqsc", split, z_matrix, precision=HIGHEST)
        return result.reshape(3, size_x, size_y, size_z)

    def assemble(values_in):
        padded = with_halo(values_in, (("gx", 1), ("gy", 2)), 1)
        along_y = pair_core(pair_core(padded, 1, node_count), 2, node_count)
        padded_z = jnp.pad(along_y, ((0, 0), (0, 0), (0, 0), (1, 1)))
        return free[None] * pair_core(padded_z, 3, node_count)

    def inner_local(first, second):
        return jnp.sum(first * second * inverse_mult[None])

    loads = assemble(rhs_loads)
    adjoint = jnp.zeros_like(loads)
    residual = loads

    def squares(values_in):
        return lax.psum(inner_local(values_in, values_in), ("gx", "gy"))

    direction = loads
    norm_now = squares(residual)
    for turn_index in range(ITERS):
        stiffness_values_in = direction
        gradients = [
            derive(stiffness_values_in, 0),
            derive(stiffness_values_in, 1),
            derive(stiffness_values_in, 2),
        ]
        spread = gradients[0][0] + gradients[1][1] + gradients[2][2]
        summed = jnp.zeros_like(stiffness_values_in)
        for stiffness_direction in range(3):
            mirror = jnp.stack(
                [
                    gradients[0][stiffness_direction],
                    gradients[1][stiffness_direction],
                    gradients[2][stiffness_direction],
                ]
            )
            stress = shear_nodes * (gradients[stiffness_direction] + mirror)
            stress = stress.at[stiffness_direction].add(lame_nodes * spread)
            if stiffness_direction == 0:
                derive_split = stress.reshape(3, size_x // node_count, node_count, size_y, size_z)
                derive_result = jnp.einsum(
                    "ai,xeayz->xeiyz", derivative, derive_split, precision=HIGHEST
                )
            elif stiffness_direction == 1:
                derive_split = stress.reshape(3, size_x, size_y // node_count, node_count, size_z)
                derive_result = jnp.einsum(
                    "bj,xpfbz->xpfjz", derivative, derive_split, precision=HIGHEST
                )
            else:
                derive_split = stress.reshape(3, size_x, size_y, size_z // tile_len, tile_len)
                derive_result = jnp.einsum(
                    "xpqsc,kc->xpqsk", derive_split, z_matrix, precision=HIGHEST
                )
            summed = summed + derive_result.reshape(3, size_x, size_y, size_z)
        image_vec = assemble(summed)
        step_size = norm_now / lax.psum(inner_local(direction, image_vec), ("gx", "gy"))
        adjoint = adjoint + step_size * direction
        residual = residual - step_size * image_vec
        if turn_index + 1 < ITERS:
            norm_next = squares(residual)
            direction = residual + norm_next / norm_now * direction
            norm_now = norm_next
    return (adjoint, residual)


def solution(mesh):
    in_specs = (P(None, "gx", "gy", None), P("gx", "gy", None), P("gx", "gy"))
    out_specs = (P(None, "gx", "gy", None), P(None, "gx", "gy", None))
    return jax.shard_map(local, mesh=mesh, in_specs=in_specs, out_specs=out_specs, check_vma=False)
```

profile of v0, /device:TPU:1, one launch (start us, length us, event | category | flops | bytes accessed | tf_op | source)
XLA Modules:
  0.0 367.4 jit_solution(9052134638156317531)
XLA Ops:
  5.1 5.4 %collective-permute-start = (f32[3,1,32,768]{3,1,2,0:T(1,128)}, f32[3,1,32,768]{3,1,2,0:T(1,128)}, u32[]{:S(2)}, u32[]{:S(2)}) collective-permute-start(f32[3,1,32,768]{3,1,2,0:T(1,128)} %copy.105), channel_id=1, source_target_pairs={{0,8},{8,16},{16,24},{24,32},{32,40},{40,48},{48,56},{56,64},{64,7... | collective-permute-start | bytes 884744 | tf_op jit(solution)/shard_map/ppermute | solution.py:34
  15.1 3.0 copy.107
  20.8 4.8 %collective-permute-start.2 = (f32[3,10,1,768]{3,1,2,0:T(8,128)S(1)}, f32[3,10,1,768]{3,1,2,0:T(8,128)S(1)}, u32[]{:S(2)}, u32[]{:S(2)}) collective-permute-start(f32[3,10,1,768]{3,1,2,0:T(8,128)S(1)} %get-tuple-element.97), channel_id=1, source_target_pairs={{0,1},{1,2},{2,3},{3,4},{4,5},{5,6},{6,7},{8,9},{9,10},{10,11},{11... | collective-permute-start | bytes 276488 | tf_op jit(solution)/shard_map/ppermute | solution.py:34
  27.7 4.4 %collective-permute-done.3 = f32[3,10,1,768]{3,1,2,0:T(8,128)S(1)} collective-permute-done((f32[3,10,1,768]{3,1,2,0:T(8,128)S(1)}, f32[3,10,1,768]{3,1,2,0:T(8,128)S(1)}, u32[]{:S(2)}, u32[]{:S(2)}) %collective-permute-start.3) | collective-permute-done | bytes 92192 | tf_op jit(solution)/shard_map/ppermute | solution.py:37
  32.1 2.4 pad_maximum_fusion
  37.1 2.8 fusion.57
  46.4 2.6 fusion.49
  55.6 2.1 fusion.101
  57.8 3.0 fusion.60
  64.5 2.5 collective-permute-start.4
  68.3 2.8 collective-permute-done.4
  71.1 4.1 %collective-permute-done.5 = f32[3,1,32,768]{3,1,2,0:T(1,128)S(1)} collective-permute-done((f32[3,1,32,768]{3,1,2,0:T(1,128)S(1)}, f32[3,1,32,768]{3,1,2,0:T(1,128)S(1)}, u32[]{:S(2)}, u32[]{:S(2)}) %collective-permute-start.5) | collective-permute-done | bytes 294944 | tf_op jit(solution)/shard_map/ppermute | solution.py:37
  75.2 4.7 %collective-permute-start.6 = (f32[3,10,1,768]{3,1,2,0:T(8,128)S(1)}, f32[3,10,1,768]{3,1,2,0:T(8,128)S(1)}, u32[]{:S(2)}, u32[]{:S(2)}) collective-permute-start(f32[3,10,1,768]{3,1,2,0:T(8,128)S(1)} %get-tuple-element.95), channel_id=1, source_target_pairs={{0,1},{1,2},{2,3},{3,4},{4,5},{5,6},{6,7},{8,9},{9,10},{10,11},{11... | collective-permute-start | bytes 276488 | tf_op jit(solution)/shard_map/ppermute | solution.py:34
  82.0 4.4 %collective-permute-done.7 = f32[3,10,1,768]{3,1,2,0:T(8,128)S(1)} collective-permute-done((f32[3,10,1,768]{3,1,2,0:T(8,128)S(1)}, f32[3,10,1,768]{3,1,2,0:T(8,128)S(1)}, u32[]{:S(2)}, u32[]{:S(2)}) %collective-permute-start.7) | collective-permute-done | bytes 92192 | tf_op jit(solution)/shard_map/ppermute | solution.py:37
  88.6 4.7 %multiply_reduce_fusion.2 = (f32[]{:T(128)}, f32[]{:T(128)}, f32[3,8,32,768]{3,1,2,0:T(8,128)}) fusion(f32[8,32,768]{2,0,1:T(8,128)S(1)} %get-tuple-element.145, pred[768]{0:T(1024)(128)(4,1)S(1)} %copy-done.9, f32[3,8,32,768]{3,1,2,0:T(8,128)S(1)} %fusion.23, pred[768]{0:T(1024)(128)(4,1)S(1)} %copy-done.10, f32[8,32,768]{2,0,1:T(8,128)S(1)} %get-tuple-element.144, ...), kind=kLoop, calls=%fused_computation.88 | loop fusion | flops 9437182 | bytes 8652296 | tf_op jit(solution)/shard_map/reduce_sum | solution.py:146
  93.3 68.9 %all-reduce.3 = (f32[]{:T(128)}, f32[]{:T(128)}) all-reduce(f32[]{:T(128)} %get-tuple-element.81, f32[]{:T(128)} %get-tuple-element.80), channel_id=1, replica_groups=mesh['gx'=16,'gy'=8] {'gx','gy'}, use_global_device_ids=true, to_apply=%region_1.2 | all-reduce | flops 2 | bytes 16 | tf_op jit(solution)/shard_map/psum | solution.py:153
  163.5 3.8 %multiply_reduce_fusion.1 = f32[]{:T(128)} fusion(f32[8,32,768]{2,0,1:T(8,128)} %copy-done.3, f32[3,8,32,768]{3,1,2,0:T(8,128)} %get-tuple-element.88, f32[]{:T(128)S(6)} %div.9, pred[768]{0:T(1024)(128)(4,1)S(1)} %copy-done.9, f32[3,8,32,768]{3,1,2,0:T(8,128)S(1)} %fusion.25, pred[768]{0:T(1024)(128)(4,1)S(1)} %copy-done.10, ...), kind=kLoop, calls=%fused_computation.86 | loop fusion | flops 5898239 | bytes 6293000 | tf_op jit(solution)/shard_map/reduce_sum | solution.py:146
  167.3 64.5 %psum.30 = f32[]{:T(128)} all-reduce(f32[]{:T(128)} %multiply_reduce_fusion.1), channel_id=1, replica_groups=mesh['gx'=16,'gy'=8] {'gx','gy'}, use_global_device_ids=true, to_apply=%region_5.6 | all-reduce | flops 1 | bytes 8 | tf_op jit(solution)/shard_map/psum | solution.py:153
  233.1 3.0 multiply_add_fusion.1
  238.1 2.7 fusion.63
  242.5 2.5 fusion.43
  256.3 2.7 fusion.66
  260.4 2.2 fusion.35
  265.6 4.5 %collective-permute-done.8 = f32[3,1,32,768]{3,1,2,0:T(1,128)S(1)} collective-permute-done((f32[3,1,32,768]{3,1,2,0:T(1,128)S(1)}, f32[3,1,32,768]{3,1,2,0:T(1,128)S(1)}, u32[]{:S(2)}, u32[]{:S(2)}) %collective-permute-start.8) | collective-permute-done | bytes 294944 | tf_op jit(solution)/shard_map/ppermute | solution.py:34
  270.1 4.0 %collective-permute-done.9 = f32[3,1,32,768]{3,1,2,0:T(1,128)S(1)} collective-permute-done((f32[3,1,32,768]{3,1,2,0:T(1,128)S(1)}, f32[3,1,32,768]{3,1,2,0:T(1,128)S(1)}, u32[]{:S(2)}, u32[]{:S(2)}) %collective-permute-start.9) | collective-permute-done | bytes 294944 | tf_op jit(solution)/shard_map/ppermute | solution.py:37
  274.2 4.1 %collective-permute-start.10 = (f32[3,10,1,768]{3,1,2,0:T(8,128)S(1)}, f32[3,10,1,768]{3,1,2,0:T(8,128)S(1)}, u32[]{:S(2)}, u32[]{:S(2)}) collective-permute-start(f32[3,10,1,768]{3,1,2,0:T(8,128)S(1)} %get-tuple-element.93), channel_id=1, source_target_pairs={{0,1},{1,2},{2,3},{3,4},{4,5},{5,6},{6,7},{8,9},{9,10},{10,11},{11... | collective-permute-start | bytes 276488 | tf_op jit(solution)/shard_map/ppermute | solution.py:34
  280.4 4.4 %collective-permute-done.11 = f32[3,10,1,768]{3,1,2,0:T(8,128)S(1)} collective-permute-done((f32[3,10,1,768]{3,1,2,0:T(8,128)S(1)}, f32[3,10,1,768]{3,1,2,0:T(8,128)S(1)}, u32[]{:S(2)}, u32[]{:S(2)}) %collective-permute-start.11) | collective-permute-done | bytes 92192 | tf_op jit(solution)/shard_map/ppermute | solution.py:37
  287.6 3.4 multiply_reduce_fusion
  291.0 66.2 %psum.31 = f32[]{:T(128)} all-reduce(f32[]{:T(128)} %get-tuple-element.84), channel_id=1, replica_groups=mesh['gx'=16,'gy'=8] {'gx','gy'}, use_global_device_ids=true, to_apply=%region_7.8 | all-reduce | flops 1 | bytes 8 | tf_op jit(solution)/shard_map/psum | solution.py:193
  358.5 4.4 %multiply_subtract_fusion = (f32[3,8,32,768]{3,1,2,0:T(8,128)S(1)}, f32[3,8,32,768]{3,1,2,0:T(8,128)S(1)}) fusion(f32[3,8,32,768]{3,1,2,0:T(8,128)} %get-tuple-element.85, f32[]{:T(128)S(6)} %div.11, f32[3,8,32,768]{3,1,2,0:T(8,128)} %get-tuple-element.88, f32[]{:T(128)S(6)} %div.9, f32[3,8,32,768]{3,1,2,0:T(8,128)} %copy-done, ...), kind=kLoop, calls=%fused_computation.82 | loop fusion | flops 7077888 | bytes 14943752 | tf_op jit(solution)/shard_map/sub | solution.py:195
  362.9 2.1 copy.152
  365.0 2.1 copy.151
  (142 shorter events, 62.5 us)
Async XLA Ops:
  0.6 12.8 %copy-start.25 = (f32[32]{0:T(128)S(1)}, f32[32]{0:T(128)}, u32[]{:S(2)}) copy-start(f32[32]{0:T(128)} %constant.270.clone) | copy-start | bytes 388
  0.6 12.8 %copy-start.26 = (f32[8]{0:T(128)S(1)}, f32[8]{0:T(128)}, u32[]{:S(2)}) copy-start(f32[8]{0:T(128)} %constant.269.clone) | copy-start | bytes 100
  0.7 12.9 %copy-start.13 = (f32[768]{0:T(1024)S(1)}, f32[768]{0:T(1024)}, u32[]{:S(2)}) copy-start(f32[768]{0:T(1024)} %constant.271.clone) | copy-start | bytes 9220
  0.7 11.6 %copy-start.24 = (s32[1,4,96]{2,1,0:T(4,128)S(1)}, s32[1,4,96]{2,1,0:T(4,128)}, u32[]{:S(2)}) copy-start(s32[1,4,96]{2,1,0:T(4,128)} %param.21) | copy-start | bytes 4612
  2.8 17.1 %collective-permute-start.1 = (f32[3,1,32,768]{3,1,2,0:T(1,128)}, f32[3,1,32,768]{3,1,2,0:T(1,128)S(1)}, u32[]{:S(2)}, u32[]{:S(2)}) collective-permute-start(f32[3,1,32,768]{3,1,2,0:T(1,128)} %copy.106), channel_id=1, source_target_pairs={{8,0},{16,8},{24,16},{32,24},{40,32},{48,40},{56,48},{64,56},{72,6... | collective-permute-start | bytes 884744 | tf_op jit(solution)/shard_map/ppermute | solution.py:37
  5.1 14.8 %collective-permute-start = (f32[3,1,32,768]{3,1,2,0:T(1,128)}, f32[3,1,32,768]{3,1,2,0:T(1,128)}, u32[]{:S(2)}, u32[]{:S(2)}) collective-permute-start(f32[3,1,32,768]{3,1,2,0:T(1,128)} %copy.105), channel_id=1, source_target_pairs={{0,8},{8,16},{16,24},{24,32},{32,40},{40,48},{48,56},{56,64},{64,7... | collective-permute-start | bytes 884744 | tf_op jit(solution)/shard_map/ppermute | solution.py:34
  15.1 3.1 copy-start.23
  19.9 68.7 %copy-start.3 = (f32[8,32,768]{2,0,1:T(8,128)}, f32[8,32,768]{2,0,1:T(8,128)S(1)}, u32[]{:S(2)}) copy-start(f32[8,32,768]{2,0,1:T(8,128)S(1)} %get-tuple-element.145) | copy-start | bytes 2359300
  20.8 6.9 %collective-permute-start.2 = (f32[3,10,1,768]{3,1,2,0:T(8,128)S(1)}, f32[3,10,1,768]{3,1,2,0:T(8,128)S(1)}, u32[]{:S(2)}, u32[]{:S(2)}) collective-permute-start(f32[3,10,1,768]{3,1,2,0:T(8,128)S(1)} %get-tuple-element.97), channel_id=1, source_target_pairs={{0,1},{1,2},{2,3},{3,4},{4,5},{5,6},{6,7},{8,9},{9,10},{10,11},{11... | collective-permute-start | bytes 276488 | tf_op jit(solution)/shard_map/ppermute | solution.py:34
  25.6 6.5 %collective-permute-start.3 = (f32[3,10,1,768]{3,1,2,0:T(8,128)S(1)}, f32[3,10,1,768]{3,1,2,0:T(8,128)S(1)}, u32[]{:S(2)}, u32[]{:S(2)}) collective-permute-start(f32[3,10,1,768]{3,1,2,0:T(8,128)S(1)} %get-tuple-element.98), channel_id=1, source_target_pairs={{1,0},{2,1},{3,2},{4,3},{5,4},{6,5},{7,6},{9,8},{10,9},{11,10},{12... | collective-permute-start | bytes 276488 | tf_op jit(solution)/shard_map/ppermute | solution.py:37
  27.6 60.6 %copy-start.15 = (pred[32]{0:T(512)(128)(4,1)}, pred[32]{0:T(512)(128)(4,1)S(1)}, u32[]{:S(2)}) copy-start(pred[32]{0:T(512)(128)(4,1)S(1)} %get-tuple-element.138) | copy-start | bytes 100
  27.6 60.6 %copy-start.17 = (pred[32]{0:T(512)(128)(4,1)}, pred[32]{0:T(512)(128)(4,1)S(1)}, u32[]{:S(2)}) copy-start(pred[32]{0:T(512)(128)(4,1)S(1)} %get-tuple-element.139) | copy-start | bytes 100
  27.6 6.9 %copy-start.19 = (pred[8]{0:T(512)(128)(4,1)S(1)}, pred[8]{0:T(512)(128)(4,1)}, u32[]{:S(2)}) copy-start(pred[8]{0:T(512)(128)(4,1)} %get-tuple-element.140) | copy-start | bytes 28
  27.6 6.9 %copy-start.21 = (pred[8]{0:T(512)(128)(4,1)S(1)}, pred[8]{0:T(512)(128)(4,1)}, u32[]{:S(2)}) copy-start(pred[8]{0:T(512)(128)(4,1)} %get-tuple-element.141) | copy-start | bytes 28
  35.8 1.3 copy-start.11
  41.5 1.3 copy-start.12
  45.0 1.4 copy-start.8
  50.8 1.2 copy-start.1
  51.9 1.7 copy-start.14
  53.6 1.1 copy-start.7
  64.5 6.6 %collective-permute-start.4 = (f32[3,1,32,768]{3,1,2,0:T(1,128)S(1)}, f32[3,1,32,768]{3,1,2,0:T(1,128)S(1)}, u32[]{:S(2)}, u32[]{:S(2)}) collective-permute-start(f32[3,1,32,768]{3,1,2,0:T(1,128)S(1)} %get-tuple-element.113), channel_id=1, source_target_pairs={{0,8},{8,16},{16,24},{24,32},{32,40},{40,48},{48,56},{56,64},{64,7... | collective-permute-start | bytes 884744 | tf_op jit(solution)/shard_map/ppermute | solution.py:34
  67.0 8.2 %collective-permute-start.5 = (f32[3,1,32,768]{3,1,2,0:T(1,128)S(1)}, f32[3,1,32,768]{3,1,2,0:T(1,128)S(1)}, u32[]{:S(2)}, u32[]{:S(2)}) collective-permute-start(f32[3,1,32,768]{3,1,2,0:T(1,128)S(1)} %get-tuple-element.114), channel_id=1, source_target_pairs={{8,0},{16,8},{24,16},{32,24},{40,32},{48,40},{56,48},{64,56},{72,6... | collective-permute-start | bytes 884744 | tf_op jit(solution)/shard_map/ppermute | solution.py:37
  75.2 6.8 %collective-permute-start.6 = (f32[3,10,1,768]{3,1,2,0:T(8,128)S(1)}, f32[3,10,1,768]{3,1,2,0:T(8,128)S(1)}, u32[]{:S(2)}, u32[]{:S(2)}) collective-permute-start(f32[3,10,1,768]{3,1,2,0:T(8,128)S(1)} %get-tuple-element.95), channel_id=1, source_target_pairs={{0,1},{1,2},{2,3},{3,4},{4,5},{5,6},{6,7},{8,9},{9,10},{10,11},{11... | collective-permute-start | bytes 276488 | tf_op jit(solution)/shard_map/ppermute | solution.py:34
  80.0 6.5 %collective-permute-start.7 = (f32[3,10,1,768]{3,1,2,0:T(8,128)S(1)}, f32[3,10,1,768]{3,1,2,0:T(8,128)S(1)}, u32[]{:S(2)}, u32[]{:S(2)}) collective-permute-start(f32[3,10,1,768]{3,1,2,0:T(8,128)S(1)} %get-tuple-element.96), channel_id=1, source_target_pairs={{1,0},{2,1},{3,2},{4,3},{5,4},{6,5},{7,6},{9,8},{10,9},{11,10},{12... | collective-permute-start | bytes 276488 | tf_op jit(solution)/shard_map/ppermute | solution.py:37
  236.0 50.9 %copy-start = (f32[3,8,32,768]{3,1,2,0:T(8,128)}, f32[3,8,32,768]{3,1,2,0:T(8,128)S(1)}, u32[]{:S(2)}) copy-start(f32[3,8,32,768]{3,1,2,0:T(8,128)S(1)} %multiply_add_fusion.1) | copy-start | bytes 7077892
  248.3 1.4 copy-start.2
  263.0 7.1 %collective-permute-start.8 = (f32[3,1,32,768]{3,1,2,0:T(1,128)S(1)}, f32[3,1,32,768]{3,1,2,0:T(1,128)S(1)}, u32[]{:S(2)}, u32[]{:S(2)}) collective-permute-start(f32[3,1,32,768]{3,1,2,0:T(1,128)S(1)} %get-tuple-element.101), channel_id=1, source_target_pairs={{0,8},{8,16},{16,24},{24,32},{32,40},{40,48},{48,56},{56,64},{64,7... | collective-permute-start | bytes 884744 | tf_op jit(solution)/shard_map/ppermute | solution.py:34
  264.3 9.8 %collective-permute-start.9 = (f32[3,1,32,768]{3,1,2,0:T(1,128)S(1)}, f32[3,1,32,768]{3,1,2,0:T(1,128)S(1)}, u32[]{:S(2)}, u32[]{:S(2)}) collective-permute-start(f32[3,1,32,768]{3,1,2,0:T(1,128)S(1)} %get-tuple-element.102), channel_id=1, source_target_pairs={{8,0},{16,8},{24,16},{32,24},{40,32},{48,40},{56,48},{64,56},{72,6... | collective-permute-start | bytes 884744 | tf_op jit(solution)/shard_map/ppermute | solution.py:37
  274.2 6.2 %collective-permute-start.10 = (f32[3,10,1,768]{3,1,2,0:T(8,128)S(1)}, f32[3,10,1,768]{3,1,2,0:T(8,128)S(1)}, u32[]{:S(2)}, u32[]{:S(2)}) collective-permute-start(f32[3,10,1,768]{3,1,2,0:T(8,128)S(1)} %get-tuple-element.93), channel_id=1, source_target_pairs={{0,1},{1,2},{2,3},{3,4},{4,5},{5,6},{6,7},{8,9},{9,10},{10,11},{11... | collective-permute-start | bytes 276488 | tf_op jit(solution)/shard_map/ppermute | solution.py:34
  278.3 7.5 %copy-start.20 = (pred[8]{0:T(512)(128)(4,1)S(1)}, pred[8]{0:T(512)(128)(4,1)}, u32[]{:S(2)}) copy-start(pred[8]{0:T(512)(128)(4,1)} %get-tuple-element.140) | copy-start | bytes 28
  278.3 7.5 %copy-start.22 = (pred[8]{0:T(512)(128)(4,1)S(1)}, pred[8]{0:T(512)(128)(4,1)}, u32[]{:S(2)}) copy-start(pred[8]{0:T(512)(128)(4,1)} %get-tuple-element.141) | copy-start | bytes 28
  278.3 6.5 %collective-permute-start.11 = (f32[3,10,1,768]{3,1,2,0:T(8,128)S(1)}, f32[3,10,1,768]{3,1,2,0:T(8,128)S(1)}, u32[]{:S(2)}, u32[]{:S(2)}) collective-permute-start(f32[3,10,1,768]{3,1,2,0:T(8,128)S(1)} %get-tuple-element.94), channel_id=1, source_target_pairs={{1,0},{2,1},{3,2},{4,3},{5,4},{6,5},{7,6},{9,8},{10,9},{11,10},{12... | collective-permute-start | bytes 276488 | tf_op jit(solution)/shard_map/ppermute | solution.py:37
  (7 other events, 6.2 us)
where the time goes:
time: 372 us; the launch traced here: 367 us
  blocking collectives  200 us (54%)
  other arithmetic  42.2 us (11%)
  starting transfers between devices  32.4 us (9%)
  local copies, waits for them, and re-layouts  29.6 us (8%)
  matrix products  29 us (8%)
  waiting for transfers between devices  28.9 us (8%)
  between operations  5.65 us (2%)
    psum x2, blocking collectives, squares(): return lax.psum(inner_local(values_in, values_in), ('gx', 'gy'))  133 us
    psum x1, blocking collectives, local(): lax.psum(inner_local(direction, image_vec), ('gx', 'gy'))  66.2 us
    ppermute x6, starting transfers between devices, with_halo(): lax.ppermute(lax.slice_in_dim(block, block.shape[dim] - width, None, axis...  22.8 us
    ppermute x6, waiting for transfers between devices, with_halo(): lax.ppermute(lax.slice_in_dim(block, 0, width, axis=dim), axis, backward)  21.3 us
    reduce_sum x3, other arithmetic, inner_local(): return jnp.sum(first * second * inverse_mult[None])  11.9 us
    unnamed x57, local copies, waits for them, and re-layouts  9.86 us
    ppermute x6, starting transfers between devices, with_halo(): lax.ppermute(lax.slice_in_dim(block, 0, width, axis=dim), axis, backward)  9.63 us
    ppermute x6, waiting for transfers between devices, with_halo(): lax.ppermute(lax.slice_in_dim(block, block.shape[dim] - width, None, axis...  7.63 us
  transfers between devices with their start and end apart: 12, of which 10 were waited for; matrix products, arithmetic and copies ran while one was open for 3% of the time, Pallas kernels for 0%

commit v1 on v0

v1 whole, which is shorter than its diff:
```python
import functools

import jax
import jax.numpy as jnp
import numpy as np
from jax import lax
from jax.experimental import pallas as pl
from jax.experimental.pallas import tpu as pltpu
from jax.sharding import PartitionSpec as P

ORDER = 7
NODES = ORDER + 1
LANES = 128

POISSON = 0.3
LAME_FIRST = POISSON / ((1.0 + POISSON) * (1.0 - 2.0 * POISSON))
LAME_SHEAR = 1.0 / (2.0 * (1.0 + POISSON))
SOLID_MODULUS = 0.1
VOID_MODULUS = 0.001
HIGHEST = lax.Precision.HIGHEST
INTERIOR_POINTS = (
    -0.8717401485096066,
    -0.5917001814331423,
    -0.2092992179024789,
    0.2092992179024789,
    0.5917001814331423,
    0.8717401485096066,
)
VMEM_LIMIT = 40 * 1024 * 1024


def legendre_value(poly_order, point):
    previous = 1.0
    current = point
    for degree in range(1, poly_order):
        following = ((2.0 * degree + 1.0) * point * current - degree * previous) / (degree + 1.0)
        previous = current
        current = following
    return current


def gll_tables(poly_order):
    points = np.array([-1.0] + list(INTERIOR_POINTS) + [1.0])
    values = np.array([legendre_value(poly_order, float(point)) for point in points])
    weights = 2.0 / (poly_order * (poly_order + 1) * values**2)
    node_count = poly_order + 1
    derivative = np.zeros((node_count, node_count))
    for row_index in range(node_count):
        for col_index in range(node_count):
            if row_index != col_index:
                derivative[row_index, col_index] = values[row_index] / (
                    values[col_index] * (points[row_index] - points[col_index])
                )
    derivative[0, 0] = -poly_order * (poly_order + 1) / 4.0
    derivative[poly_order, poly_order] = poly_order * (poly_order + 1) / 4.0
    return (derivative, weights)


DERIV, WEIGHTS = gll_tables(ORDER)
HALF = NODES // 2
ODD = [[0.5 * (DERIV[a, i] - DERIV[a, ORDER - i]) for i in range(HALF)] for a in range(HALF)]
EVEN = [[0.5 * (DERIV[a, i] + DERIV[a, ORDER - i]) for i in range(HALF)] for a in range(HALF)]


def shared_halves(local_len, offset, global_len, node_count):
    position = jnp.arange(local_len, dtype=jnp.int32)
    node_index = position % node_count
    global_pos = position + offset
    shared = (node_index == 0) & (global_pos > 0) | (node_index == node_count - 1) & (
        global_pos < global_len - 1
    )
    return jnp.where(shared, 0.5, 1.0).astype(jnp.float32)


def combine(coefs, terms):
    total = None
    for coef, term in zip(coefs, terms):
        part = float(coef) * term
        total = part if total is None else total + part
    return total


def row_sum_y(v_ref, lo, hi, comp, plane, elem, n_elem):
    base = elem * NODES
    own = v_ref[comp, plane, base : base + NODES, :]
    below = lo if elem == 0 else v_ref[comp, plane, base - 1 : base, :]
    above = hi if elem == n_elem - 1 else v_ref[comp, plane, base + NODES : base + NODES + 1, :]
    sub = lax.broadcasted_iota(jnp.int32, own.shape, 0)
    below = jnp.broadcast_to(below, own.shape)
    above = jnp.broadcast_to(above, own.shape)
    return own + jnp.where(sub == 0, below, jnp.where(sub == ORDER, above, 0.0))


def sum_z(rows):
    size = rows.shape[-1]
    lane = lax.broadcasted_iota(jnp.int32, rows.shape, 1)
    ahead = pltpu.roll(rows, size - 1, 1)
    behind = pltpu.roll(rows, 1, 1)
    upper = (lane % NODES == ORDER) & (lane < size - 1)
    lower = (lane % NODES == 0) & (lane > 0)
    return rows + jnp.where(upper, ahead, jnp.where(lower, behind, 0.0))


def assembled_strip(v_ref, ylo_ref, yhi_ref, xlo_ref, xhi_ref, free_ref, comp, plane, elem, n_elem):
    lo = ylo_ref[comp, plane : plane + 1, :]
    hi = yhi_ref[comp, plane : plane + 1, :]
    rows = row_sum_y(v_ref, lo, hi, comp, plane, elem, n_elem)
    base = elem * NODES
    if plane == 0:
        rows = rows + xlo_ref[comp, base : base + NODES, :]
    if plane == ORDER:
        rows = rows + xhi_ref[comp, base : base + NODES, :]
    rows = sum_z(rows)
    head = rows[:, :LANES] * free_ref[plane, base : base + NODES, :]
    return jnp.concatenate([head, rows[:, LANES:]], axis=1)


def fold(strip):
    total = strip[:, :LANES]
    for start in range(LANES, strip.shape[1], LANES):
        total = total + strip[:, start : start + LANES]
    return total


def apply_kernel(
    v_ref, ylo_ref, yhi_ref, xlo_ref, xhi_ref, free_ref, elem_ref, half_ref, halfz_ref,
    zmat_ref, ycol_ref, sums_in_ref,
    u_ref, k_ref, flo_ref, fhi_ref, sums_ref,
    grad_ref, stress_ref, side_ref, *, slot,
):
    comps, planes, size_y, size_z = v_ref.shape
    n_elem = size_y // NODES
    n_tile = size_z // LANES
    square = jnp.zeros((NODES, LANES), jnp.float32)
    for elem in range(n_elem):
        base = elem * NODES
        for plane in range(planes):
            part = None
            for comp in range(comps):
                strip = assembled_strip(
                    v_ref, ylo_ref, yhi_ref, xlo_ref, xhi_ref, free_ref, comp, plane, elem, n_elem
                )
                u_ref[comp, plane, base : base + NODES, :] = strip
                part = strip * strip if part is None else part + strip * strip
            part = fold(part * halfz_ref[0:1, :])
            square = square + part * half_ref[plane, base : base + NODES, :]

    rows = comps * planes * size_y
    for tile in range(n_tile):
        lanes = slice(tile * LANES, (tile + 1) * LANES)
        flat = u_ref[:, :, :, lanes].reshape(rows, LANES)
        grad_ref[:, :, :, lanes] = jnp.dot(
            flat, zmat_ref[0], precision=HIGHEST, preferred_element_type=jnp.float32
        ).reshape(comps, planes, size_y, LANES)

    def block(tile, elem):
        lanes = pl.ds(pl.multiple_of(tile * LANES, LANES), LANES)
        base = elem * NODES
        sub = slice(base, base + NODES)
        even, odd = [], []
        for comp in range(3):
            vals = [u_ref[comp, i, sub, lanes] for i in range(NODES)]
            even.append([vals[i] + vals[ORDER - i] for i in range(HALF)])
            odd.append([vals[i] - vals[ORDER - i] for i in range(HALF)])
        scale = elem_ref[sub, lanes]
        xsum = [[None] * HALF for _ in range(3)]
        xdif = [[None] * HALF for _ in range(3)]
        for pair in range(HALF):
            first = [combine(ODD[pair], odd[c]) for c in range(3)]
            second = [combine(EVEN[pair], even[c]) for c in range(3)]
            side_x = []
            for plane, sign in ((pair, 1), (ORDER - pair, -1)):
                gx = [first[c] + second[c] if sign > 0 else first[c] - second[c] for c in range(3)]
                gy = []
                for c in range(3):
                    total = None
                    for j in range(NODES):
                        row = u_ref[c, plane, base + j : base + j + 1, lanes]
                        part = ycol_ref[0, j] * jnp.broadcast_to(row, (NODES, LANES))
                        total = part if total is None else total + part
                    gy.append(total)
                gz = [grad_ref[c, plane, sub, lanes] for c in range(3)]
                shear = scale * float(LAME_SHEAR * WEIGHTS[plane])
                twice = scale * float(2.0 * LAME_SHEAR * WEIGHTS[plane])
                spread = (gx[0] + gy[1] + gz[2]) * (scale * float(LAME_FIRST * WEIGHTS[plane]))
                sxx = twice * gx[0] + spread
                syy = twice * gy[1] + spread
                szz = twice * gz[2] + spread
                sxy = shear * (gx[1] + gy[0])
                sxz = shear * (gx[2] + gz[0])
                syz = shear * (gy[2] + gz[1])
                side_x.append((sxx, sxy, sxz))
                for c, value in enumerate((sxz, syz, szz)):
                    stress_ref[c, plane, sub, lanes] = value
                for c, value in enumerate((sxy, syy, syz)):
                    side_ref[c, plane, :, :] = value
            for c in range(3):
                se = side_x[0][c] + side_x[1][c]
                so = side_x[0][c] - side_x[1][c]
                for i in range(HALF):
                    add_x = float(EVEN[pair][i]) * so
                    add_y = float(ODD[pair][i]) * se
                    xsum[c][i] = add_x if pair == 0 else xsum[c][i] + add_x
                    xdif[c][i] = add_y if pair == 0 else xdif[c][i] + add_y
        for c in range(3):
            for plane in range(NODES):
                i = min(plane, ORDER - plane)
                total = xsum[c][i] + xdif[c][i] if plane < HALF else xsum[c][i] - xdif[c][i]
                for b in range(NODES):
                    row = side_ref[c, plane, b : b + 1, :]
                    total = total + ycol_ref[1, b] * jnp.broadcast_to(row, (NODES, LANES))
                k_ref[c, plane, sub, lanes] = total

    @pl.loop(0, n_tile)
    def _(tile):
        for elem in range(n_elem):
            block(tile, elem)

    energy = jnp.zeros((NODES, LANES), jnp.float32)
    for tile in range(n_tile):
        lanes = slice(tile * LANES, (tile + 1) * LANES)
        flat = stress_ref[:, :, :, lanes].reshape(rows, LANES)
        total = jnp.dot(
            flat, zmat_ref[1], precision=HIGHEST, preferred_element_type=jnp.float32
        ).reshape(comps, planes, size_y, LANES)
        total = total + k_ref[:, :, :, lanes]
        k_ref[:, :, :, lanes] = total
        product = (total * u_ref[:, :, :, lanes]).reshape(rows // NODES, NODES, LANES)
        energy = energy + jnp.sum(product, axis=0)
    for comp in range(comps):
        for plane in range(planes):
            flo_ref[comp, plane : plane + 1, :] = k_ref[comp, plane, 0:1, :]
            fhi_ref[comp, plane : plane + 1, :] = k_ref[comp, plane, size_y - 1 : size_y, :]
    lane = lax.broadcasted_iota(jnp.int32, sums_ref.shape, 1)
    known = jnp.zeros(sums_ref.shape, jnp.float32) if slot == 0 else sums_in_ref[...]
    known = jnp.where(lane == 2 * slot, jnp.sum(square), known)
    sums_ref[...] = jnp.where(lane == 2 * slot + 1, jnp.sum(energy), known)


def rows_kernel(v_ref, lo_ref, hi_ref):
    comps, planes, size_y, _ = v_ref.shape
    for comp in range(comps):
        for plane in range(planes):
            lo_ref[comp, plane : plane + 1, :] = v_ref[comp, plane, 0:1, :]
            hi_ref[comp, plane : plane + 1, :] = v_ref[comp, plane, size_y - 1 : size_y, :]


def faces_kernel(vlo_ref, vhi_ref, ylo_ref, yhi_ref, xlo_ref, xhi_ref):
    comps, _, size_y, _ = vlo_ref.shape
    n_elem = size_y // NODES
    for v_ref, plane, out_ref in ((vlo_ref, 0, xlo_ref), (vhi_ref, ORDER, xhi_ref)):
        for comp in range(comps):
            lo = ylo_ref[comp, plane : plane + 1, :]
            hi = yhi_ref[comp, plane : plane + 1, :]
            for elem in range(n_elem):
                base = elem * NODES
                out_ref[comp, base : base + NODES, :] = row_sum_y(
                    v_ref, lo, hi, comp, 0, elem, n_elem
                )


def finish_kernel(
    k_ref, ylo_ref, yhi_ref, xlo_ref, xhi_ref, free_ref, r_ref, q_ref, sums_ref, adj_ref, res_ref
):
    comps, planes, size_y, _ = k_ref.shape
    n_elem = size_y // NODES
    sums = jnp.sum(sums_ref[...], axis=0, keepdims=True)
    lane = lax.broadcasted_iota(jnp.int32, sums.shape, 1)
    m0, m1, m2, m3 = [
        jnp.sum(jnp.where(lane == i, sums, 0.0), axis=1, keepdims=True) for i in range(4)
    ]
    first = m0 / m1
    following = first * first * m2 - m0
    ratio = following / m0
    grow = 1.0 + ratio
    second = following / (grow * grow * m1 - 2.0 * first * grow * m2 + first * first * m3)
    lead = first + second * grow
    cross = first * second
    for elem in range(n_elem):
        base = elem * NODES
        sub = slice(base, base + NODES)
        for plane in range(planes):
            for comp in range(comps):
                strip = assembled_strip(
                    k_ref, ylo_ref, yhi_ref, xlo_ref, xhi_ref, free_ref, comp, plane, elem, n_elem
                )
                loads = r_ref[comp, plane, sub, :]
                image = q_ref[comp, plane, sub, :]
                adj_ref[comp, plane, sub, :] = lead * loads - cross * image
                res_ref[comp, plane, sub, :] = loads - lead * image + cross * strip


def halo(low_side, high_side, axis):
    count = lax.axis_size(axis)
    forward = [(i, i + 1) for i in range(count - 1)]
    backward = [(target, source) for source, target in forward]
    return lax.ppermute(high_side, axis, forward), lax.ppermute(low_side, axis, backward)


def local(rhs_loads, flags, fixed):
    comps, size_x, size_y, size_z = rhs_loads.shape
    axes = ("gx", "gy")
    devices = lax.axis_size("gx") * lax.axis_size("gy")
    params = pltpu.CompilerParams(vmem_limit_bytes=VMEM_LIMIT)
    f32 = jnp.float32
    field = jax.ShapeDtypeStruct(rhs_loads.shape, f32)
    y_side = jax.ShapeDtypeStruct((comps, size_x, size_z), f32)
    x_side = jax.ShapeDtypeStruct((comps, size_y, size_z), f32)
    whole = pl.BlockSpec(memory_space=pltpu.VMEM)

    modulus = jnp.where(flags[0] == 1, SOLID_MODULUS, VOID_MODULUS).astype(f32)
    modulus = jnp.repeat(jnp.repeat(modulus, NODES, axis=0), NODES, axis=1)
    weight_y = jnp.asarray(np.tile(WEIGHTS, size_y // NODES), f32)
    weight_z = jnp.asarray(np.tile(WEIGHTS, size_z // NODES), f32)
    elem_scale = modulus * weight_y[:, None] * weight_z[None, :]
    free = 1.0 - fixed.astype(f32)[:, :, None] * (jnp.arange(LANES) == 0).astype(f32)
    half_xy = (
        shared_halves(size_x, lax.axis_index("gx") * size_x, size_x * lax.axis_size("gx"), NODES)[
            :, None, None
        ]
        * shared_halves(
            size_y, lax.axis_index("gy") * size_y, size_y * lax.axis_size("gy"), NODES
        )[None, :, None]
        * jnp.ones((LANES,), f32)
    )
    half_z = jnp.broadcast_to(shared_halves(size_z, 0, size_z, NODES)[None], (NODES, size_z))
    z_mat = jnp.asarray(
        np.stack([np.kron(np.eye(LANES // NODES), m) for m in (DERIV.T, DERIV)]), f32
    )
    y_col = jnp.asarray(
        np.broadcast_to(
            np.stack([DERIV.T, DERIV])[:, :, :, None], (2, NODES, NODES, LANES)
        ),
        f32,
    )

    def faces(v, ylo, yhi):
        block = (comps, 1, size_y, size_z)
        side = pl.BlockSpec((comps, size_x, size_z), lambda i: (0, 0, 0))
        out = pl.BlockSpec((comps, size_y, size_z), lambda i: (0, 0, 0))
        return pl.pallas_call(
            faces_kernel,
            grid=(1,),
            in_specs=[
                pl.BlockSpec(block, lambda i: (0, 0, 0, 0)),
                pl.BlockSpec(block, lambda i: (0, size_x - 1, 0, 0)),
                side,
                side,
            ],
            out_specs=[out, out],
            out_shape=[x_side, x_side],
            compiler_params=params,
            name="faces",
        )(v, v, ylo, yhi)

    def apply_stiffness(v, halos, sums, slot):
        return pl.pallas_call(
            functools.partial(apply_kernel, slot=slot),
            in_specs=[whole] * 12,
            out_specs=[whole] * 5,
            out_shape=[
                field, field, y_side, y_side, jax.ShapeDtypeStruct((devices, LANES), f32)
            ],
            scratch_shapes=[
                pltpu.VMEM(rhs_loads.shape, f32),
                pltpu.VMEM(rhs_loads.shape, f32),
                pltpu.VMEM((comps, size_x, NODES, LANES), f32),
            ],
            compiler_params=params,
            name="stiffness",
        )(v, *halos, free, elem_scale, half_xy, half_z, z_mat, y_col, sums)

    def exchange(v, low_rows, high_rows):
        ylo, yhi = halo(low_rows, high_rows, "gy")
        xlo, xhi = halo(*faces(v, ylo, yhi), "gx")
        return ylo, yhi, xlo, xhi

    low_rows, high_rows = pl.pallas_call(
        rows_kernel,
        in_specs=[whole],
        out_specs=[whole] * 2,
        out_shape=[y_side, y_side],
        compiler_params=params,
        name="rows",
    )(rhs_loads)
    sums = jnp.zeros((devices, LANES), f32)
    halos = exchange(rhs_loads, low_rows, high_rows)
    loads, k_loads, low_rows, high_rows, sums = apply_stiffness(rhs_loads, halos, sums, 0)
    halos = exchange(k_loads, low_rows, high_rows)
    image, k_image, low_rows, high_rows, sums = apply_stiffness(k_loads, halos, sums, 1)
    halos = exchange(k_image, low_rows, high_rows)
    sums = lax.all_to_all(sums, axes, 0, 0, tiled=True)
    return tuple(
        pl.pallas_call(
            finish_kernel,
            in_specs=[whole] * 9,
            out_specs=[whole] * 2,
            out_shape=[field, field],
            compiler_params=params,
            name="finish",
        )(k_image, *halos, free, loads, image, sums)
    )


def solution(mesh):
    in_specs = (P(None, "gx", "gy", None), P("gx", "gy", None), P("gx", "gy"))
    out_specs = (P(None, "gx", "gy", None), P(None, "gx", "gy", None))
    return jax.shard_map(local, mesh=mesh, in_specs=in_specs, out_specs=out_specs, check_vma=False)
```

time: 372 us -> 107 us (0.29); the launches traced: 367 us -> 107 us
  blocking collectives: 200 us -> 20.8 us
  other arithmetic: 42.2 us -> 0.28 us
  matrix products: 29 us -> 0 us
  local copies, waits for them, and re-layouts: 29.6 us -> 2.04 us
  Pallas kernels: 0 us -> 23.9 us
  between operations: 5.65 us -> 0.97 us
    psum x3 -> x0, blocking collectives: 200 us -> none  [the longest x2 133 us: squares(): return lax.psum(inner_local(values_in, values_in), ('gx', 'gy'))]
    dot_general x12 -> x0, matrix products: 29 us -> none  [the longest x2 5.72 us: local(): jnp.einsum('bj,xpfbz->xpfjz', derivative, derive_split, precision=HIGHEST)]
    pallas_call x0 -> x7, Pallas kernels: none -> 23.9 us  [the longest x2 19.7 us: apply_stiffness(): pl.pallas_call(functools.partial(apply_kernel, slot=slot), in_specs=[whol...]
    all_to_all x0 -> x1, blocking collectives: none -> 20.8 us  [local(): sums = lax.all_to_all(sums, axes, 0, 0, tiled=True)]
    slice x24 -> x0, local copies, waits for them, and re-layouts: 13.1 us -> none  [the longest x4 2.86 us: with_halo(): lax.slice_in_dim(block, block.shape[dim] - width, None, axis=dim)]
    reduce_sum x3 -> x0, other arithmetic: 11.9 us -> none  [inner_local(): return jnp.sum(first * second * inverse_mult[None])]
    unnamed x57 -> x16, local copies, waits for them, and re-layouts: 9.86 us -> 1.69 us
    add x7 -> x0, other arithmetic: 6.31 us -> none  [the longest x6 3.36 us: pair_core(): middle + jnp.where(upper_node, ahead, 0.0)]
  transfers between devices with their start and end apart: 12 -> 12, of which waited for: 10 -> 7; matrix products, arithmetic and copies ran while one was open for 3% -> 0% of each run, Pallas kernels for 0% -> 0%
where the time goes in v1:
time: 107 us
  starting transfers between devices  33.3 us (31%)
  waiting for transfers between devices  25.5 us (24%)
  Pallas kernels  23.9 us (22%)
  blocking collectives  20.8 us (19%)
  local copies, waits for them, and re-layouts  2.04 us (2%)
    ppermute x6, starting transfers between devices, halo(): lax.ppermute(high_side, axis, forward)  23.4 us
    all_to_all x1, blocking collectives, local(): sums = lax.all_to_all(sums, axes, 0, 0, tiled=True)  20.8 us
    pallas_call x2, Pallas kernels, apply_stiffness(): pl.pallas_call(functools.partial(apply_kernel, slot=slot), in_specs=[whol...  19.7 us
    ppermute x6, waiting for transfers between devices, halo(): lax.ppermute(low_side, axis, backward)  18.9 us
    ppermute x6, starting transfers between devices, halo(): lax.ppermute(low_side, axis, backward)  9.82 us
    ppermute x6, waiting for transfers between devices, halo(): lax.ppermute(high_side, axis, forward)  6.62 us
    pallas_call x1, Pallas kernels, local(): pl.pallas_call(finish_kernel, in_specs=[whole] * 9, out_specs=[whole] * 2...  3.65 us
  transfers between devices with their start and end apart: 12, of which 7 were waited for; matrix products, arithmetic and copies ran while one was open for 0% of the time, Pallas kernels for 0%

profile of v1, /device:TPU:1, one launch (start us, length us, event | category | flops | bytes accessed | tf_op | source)
XLA Modules:
  0.0 106.7 jit_solution(3319747330232374452)
XLA Ops:
  0.6 1.7 %copy-done = f32[3,8,32,768]{3,2,1,0:T(8,128)S(1)} copy-done((f32[3,8,32,768]{3,2,1,0:T(8,128)S(1)}, f32[3,8,32,768]{3,2,1,0:T(8,128)}, u32[]{:S(2)}) %copy-start) | copy-done | bytes 2359320
  2.4 5.1 %collective-permute-start = (f32[3,8,768]{2,1,0:T(8,128)S(1)}, f32[3,8,768]{2,1,0:T(8,128)S(1)}, u32[]{:S(2)}, u32[]{:S(2)}) collective-permute-start(f32[3,8,768]{2,1,0:T(8,128)S(1)} %get-tuple-element.20), channel_id=1, source_target_pairs={{0,1},{1,2},{2,3},{3,4},{4,5},{5,6},{6,7},{8,9},{9,10},{10,11},{11... | collective-permute-start | bytes 221192 | tf_op jit(solution)/shard_map/ppermute | solution.py:297
  7.4 1.9 %collective-permute-start.1 = (f32[3,8,768]{2,1,0:T(8,128)S(1)}, f32[3,8,768]{2,1,0:T(8,128)S(1)}, u32[]{:S(2)}, u32[]{:S(2)}) collective-permute-start(f32[3,8,768]{2,1,0:T(8,128)S(1)} %get-tuple-element.21), channel_id=1, source_target_pairs={{1,0},{2,1},{3,2},{4,3},{5,4},{6,5},{7,6},{9,8},{10,9},{11,10},{12... | collective-permute-start | bytes 221192 | tf_op jit(solution)/shard_map/ppermute | solution.py:297
  9.5 0.1 copy.13
  9.6 0.1 multiply_subtract_fusion.free_ref
  9.8 0.1 copy.14
  10.0 3.2 %collective-permute-done.1.yhi_ref = f32[3,8,768]{2,1,0:T(8,128)S(1)} collective-permute-done((f32[3,8,768]{2,1,0:T(8,128)S(1)}, f32[3,8,768]{2,1,0:T(8,128)S(1)}, u32[]{:S(2)}, u32[]{:S(2)}) %collective-permute-start.1) | collective-permute-done | bytes 73760 | tf_op jit(solution)/shard_map/ppermute | solution.py:297
  13.1 0.2 faces.3
  13.3 3.2 %collective-permute-start.2 = (f32[3,32,768]{2,1,0:T(8,128)S(1)}, f32[3,32,768]{2,1,0:T(8,128)S(1)}, u32[]{:S(2)}, u32[]{:S(2)}) collective-permute-start(f32[3,32,768]{2,1,0:T(8,128)S(1)} %get-tuple-element.22), channel_id=1, source_target_pairs={{0,8},{8,16},{16,24},{24,32},{32,40},{40,48},{48,56},{56,64},{64,7... | collective-permute-start | bytes 884744 | tf_op jit(solution)/shard_map/ppermute | solution.py:297
  16.5 1.3 %collective-permute-start.3 = (f32[3,32,768]{2,1,0:T(8,128)S(1)}, f32[3,32,768]{2,1,0:T(8,128)S(1)}, u32[]{:S(2)}, u32[]{:S(2)}) collective-permute-start(f32[3,32,768]{2,1,0:T(8,128)S(1)} %get-tuple-element.23), channel_id=1, source_target_pairs={{8,0},{16,8},{24,16},{32,24},{40,32},{48,40},{56,48},{64,56},{72,6... | collective-permute-start | bytes 884744 | tf_op jit(solution)/shard_map/ppermute | solution.py:297
  17.8 0.1 multiply_multiply_fusion.elem_ref
  17.9 3.3 %collective-permute-done.2.xlo_ref = f32[3,32,768]{2,1,0:T(8,128)S(1)} collective-permute-done((f32[3,32,768]{2,1,0:T(8,128)S(1)}, f32[3,32,768]{2,1,0:T(8,128)S(1)}, u32[]{:S(2)}, u32[]{:S(2)}) %collective-permute-start.2) | collective-permute-done | bytes 294944 | tf_op jit(solution)/shard_map/ppermute | solution.py:297
  21.3 4.1 %collective-permute-done.3.xhi_ref = f32[3,32,768]{2,1,0:T(8,128)S(1)} collective-permute-done((f32[3,32,768]{2,1,0:T(8,128)S(1)}, f32[3,32,768]{2,1,0:T(8,128)S(1)}, u32[]{:S(2)}, u32[]{:S(2)}) %collective-permute-start.3) | collective-permute-done | bytes 294944 | tf_op jit(solution)/shard_map/ppermute | solution.py:297
  25.4 0.1 mul.70.half_ref
  25.5 9.8 %stiffness.2 = (f32[3,8,32,768]{3,2,1,0:T(8,128)S(1)}, f32[3,8,32,768]{3,2,1,0:T(8,128)S(1)}, f32[3,8,768]{2,1,0:T(8,128)S(1)}, f32[3,8,768]{2,1,0:T(8,128)S(1)}, f32[128,128]{1,0:T(8,128)S(1)}) custom-call(f32[3,8,32,768]{3,2,1,0:T(8,128)S(1)} %copy-done.1, f32[3,8,768]{2,1,0:T(8,128)S(1)} %collective-permute-done.ylo_ref, ...), custom_call_target="tpu_custom_call" | custom-call | tf_op jit(solution)/shard_map/stiffness/pallas_call | solution.py:357
  35.4 4.2 %collective-permute-start.4 = (f32[3,8,768]{2,1,0:T(8,128)S(1)}, f32[3,8,768]{2,1,0:T(8,128)S(1)}, u32[]{:S(2)}, u32[]{:S(2)}) collective-permute-start(f32[3,8,768]{2,1,0:T(8,128)S(1)} %get-tuple-element.25), channel_id=1, source_target_pairs={{0,1},{1,2},{2,3},{3,4},{4,5},{5,6},{6,7},{8,9},{9,10},{10,11},{11... | collective-permute-start | bytes 221192 | tf_op jit(solution)/shard_map/ppermute | solution.py:297
  39.6 1.9 %collective-permute-start.5 = (f32[3,8,768]{2,1,0:T(8,128)S(1)}, f32[3,8,768]{2,1,0:T(8,128)S(1)}, u32[]{:S(2)}, u32[]{:S(2)}) collective-permute-start(f32[3,8,768]{2,1,0:T(8,128)S(1)} %get-tuple-element.26), channel_id=1, source_target_pairs={{1,0},{2,1},{3,2},{4,3},{5,4},{6,5},{7,6},{9,8},{10,9},{11,10},{12... | collective-permute-start | bytes 221192 | tf_op jit(solution)/shard_map/ppermute | solution.py:297
  41.5 3.7 %collective-permute-done.5.yhi_ref = f32[3,8,768]{2,1,0:T(8,128)S(1)} collective-permute-done((f32[3,8,768]{2,1,0:T(8,128)S(1)}, f32[3,8,768]{2,1,0:T(8,128)S(1)}, u32[]{:S(2)}, u32[]{:S(2)}) %collective-permute-start.5) | collective-permute-done | bytes 73760 | tf_op jit(solution)/shard_map/ppermute | solution.py:297
  45.3 0.2 faces.4
  45.4 3.2 %collective-permute-start.6 = (f32[3,32,768]{2,1,0:T(8,128)S(1)}, f32[3,32,768]{2,1,0:T(8,128)S(1)}, u32[]{:S(2)}, u32[]{:S(2)}) collective-permute-start(f32[3,32,768]{2,1,0:T(8,128)S(1)} %get-tuple-element.27), channel_id=1, source_target_pairs={{0,8},{8,16},{16,24},{24,32},{32,40},{40,48},{48,56},{56,64},{64,7... | collective-permute-start | bytes 884744 | tf_op jit(solution)/shard_map/ppermute | solution.py:297
  48.7 1.5 %collective-permute-start.7 = (f32[3,32,768]{2,1,0:T(8,128)S(1)}, f32[3,32,768]{2,1,0:T(8,128)S(1)}, u32[]{:S(2)}, u32[]{:S(2)}) collective-permute-start(f32[3,32,768]{2,1,0:T(8,128)S(1)} %get-tuple-element.28), channel_id=1, source_target_pairs={{8,0},{16,8},{24,16},{32,24},{40,32},{48,40},{56,48},{64,56},{72,6... | collective-permute-start | bytes 884744 | tf_op jit(solution)/shard_map/ppermute | solution.py:297
  50.1 3.3 %collective-permute-done.6.xlo_ref = f32[3,32,768]{2,1,0:T(8,128)S(1)} collective-permute-done((f32[3,32,768]{2,1,0:T(8,128)S(1)}, f32[3,32,768]{2,1,0:T(8,128)S(1)}, u32[]{:S(2)}, u32[]{:S(2)}) %collective-permute-start.6) | collective-permute-done | bytes 294944 | tf_op jit(solution)/shard_map/ppermute | solution.py:297
  53.4 4.1 %collective-permute-done.7.xhi_ref = f32[3,32,768]{2,1,0:T(8,128)S(1)} collective-permute-done((f32[3,32,768]{2,1,0:T(8,128)S(1)}, f32[3,32,768]{2,1,0:T(8,128)S(1)}, u32[]{:S(2)}, u32[]{:S(2)}) %collective-permute-start.7) | collective-permute-done | bytes 294944 | tf_op jit(solution)/shard_map/ppermute | solution.py:297
  57.5 9.9 %stiffness.3 = (f32[3,8,32,768]{3,2,1,0:T(8,128)S(1)}, f32[3,8,32,768]{3,2,1,0:T(8,128)S(1)}, f32[3,8,768]{2,1,0:T(8,128)S(1)}, f32[3,8,768]{2,1,0:T(8,128)S(1)}, f32[128,128]{1,0:T(8,128)S(1)}) custom-call(f32[3,8,32,768]{3,2,1,0:T(8,128)S(1)} %get-tuple-element.24.vlo_ref.vhi_ref.v_ref, f32[3,8,768]{2,1,0:T(8,128)S(1)} %collective-permute-done.4.ylo_ref, ...), custom_call_target="tpu_custom_call" | custom-call | tf_op jit(solution)/shard_map/stiffness/pallas_call | solution.py:357
  67.4 3.9 %collective-permute-start.8 = (f32[3,8,768]{2,1,0:T(8,128)S(1)}, f32[3,8,768]{2,1,0:T(8,128)S(1)}, u32[]{:S(2)}, u32[]{:S(2)}) collective-permute-start(f32[3,8,768]{2,1,0:T(8,128)S(1)} %get-tuple-element.31), channel_id=1, source_target_pairs={{0,1},{1,2},{2,3},{3,4},{4,5},{5,6},{6,7},{8,9},{9,10},{10,11},{11... | collective-permute-start | bytes 221192 | tf_op jit(solution)/shard_map/ppermute | solution.py:297
  71.3 1.9 %collective-permute-start.9 = (f32[3,8,768]{2,1,0:T(8,128)S(1)}, f32[3,8,768]{2,1,0:T(8,128)S(1)}, u32[]{:S(2)}, u32[]{:S(2)}) collective-permute-start(f32[3,8,768]{2,1,0:T(8,128)S(1)} %get-tuple-element.32), channel_id=1, source_target_pairs={{1,0},{2,1},{3,2},{4,3},{5,4},{6,5},{7,6},{9,8},{10,9},{11,10},{12... | collective-permute-start | bytes 221192 | tf_op jit(solution)/shard_map/ppermute | solution.py:297
  73.2 3.7 %collective-permute-done.9.yhi_ref = f32[3,8,768]{2,1,0:T(8,128)S(1)} collective-permute-done((f32[3,8,768]{2,1,0:T(8,128)S(1)}, f32[3,8,768]{2,1,0:T(8,128)S(1)}, u32[]{:S(2)}, u32[]{:S(2)}) %collective-permute-start.9) | collective-permute-done | bytes 73760 | tf_op jit(solution)/shard_map/ppermute | solution.py:297
  77.0 0.2 faces.5
  77.1 3.8 %collective-permute-start.10 = (f32[3,32,768]{2,1,0:T(8,128)S(1)}, f32[3,32,768]{2,1,0:T(8,128)S(1)}, u32[]{:S(2)}, u32[]{:S(2)}) collective-permute-start(f32[3,32,768]{2,1,0:T(8,128)S(1)} %get-tuple-element.33), channel_id=1, source_target_pairs={{0,8},{8,16},{16,24},{24,32},{32,40},{40,48},{48,56},{56,64},{64,7... | collective-permute-start | bytes 884744 | tf_op jit(solution)/shard_map/ppermute | solution.py:297
  81.0 1.3 %collective-permute-start.11 = (f32[3,32,768]{2,1,0:T(8,128)S(1)}, f32[3,32,768]{2,1,0:T(8,128)S(1)}, u32[]{:S(2)}, u32[]{:S(2)}) collective-permute-start(f32[3,32,768]{2,1,0:T(8,128)S(1)} %get-tuple-element.34), channel_id=1, source_target_pairs={{8,0},{16,8},{24,16},{32,24},{40,32},{48,40},{56,48},{64,56},{72,6... | collective-permute-start | bytes 884744 | tf_op jit(solution)/shard_map/ppermute | solution.py:297
  82.3 20.8 %all_to_all.11 = f32[128,1,128]{2,1,0:T(1,128)S(1)} all-to-all(f32[128,1,128]{2,1,0:T(1,128)S(1)} %bitcast.11), channel_id=1, replica_groups=mesh['gx'=16,'gy'=8] {'gx','gy'}, dimensions={0} | all-to-all | bytes 131072 | tf_op jit(solution)/shard_map/all_to_all | solution.py:392
  103.1 3.7 %finish.1 = (f32[3,8,32,768]{3,2,1,0:T(8,128)}, f32[3,8,32,768]{3,2,1,0:T(8,128)}) custom-call(f32[3,8,32,768]{3,2,1,0:T(8,128)S(1)} %get-tuple-element.30.vlo_ref.vhi_ref.k_ref, f32[3,8,768]{2,1,0:T(8,128)S(1)} %collective-permute-done.8.ylo_ref, f32[3,8,768]{2,1,0:T(8,128)S(1)} %collective-permute-done.9.yhi_ref, ...), custom_call_target="tpu_custom_call" | custom-call | tf_op jit(solution)/shard_map/finish/pallas_call | solution.py:394
  (32 shorter events, 0.2 us)
Async XLA Ops:
  0.6 1.7 %copy-start = (f32[3,8,32,768]{3,2,1,0:T(8,128)S(1)}, f32[3,8,32,768]{3,2,1,0:T(8,128)}, u32[]{:S(2)}) copy-start(f32[3,8,32,768]{3,2,1,0:T(8,128)} %v_ref.3) | copy-start | bytes 7077892
  2.3 7.1 %copy-start.6 = (s32[1,4,96]{2,1,0:T(4,128)S(1)}, s32[1,4,96]{2,1,0:T(4,128)}, u32[]{:S(2)}) copy-start(s32[1,4,96]{2,1,0:T(4,128)} %param.8) | copy-start | bytes 4612
  2.3 7.1 %copy-start.5 = (s32[8,32]{1,0:T(8,128)S(1)}, s32[8,32]{1,0:T(8,128)}, u32[]{:S(2)}) copy-start(s32[8,32]{1,0:T(8,128)} %param.9) | copy-start | bytes 3076
  2.3 10.8 %copy-start.1 = (f32[3,8,32,768]{3,2,1,0:T(8,128)S(1)}, f32[3,8,32,768]{3,2,1,0:T(8,128)}, u32[]{:S(2)}) copy-start(f32[3,8,32,768]{3,2,1,0:T(8,128)} %v_ref.3) | copy-start | bytes 7077892
  2.4 7.6 %collective-permute-start = (f32[3,8,768]{2,1,0:T(8,128)S(1)}, f32[3,8,768]{2,1,0:T(8,128)S(1)}, u32[]{:S(2)}, u32[]{:S(2)}) collective-permute-start(f32[3,8,768]{2,1,0:T(8,128)S(1)} %get-tuple-element.20), channel_id=1, source_target_pairs={{0,1},{1,2},{2,3},{3,4},{4,5},{5,6},{6,7},{8,9},{9,10},{10,11},{11... | collective-permute-start | bytes 221192 | tf_op jit(solution)/shard_map/ppermute | solution.py:297
  7.4 5.7 %collective-permute-start.1 = (f32[3,8,768]{2,1,0:T(8,128)S(1)}, f32[3,8,768]{2,1,0:T(8,128)S(1)}, u32[]{:S(2)}, u32[]{:S(2)}) collective-permute-start(f32[3,8,768]{2,1,0:T(8,128)S(1)} %get-tuple-element.21), channel_id=1, source_target_pairs={{1,0},{2,1},{3,2},{4,3},{5,4},{6,5},{7,6},{9,8},{10,9},{11,10},{12... | collective-permute-start | bytes 221192 | tf_op jit(solution)/shard_map/ppermute | solution.py:297
  9.9 7.9 %copy-start.4 = (f32[768]{0:T(1024)S(1)}, f32[768]{0:T(1024)}, u32[]{:S(2)}) copy-start(f32[768]{0:T(1024)} %constant.80.clone) | copy-start | bytes 9220
  9.9 7.9 %copy-start.7 = (f32[32]{0:T(128)S(1)}, f32[32]{0:T(128)}, u32[]{:S(2)}) copy-start(f32[32]{0:T(128)} %constant.79.clone) | copy-start | bytes 388
  9.9 15.6 %copy-start.2 = (f32[2,128,128]{2,1,0:T(8,128)S(1)}, f32[2,128,128]{2,1,0:T(8,128)}, u32[]{:S(2)}) copy-start(f32[2,128,128]{2,1,0:T(8,128)} %constant.81.clone.zmat_ref) | copy-start | bytes 393220
  9.9 15.6 %copy-start.3 = (f32[2,8,8,128]{3,2,1,0:T(8,128)S(1)}, f32[2,8,8,128]{3,2,1,0:T(8,128)}, u32[]{:S(2)}) copy-start(f32[2,8,8,128]{3,2,1,0:T(8,128)} %constant.82.clone.ycol_ref) | copy-start | bytes 196612
  13.3 8.0 %collective-permute-start.2 = (f32[3,32,768]{2,1,0:T(8,128)S(1)}, f32[3,32,768]{2,1,0:T(8,128)S(1)}, u32[]{:S(2)}, u32[]{:S(2)}) collective-permute-start(f32[3,32,768]{2,1,0:T(8,128)S(1)} %get-tuple-element.22), channel_id=1, source_target_pairs={{0,8},{8,16},{16,24},{24,32},{32,40},{40,48},{48,56},{56,64},{64,7... | collective-permute-start | bytes 884744 | tf_op jit(solution)/shard_map/ppermute | solution.py:297
  16.5 8.9 %collective-permute-start.3 = (f32[3,32,768]{2,1,0:T(8,128)S(1)}, f32[3,32,768]{2,1,0:T(8,128)S(1)}, u32[]{:S(2)}, u32[]{:S(2)}) collective-permute-start(f32[3,32,768]{2,1,0:T(8,128)S(1)} %get-tuple-element.23), channel_id=1, source_target_pairs={{8,0},{16,8},{24,16},{32,24},{40,32},{48,40},{56,48},{64,56},{72,6... | collective-permute-start | bytes 884744 | tf_op jit(solution)/shard_map/ppermute | solution.py:297
  35.4 6.2 %collective-permute-start.4 = (f32[3,8,768]{2,1,0:T(8,128)S(1)}, f32[3,8,768]{2,1,0:T(8,128)S(1)}, u32[]{:S(2)}, u32[]{:S(2)}) collective-permute-start(f32[3,8,768]{2,1,0:T(8,128)S(1)} %get-tuple-element.25), channel_id=1, source_target_pairs={{0,1},{1,2},{2,3},{3,4},{4,5},{5,6},{6,7},{8,9},{9,10},{10,11},{11... | collective-permute-start | bytes 221192 | tf_op jit(solution)/shard_map/ppermute | solution.py:297
  39.6 5.7 %collective-permute-start.5 = (f32[3,8,768]{2,1,0:T(8,128)S(1)}, f32[3,8,768]{2,1,0:T(8,128)S(1)}, u32[]{:S(2)}, u32[]{:S(2)}) collective-permute-start(f32[3,8,768]{2,1,0:T(8,128)S(1)} %get-tuple-element.26), channel_id=1, source_target_pairs={{1,0},{2,1},{3,2},{4,3},{5,4},{6,5},{7,6},{9,8},{10,9},{11,10},{12... | collective-permute-start | bytes 221192 | tf_op jit(solution)/shard_map/ppermute | solution.py:297
  45.4 8.0 %collective-permute-start.6 = (f32[3,32,768]{2,1,0:T(8,128)S(1)}, f32[3,32,768]{2,1,0:T(8,128)S(1)}, u32[]{:S(2)}, u32[]{:S(2)}) collective-permute-start(f32[3,32,768]{2,1,0:T(8,128)S(1)} %get-tuple-element.27), channel_id=1, source_target_pairs={{0,8},{8,16},{16,24},{24,32},{32,40},{40,48},{48,56},{56,64},{64,7... | collective-permute-start | bytes 884744 | tf_op jit(solution)/shard_map/ppermute | solution.py:297
  48.7 8.9 %collective-permute-start.7 = (f32[3,32,768]{2,1,0:T(8,128)S(1)}, f32[3,32,768]{2,1,0:T(8,128)S(1)}, u32[]{:S(2)}, u32[]{:S(2)}) collective-permute-start(f32[3,32,768]{2,1,0:T(8,128)S(1)} %get-tuple-element.28), channel_id=1, source_target_pairs={{8,0},{16,8},{24,16},{32,24},{40,32},{48,40},{56,48},{64,56},{72,6... | collective-permute-start | bytes 884744 | tf_op jit(solution)/shard_map/ppermute | solution.py:297
  67.4 5.8 %collective-permute-start.8 = (f32[3,8,768]{2,1,0:T(8,128)S(1)}, f32[3,8,768]{2,1,0:T(8,128)S(1)}, u32[]{:S(2)}, u32[]{:S(2)}) collective-permute-start(f32[3,8,768]{2,1,0:T(8,128)S(1)} %get-tuple-element.31), channel_id=1, source_target_pairs={{0,1},{1,2},{2,3},{3,4},{4,5},{5,6},{6,7},{8,9},{9,10},{10,11},{11... | collective-permute-start | bytes 221192 | tf_op jit(solution)/shard_map/ppermute | solution.py:297
  71.3 5.7 %collective-permute-start.9 = (f32[3,8,768]{2,1,0:T(8,128)S(1)}, f32[3,8,768]{2,1,0:T(8,128)S(1)}, u32[]{:S(2)}, u32[]{:S(2)}) collective-permute-start(f32[3,8,768]{2,1,0:T(8,128)S(1)} %get-tuple-element.32), channel_id=1, source_target_pairs={{1,0},{2,1},{3,2},{4,3},{5,4},{6,5},{7,6},{9,8},{10,9},{11,10},{12... | collective-permute-start | bytes 221192 | tf_op jit(solution)/shard_map/ppermute | solution.py:297
  77.1 25.9 %collective-permute-start.10 = (f32[3,32,768]{2,1,0:T(8,128)S(1)}, f32[3,32,768]{2,1,0:T(8,128)S(1)}, u32[]{:S(2)}, u32[]{:S(2)}) collective-permute-start(f32[3,32,768]{2,1,0:T(8,128)S(1)} %get-tuple-element.33), channel_id=1, source_target_pairs={{0,8},{8,16},{16,24},{24,32},{32,40},{40,48},{48,56},{56,64},{64,7... | collective-permute-start | bytes 884744 | tf_op jit(solution)/shard_map/ppermute | solution.py:297
  81.0 22.1 %collective-permute-start.11 = (f32[3,32,768]{2,1,0:T(8,128)S(1)}, f32[3,32,768]{2,1,0:T(8,128)S(1)}, u32[]{:S(2)}, u32[]{:S(2)}) collective-permute-start(f32[3,32,768]{2,1,0:T(8,128)S(1)} %get-tuple-element.34), channel_id=1, source_target_pairs={{8,0},{16,8},{24,16},{32,24},{40,32},{48,40},{56,48},{64,56},{72,6... | collective-permute-start | bytes 884744 | tf_op jit(solution)/shard_map/ppermute | solution.py:297

commit v2 on v1

v2 whole, which is shorter than its diff:
```python
import functools

import jax
import jax.numpy as jnp
import numpy as np
from jax import lax
from jax.experimental import pallas as pl
from jax.experimental.pallas import tpu as pltpu
from jax.sharding import PartitionSpec as P

ORDER = 7
NODES = ORDER + 1
LANES = 128

POISSON = 0.3
LAME_FIRST = POISSON / ((1.0 + POISSON) * (1.0 - 2.0 * POISSON))
LAME_SHEAR = 1.0 / (2.0 * (1.0 + POISSON))
SOLID_MODULUS = 0.1
VOID_MODULUS = 0.001
INTERIOR_POINTS = (
    -0.8717401485096066,
    -0.5917001814331423,
    -0.2092992179024789,
    0.2092992179024789,
    0.5917001814331423,
    0.8717401485096066,
)
VMEM_LIMIT = 16 * 1024 * 1024


def legendre_value(poly_order, point):
    previous = 1.0
    current = point
    for degree in range(1, poly_order):
        following = ((2.0 * degree + 1.0) * point * current - degree * previous) / (degree + 1.0)
        previous = current
        current = following
    return current


def gll_tables(poly_order):
    points = np.array([-1.0] + list(INTERIOR_POINTS) + [1.0])
    values = np.array([legendre_value(poly_order, float(point)) for point in points])
    weights = 2.0 / (poly_order * (poly_order + 1) * values**2)
    node_count = poly_order + 1
    derivative = np.zeros((node_count, node_count))
    for row_index in range(node_count):
        for col_index in range(node_count):
            if row_index != col_index:
                derivative[row_index, col_index] = values[row_index] / (
                    values[col_index] * (points[row_index] - points[col_index])
                )
    derivative[0, 0] = -poly_order * (poly_order + 1) / 4.0
    derivative[poly_order, poly_order] = poly_order * (poly_order + 1) / 4.0
    return (derivative, weights)


DERIV, WEIGHTS = gll_tables(ORDER)
HALF = NODES // 2
ODD = [[0.5 * (DERIV[a, i] - DERIV[a, ORDER - i]) for i in range(HALF)] for a in range(HALF)]
EVEN = [[0.5 * (DERIV[a, i] + DERIV[a, ORDER - i]) for i in range(HALF)] for a in range(HALF)]


def z_table(matrix):
    blocks = np.kron(np.eye(LANES // NODES), matrix).astype(np.float32)
    high = blocks.astype(jnp.bfloat16)
    low = (blocks - high.astype(np.float32)).astype(jnp.bfloat16)
    row = np.concatenate([high, low], axis=1)
    return np.concatenate([row, row], axis=0)


def shared_halves(local_len, offset, global_len, node_count):
    position = jnp.arange(local_len, dtype=jnp.int32)
    node_index = position % node_count
    global_pos = position + offset
    shared = (node_index == 0) & (global_pos > 0) | (node_index == node_count - 1) & (
        global_pos < global_len - 1
    )
    return jnp.where(shared, 0.5, 1.0).astype(jnp.float32)


def combine(coefs, terms):
    total = None
    for coef, term in zip(coefs, terms):
        part = float(coef) * term
        total = part if total is None else total + part
    return total


def parts(n_elem):
    return tuple(range(1, n_elem - 1)), (0, n_elem - 1)


def locate(refs, elem, n_elem):
    if refs[0].shape[2] == n_elem * NODES:
        return refs[0], elem * NODES
    for ref, group in zip(refs, parts(n_elem)):
        if elem in group:
            return ref, group.index(elem) * NODES


def row_sum_y(refs, lo, hi, comp, plane, elem, n_elem):
    ref, base = locate(refs, elem, n_elem)
    own = ref[comp, plane, base : base + NODES, :]
    if elem > 0:
        ref, base = locate(refs, elem - 1, n_elem)
        lo = ref[comp, plane, base + ORDER : base + NODES, :]
    if elem < n_elem - 1:
        ref, base = locate(refs, elem + 1, n_elem)
        hi = ref[comp, plane, base : base + 1, :]
    sub = lax.broadcasted_iota(jnp.int32, own.shape, 0)
    lo = jnp.broadcast_to(lo, own.shape)
    hi = jnp.broadcast_to(hi, own.shape)
    return own + jnp.where(sub == 0, lo, jnp.where(sub == ORDER, hi, 0.0))


def sum_z(rows):
    size = rows.shape[-1]
    lane = lax.broadcasted_iota(jnp.int32, rows.shape, 1)
    ahead = pltpu.roll(rows, size - 1, 1)
    behind = pltpu.roll(rows, 1, 1)
    upper = (lane % NODES == ORDER) & (lane < size - 1)
    lower = (lane % NODES == 0) & (lane > 0)
    return rows + jnp.where(upper, ahead, jnp.where(lower, behind, 0.0))


def release(rows, free):
    return jnp.concatenate([rows[:, :LANES] * free, rows[:, LANES:]], axis=1)


def fold(strip):
    total = strip[:, :LANES]
    for start in range(LANES, strip.shape[1], LANES):
        total = total + strip[:, start : start + LANES]
    return total


def is_upper(axis):
    return lax.axis_index(axis) % 2


def pick(upper, near, far):
    mask = jnp.full(near.shape, upper, jnp.int32) == 1
    return jnp.where(mask, near, far), jnp.where(mask, far, near)


def y_sides(upper, near_ref, far_ref, comp, plane):
    row = slice(plane, plane + 1)
    return pick(upper, near_ref[comp, row, :], far_ref[comp, row, :])


def column_sum(y_col_ref, which, row_of):
    total = None
    for j in range(NODES):
        part = y_col_ref[which, j] * jnp.broadcast_to(row_of(j), (NODES, LANES))
        total = part if total is None else total + part
    return total


def along_z(flat, table):
    high = flat.astype(jnp.bfloat16)
    low = (flat - high.astype(jnp.float32)).astype(jnp.bfloat16)
    both = jnp.dot(
        jnp.concatenate([high, low], axis=1), table, preferred_element_type=jnp.float32
    )
    return both[:, :LANES] + both[:, LANES:]


def main_kernel(*refs, elems, n_elem):
    v_refs, refs = refs[:2], refs[2:]
    if 0 in elems:
        ynear_ref, yfar_ref = refs[:2]
        refs = refs[2:]
    free_ref, elem_ref, half_ref, halfz_ref, zmat_ref, ycol_ref = refs[:6]
    u_ref, k_ref, square_ref = refs[6:9]
    grad_ref, stress_ref, side_ref = refs[9:]
    comps, planes, size_y, size_z = u_ref.shape
    n_tile = size_z // LANES
    y_upper = is_upper("gy")
    square = jnp.zeros((NODES, LANES), jnp.float32)
    for place, elem in enumerate(elems):
        base = elem * NODES
        sub = slice(place * NODES, (place + 1) * NODES)
        for plane in range(planes):
            part = None
            for comp in range(comps):
                lo = hi = None
                if elem in (0, n_elem - 1):
                    lo, hi = y_sides(y_upper, ynear_ref, yfar_ref, comp, plane)
                strip = sum_z(row_sum_y(v_refs, lo, hi, comp, plane, elem, n_elem))
                strip = release(strip, free_ref[plane, base : base + NODES, :])
                u_ref[comp, plane, sub, :] = strip
                part = strip * strip if part is None else part + strip * strip
            if plane not in (0, ORDER):
                part = fold(part * halfz_ref[0:1, :])
                square = square + part * half_ref[plane, base : base + NODES, :]
    square_ref[...] = square

    rows = comps * planes * size_y
    for tile in range(n_tile):
        lanes = slice(tile * LANES, (tile + 1) * LANES)
        flat = u_ref[:, :, :, lanes].reshape(rows, LANES)
        grad_ref[:, :, :, lanes] = along_z(flat, zmat_ref[0]).reshape(
            comps, planes, size_y, LANES
        )

    def block(tile, place):
        lanes = pl.ds(pl.multiple_of(tile * LANES, LANES), LANES)
        base = place * NODES
        sub = slice(base, base + NODES)
        even, odd = [], []
        for comp in range(3):
            vals = [u_ref[comp, i, sub, lanes] for i in range(NODES)]
            even.append([vals[i] + vals[ORDER - i] for i in range(HALF)])
            odd.append([vals[i] - vals[ORDER - i] for i in range(HALF)])
        scale = elem_ref[elems[place] * NODES : (elems[place] + 1) * NODES, lanes]
        xsum = [[None] * HALF for _ in range(3)]
        xdif = [[None] * HALF for _ in range(3)]
        for pair in range(HALF):
            first = [combine(ODD[pair], odd[c]) for c in range(3)]
            second = [combine(EVEN[pair], even[c]) for c in range(3)]
            side_x = []
            for plane, sign in ((pair, 1), (ORDER - pair, -1)):
                gx = [first[c] + second[c] if sign > 0 else first[c] - second[c] for c in range(3)]
                gy = [
                    column_sum(
                        ycol_ref, 0, lambda j: u_ref[c, plane, base + j : base + j + 1, lanes]
                    )
                    for c in range(3)
                ]
                gz = [grad_ref[c, plane, sub, lanes] for c in range(3)]
                shear = scale * float(LAME_SHEAR * WEIGHTS[plane])
                twice = scale * float(2.0 * LAME_SHEAR * WEIGHTS[plane])
                spread = (gx[0] + gy[1] + gz[2]) * (scale * float(LAME_FIRST * WEIGHTS[plane]))
                sxx = twice * gx[0] + spread
                syy = twice * gy[1] + spread
                szz = twice * gz[2] + spread
                sxy = shear * (gx[1] + gy[0])
                sxz = shear * (gx[2] + gz[0])
                syz = shear * (gy[2] + gz[1])
                side_x.append((sxx, sxy, sxz))
                for c, value in enumerate((sxz, syz, szz)):
                    stress_ref[c, plane, sub, lanes] = value
                for c, value in enumerate((sxy, syy, syz)):
                    side_ref[c, plane, :, :] = value
            for c in range(3):
                se = side_x[0][c] + side_x[1][c]
                so = side_x[0][c] - side_x[1][c]
                for i in range(HALF):
                    add_x = float(EVEN[pair][i]) * so
                    add_y = float(ODD[pair][i]) * se
                    xsum[c][i] = add_x if pair == 0 else xsum[c][i] + add_x
                    xdif[c][i] = add_y if pair == 0 else xdif[c][i] + add_y
        for c in range(3):
            for plane in range(NODES):
                i = min(plane, ORDER - plane)
                total = xsum[c][i] + xdif[c][i] if plane < HALF else xsum[c][i] - xdif[c][i]
                k_ref[c, plane, sub, lanes] = total + column_sum(
                    ycol_ref, 1, lambda b: side_ref[c, plane, b : b + 1, :]
                )

    @pl.loop(0, n_tile)
    def _(tile):
        for place in range(len(elems)):
            block(tile, place)

    for tile in range(n_tile):
        lanes = slice(tile * LANES, (tile + 1) * LANES)
        flat = stress_ref[:, :, :, lanes].reshape(rows, LANES)
        k_ref[:, :, :, lanes] += along_z(flat, zmat_ref[1]).reshape(comps, planes, size_y, LANES)


SHEAR, FIRST = float(LAME_SHEAR), float(LAME_FIRST)
DIAG = 2.0 * SHEAR + FIRST
ENDS = (0, ORDER)
THROUGH = np.einsum("ai,a,ap->ip", DERIV, WEIGHTS, DERIV)
ONWARD = DERIV.T
BACKWARD = WEIGHTS[:, None] * DERIV


def spread_pair(total_p, total_m, table, i, sign, even, odd):
    alpha = 0.5 * float(table[i, 0] + table[i, ORDER]) * even
    beta = 0.5 * float(table[i, 0] - table[i, ORDER]) * odd
    plus, minus = (alpha, beta) if sign > 0 else (beta, alpha)
    if total_p is None:
        return plus, minus
    return total_p + plus, total_m + minus


def update_kernel(*refs, elems, n_elem, slot, last):
    u_ref, kin_ref, xnear_ref, xfar_ref = refs[:4]
    free_ref, elem_ref, half_ref, halfz_ref, zmat_ref, ycol_ref = refs[4:10]
    squares_refs, refs = (refs[10:12], refs[12:]) if 0 in elems else ((), refs[10:])
    carry_ref, k_ref, face_ref, sums_ref = refs[:4]
    refs = refs[4:]
    if 0 in elems:
        near_ref, far_ref = refs[:2]
        refs = refs[2:]
    add_ref, grad_ref, keep_ref, zin_ref, zout_ref, side_ref = refs
    comps, planes, size_y, size_z = k_ref.shape
    n_tile = size_z // LANES
    x_upper = is_upper("gx")
    square = jnp.zeros((NODES, LANES), jnp.float32)
    for ref in squares_refs:
        square = square + ref[...]
    for place, elem in enumerate(elems):
        rows = slice(elem * NODES, (elem + 1) * NODES)
        own = slice(place * NODES, (place + 1) * NODES)
        for end, plane in enumerate(ENDS):
            part = None
            for comp in range(comps):
                strip = pick(x_upper, xnear_ref[comp, rows, :], xfar_ref[comp, rows, :])[end]
                strip = release(sum_z(strip), free_ref[plane, rows, :])
                add_ref[comp, end, own, :] = strip
                strip = strip + u_ref[comp, plane, own, :]
                face_ref[comp, end, own, :] = strip
                part = strip * strip if part is None else part + strip * strip
            square = square + fold(part * halfz_ref[0:1, :]) * half_ref[plane, rows, :]

    for tile in range(n_tile):
        lanes = slice(tile * LANES, (tile + 1) * LANES)
        flat = add_ref[:, :, :, lanes].reshape(comps * 2 * size_y, LANES)
        grad_ref[:, :, :, lanes] = along_z(flat, zmat_ref[0]).reshape(comps, 2, size_y, LANES)

    @pl.loop(0, n_tile)
    def _(tile):
        lanes = pl.ds(pl.multiple_of(tile * LANES, LANES), LANES)
        for place, elem in enumerate(elems):
            base = place * NODES
            sub = slice(base, base + NODES)
            scale = elem_ref[elem * NODES : (elem + 1) * NODES, lanes]
            for end, plane in enumerate(ENDS):
                gy = [
                    column_sum(
                        ycol_ref, 0, lambda j: add_ref[c, end, base + j : base + j + 1, lanes]
                    )
                    for c in range(3)
                ]
                gz = [grad_ref[c, end, sub, lanes] for c in range(3)]
                own = scale * float(WEIGHTS[plane])
                axx = own * (FIRST * (gy[1] + gz[2]))
                axy = own * (SHEAR * gy[0])
                axz = own * (SHEAR * gz[0])
                ayy = own * (DIAG * gy[1] + FIRST * gz[2])
                azz = own * (DIAG * gz[2] + FIRST * gy[1])
                ayz = own * (SHEAR * (gy[2] + gz[1]))
                scaled = [scale * add_ref[c, end, sub, lanes] for c in range(3)]
                for c, value in enumerate((SHEAR * scaled[2], FIRST * scaled[0], axz, ayz, azz)):
                    zin_ref[c, end, sub, lanes] = value
                for c, value in enumerate((SHEAR * scaled[1], FIRST * scaled[0], axy, ayy, ayz)):
                    side_ref[c, end, :, :] = value
                for c, value in enumerate((axx, axy, axz)):
                    keep_ref[c, end, sub, lanes] = value
                for c in range(5):
                    keep_ref[3 + c, end, sub, lanes] = column_sum(
                        ycol_ref, 1, lambda b: side_ref[c, end, b : b + 1, :]
                    )

    for tile in range(n_tile):
        lanes = slice(tile * LANES, (tile + 1) * LANES)
        flat = zin_ref[:, :, :, lanes].reshape(5 * 2 * size_y, LANES)
        zout_ref[:, :, :, lanes] = along_z(flat, zmat_ref[1]).reshape(5, 2, size_y, LANES)

    def tile_energy(tile, energy):
        lanes = pl.ds(pl.multiple_of(tile * LANES, LANES), LANES)
        for place, elem in enumerate(elems):
            sub = slice(place * NODES, (place + 1) * NODES)
            scale = elem_ref[elem * NODES : (elem + 1) * NODES, lanes]
            zout = [[zout_ref[c, end, sub, lanes] for end in range(2)] for c in range(5)]
            kept = [[keep_ref[c, end, sub, lanes] for end in range(2)] for c in range(8)]
            back = (
                [kept[3][end] + zout[0][end] for end in range(2)],
                kept[4],
                zout[1],
            )
            for c in range(3):
                factor = scale * (DIAG if c == 0 else SHEAR)
                pairs = (
                    ([factor * add_ref[c, end, sub, lanes] for end in range(2)], THROUGH, 1),
                    (kept[c], ONWARD, -1),
                    (back[c], BACKWARD, -1),
                )
                pairs = [(v[0] + v[1], v[0] - v[1], table, sign) for v, table, sign in pairs]
                for i in range(HALF):
                    plus = minus = None
                    for even, odd, table, sign in pairs:
                        plus, minus = spread_pair(plus, minus, table, i, sign, even, odd)
                    for plane, value in ((i, plus + minus), (ORDER - i, plus - minus)):
                        value = value + kin_ref[c, plane, sub, lanes]
                        if plane in ENDS:
                            end = ENDS.index(plane)
                            value = value + (kept[5 + c][end] + zout[2 + c][end])
                            vector = face_ref[c, end, sub, lanes]
                        else:
                            vector = u_ref[c, plane, sub, lanes]
                        k_ref[c, plane, sub, lanes] = value
                        energy = energy + value * vector
        return energy

    energy = lax.fori_loop(0, n_tile, tile_energy, jnp.zeros((NODES, LANES), jnp.float32))
    if 0 in elems:
        put_rows(
            lambda comp, plane: k_ref[comp, plane, 0:1, :],
            lambda comp, plane: k_ref[comp, plane, size_y - 1 : size_y, :],
            near_ref,
            far_ref,
        )
    moments = [carry_ref[i] for i in range(4)]
    moments[2 * slot] = moments[2 * slot] + square
    moments[2 * slot + 1] = moments[2 * slot + 1] + energy
    if not last:
        for i in range(4):
            sums_ref[i] = moments[i]
    else:
        lane = lax.broadcasted_iota(jnp.int32, sums_ref.shape, 1)
        known = jnp.zeros(sums_ref.shape, jnp.float32)
        for i in range(4):
            known = jnp.where(lane == i, jnp.sum(moments[i]), known)
        sums_ref[...] = known


def put_rows(lo_of, hi_of, near_ref, far_ref):
    y_upper = is_upper("gy")
    comps, planes, _ = near_ref.shape
    for comp in range(comps):
        for plane in range(planes):
            row = slice(plane, plane + 1)
            far_ref[comp, row, :], near_ref[comp, row, :] = pick(
                y_upper, hi_of(comp, plane), lo_of(comp, plane)
            )


def rows_kernel(v_ref, near_ref, far_ref):
    size_y = v_ref.shape[2]
    put_rows(
        lambda comp, plane: v_ref[comp, plane, 0:1, :],
        lambda comp, plane: v_ref[comp, plane, size_y - 1 : size_y, :],
        near_ref,
        far_ref,
    )


def faces_kernel(vmid_ref, vedge_ref, ynear_ref, yfar_ref, near_ref, far_ref):
    comps, size_y, _ = near_ref.shape
    n_elem = size_y // NODES
    x_upper, y_upper = is_upper("gx"), is_upper("gy")
    v_refs = vmid_ref, vedge_ref
    for comp in range(comps):
        sides = [y_sides(y_upper, ynear_ref, yfar_ref, comp, plane) for plane in ENDS]
        for elem in range(n_elem):
            rows = slice(elem * NODES, (elem + 1) * NODES)
            lo, hi = [
                row_sum_y(v_refs, *side, comp, plane, elem, n_elem)
                for plane, side in zip(ENDS, sides)
            ]
            near_ref[comp, rows, :], far_ref[comp, rows, :] = pick(x_upper, lo, hi)


def finish_kernel(*refs):
    k_refs = refs[:2]
    ynear_ref, yfar_ref, xnear_ref, xfar_ref, free_ref = refs[2:7]
    r_refs, r_faces, q_refs, q_faces = refs[7:9], refs[9:11], refs[11:13], refs[13:15]
    sums_ref, adj_out, res_out, adj_ref, res_ref, sem_ref = refs[15:]
    planes, comps, size_y, _ = adj_ref.shape
    n_elem = size_y // NODES
    x_upper, y_upper = is_upper("gx"), is_upper("gy")
    sums = jnp.sum(sums_ref[...], axis=0, keepdims=True)
    lane = lax.broadcasted_iota(jnp.int32, sums.shape, 1)
    m0, m1, m2, m3 = [
        jnp.sum(jnp.where(lane == i, sums, 0.0), axis=1, keepdims=True) for i in range(4)
    ]
    first = m0 / m1
    following = first * first * m2 - m0
    ratio = following / m0
    grow = 1.0 + ratio
    second = following / (grow * grow * m1 - 2.0 * first * grow * m2 + first * first * m3)
    lead = first + second * grow
    cross = first * second
    copies = []
    for plane in range(planes):
        for elem in range(n_elem):
            sub = slice(elem * NODES, (elem + 1) * NODES)
            end = ENDS.index(plane) if plane in ENDS else None
            place = plane if end is None else end
            r_ref, row = locate(r_refs if end is None else r_faces, elem, n_elem)
            q_ref, row = locate(q_refs if end is None else q_faces, elem, n_elem)
            own = slice(row, row + NODES)
            for comp in range(comps):
                lo = hi = None
                if elem in (0, n_elem - 1):
                    lo, hi = y_sides(y_upper, ynear_ref, yfar_ref, comp, plane)
                strip = row_sum_y(k_refs, lo, hi, comp, plane, elem, n_elem)
                if end is not None:
                    strip = strip + pick(x_upper, xnear_ref[comp, sub, :], xfar_ref[comp, sub, :])[end]
                loads = r_ref[comp, place, own, :]
                image = q_ref[comp, place, own, :]
                strip = release(sum_z(strip), free_ref[plane, sub, :])
                adj_ref[plane, comp, sub, :] = lead * loads - cross * image
                res_ref[plane, comp, sub, :] = loads - lead * image + cross * strip
        for which, (ref, out) in enumerate(((adj_ref, adj_out), (res_ref, res_out))):
            copy = pltpu.make_async_copy(ref.at[plane], out.at[:, plane], sem_ref.at[which, plane])
            copy.start()
            copies.append(copy)
    for copy in copies:
        copy.wait()


def swap(near_out, far_out, axis):
    count = lax.axis_size(axis)
    inner = [(i, i ^ 1) for i in range(count)]
    outer = [(i, ((i + 1) ^ 1) - 1) for i in range(1, count - 1)]
    far = lax.ppermute(far_out, axis, outer)
    near = lax.ppermute(near_out, axis, inner)
    return near, far


def local(rhs_loads, flags, fixed):
    comps, size_x, size_y, size_z = rhs_loads.shape
    axes = ("gx", "gy")
    devices = lax.axis_size("gx") * lax.axis_size("gy")
    f32 = jnp.float32
    y_side = jax.ShapeDtypeStruct((comps, size_x, size_z), f32)
    x_side = jax.ShapeDtypeStruct((comps, size_y, size_z), f32)
    whole = pl.BlockSpec(memory_space=pltpu.VMEM)

    modulus = jnp.where(flags[0] == 1, SOLID_MODULUS, VOID_MODULUS).astype(f32)
    modulus = jnp.repeat(jnp.repeat(modulus, NODES, axis=0), NODES, axis=1)
    weight_y = jnp.asarray(np.tile(WEIGHTS, size_y // NODES), f32)
    weight_z = jnp.asarray(np.tile(WEIGHTS, size_z // NODES), f32)
    elem_scale = modulus * weight_y[:, None] * weight_z[None, :]
    free = 1.0 - fixed.astype(f32)[:, :, None] * (jnp.arange(LANES) == 0).astype(f32)
    half_xy = (
        shared_halves(size_x, lax.axis_index("gx") * size_x, size_x * lax.axis_size("gx"), NODES)[
            :, None, None
        ]
        * shared_halves(
            size_y, lax.axis_index("gy") * size_y, size_y * lax.axis_size("gy"), NODES
        )[None, :, None]
        * jnp.ones((LANES,), f32)
    )
    half_z = jnp.broadcast_to(shared_halves(size_z, 0, size_z, NODES)[None], (NODES, size_z))
    z_mat = jnp.asarray(np.stack([z_table(DERIV.T), z_table(DERIV)]))
    y_col = jnp.asarray(
        np.broadcast_to(
            np.stack([DERIV.T, DERIV])[:, :, :, None], (2, NODES, NODES, LANES)
        ),
        f32,
    )

    n_elem = size_y // NODES
    mid, edge = parts(n_elem)
    tables = (free, elem_scale, half_xy, half_z, z_mat, y_col)

    def shape(*sizes):
        return jax.ShapeDtypeStruct(sizes, f32)

    def call(
        kernel, name, args, out_shape, scratch=(), us=1.0, out_spec=whole
    ):
        return pl.pallas_call(
            kernel,
            in_specs=[whole] * len(args),
            out_specs=[out_spec] * len(out_shape),
            out_shape=list(out_shape),
            scratch_shapes=list(scratch),
            compiler_params=pltpu.CompilerParams(vmem_limit_bytes=VMEM_LIMIT),
            cost_estimate=pl.CostEstimate(
                flops=int(us * 4e6), bytes_accessed=int(us * 2.5e6), transcendentals=0
            ),
            name=name,
        )(*args)

    def main(v, y_halo, elems, name):
        some = (comps, size_x, len(elems) * NODES, size_z)
        return call(
            functools.partial(main_kernel, elems=elems, n_elem=n_elem),
            name,
            (*v, *y_halo, *tables),
            (shape(*some), shape(*some), shape(NODES, LANES)),
            (
                pltpu.VMEM(some, f32),
                pltpu.VMEM(some, f32),
                pltpu.VMEM((comps, size_x, NODES, LANES), f32),
            ),
            us=5.0,
        )

    def update(u, k, x_halo, squares, carry, elems, slot, name):
        rows = len(elems) * NODES
        last = slot == 1 and 0 not in elems
        out = [
            shape(comps, size_x, rows, size_z),
            shape(comps, 2, rows, size_z),
            shape(devices, LANES) if last else shape(4, NODES, LANES),
        ]
        if 0 in elems:
            out += [y_side, y_side]
        return call(
            functools.partial(update_kernel, elems=elems, n_elem=n_elem, slot=slot, last=last),
            name,
            (u, k, *x_halo, *tables, *squares, carry),
            out,
            (
                pltpu.VMEM((comps, 2, rows, size_z), f32),
                pltpu.VMEM((comps, 2, rows, size_z), f32),
                pltpu.VMEM((8, 2, rows, size_z), f32),
                pltpu.VMEM((5, 2, rows, size_z), f32),
                pltpu.VMEM((5, 2, rows, size_z), f32),
                pltpu.VMEM((5, 2, NODES, LANES), f32),
            ),
            us=2.0,
        )

    def halos(v, y_rows):
        y_halo = swap(*y_rows, "gy")
        sides = call(faces_kernel, "faces", (*v, *y_halo), (x_side, x_side), us=0.3)
        return y_halo, swap(*sides, "gx")

    def step(v, y_rows, carry, slot):
        y_halo, x_halo = halos(v, y_rows)
        u_mid, k_mid, sq_mid = main(v, (), mid, "middle")
        u_edge, k_edge, sq_edge = main(v, y_halo, edge, "edges")
        k_edge, f_edge, carry, *y_rows = update(
            u_edge, k_edge, x_halo, (sq_mid, sq_edge), carry, edge, slot, "update_edges"
        )
        k_mid, f_mid, carry = update(
            u_mid, k_mid, x_halo, (), carry, mid, slot, "update_middle"
        )
        return (k_mid, k_edge), (u_mid, u_edge, f_mid, f_edge), y_rows, carry

    y_rows = call(rows_kernel, "rows", (rhs_loads,), (y_side, y_side), us=0.1)
    carry = jnp.zeros((4, NODES, LANES), f32)
    k_loads, loads, y_rows, carry = step((rhs_loads, rhs_loads), y_rows, carry, 0)
    k_image, image, y_rows, sums = step(k_loads, y_rows, carry, 1)
    y_halo, x_halo = halos(k_image, y_rows)
    sums = lax.all_to_all(sums, axes, 0, 0, tiled=True)
    return tuple(
        call(
            finish_kernel,
            "finish",
            (*k_image, *y_halo, *x_halo, free, *loads, *image, sums),
            (shape(*rhs_loads.shape),) * 2,
            (
                pltpu.VMEM((size_x, comps, size_y, size_z), f32),
                pltpu.VMEM((size_x, comps, size_y, size_z), f32),
                pltpu.SemaphoreType.DMA((2, size_x)),
            ),
            us=4.0,
            out_spec=pl.BlockSpec(memory_space=pltpu.HBM),
        )
    )


def solution(mesh):
    in_specs = (P(None, "gx", "gy", None), P("gx", "gy", None), P("gx", "gy"))
    out_specs = (P(None, "gx", "gy", None), P(None, "gx", "gy", None))
    return jax.shard_map(local, mesh=mesh, in_specs=in_specs, out_specs=out_specs, check_vma=False)
```

time: 107 us -> 78.6 us (0.73)
  waiting for transfers between devices: 25.5 us -> 1.95 us
  starting transfers between devices: 33.3 us -> 25.5 us
  Pallas kernels: 23.9 us -> 25.5 us
  blocking collectives: 20.8 us -> 21.9 us
    ppermute x12, waiting for transfers between devices: 25.5 us -> 1.95 us  [the longest x6 1.93 us: swap(): far = lax.ppermute(far_out, axis, outer)]
    ppermute x12, starting transfers between devices: 33.3 us -> 25.5 us  [the longest x6 13.6 us: swap(): far = lax.ppermute(far_out, axis, outer)]
    pallas_call x7 -> x13, Pallas kernels: 23.9 us -> 25.5 us  [call(): pl.pallas_call(kernel, in_specs=[whole] * len(args), out_specs=[out_spec]...]
    all_to_all x1, blocking collectives: 20.8 us -> 21.9 us  [local(): sums = lax.all_to_all(sums, axes, 0, 0, tiled=True)]
  transfers between devices with their start and end apart: 12 -> 12, of which waited for: 7 -> 2; matrix products, arithmetic and copies ran while one was open for 0% -> 1% of each run, Pallas kernels for 0% -> 24%
where the time goes in v2:
time: 78.6 us; the launch traced here: 78.3 us
  Pallas kernels  25.5 us (32%)
  starting transfers between devices  25.5 us (32%)
  blocking collectives  21.9 us (28%)
  local copies, waits for them, and re-layouts  2.04 us (3%)
  waiting for transfers between devices  1.95 us (2%)
  between operations  1.18 us (2%)
    pallas_call x13, Pallas kernels, call(): pl.pallas_call(kernel, in_specs=[whole] * len(args), out_specs=[out_spec]...  25.5 us
    all_to_all x1, blocking collectives, local(): sums = lax.all_to_all(sums, axes, 0, 0, tiled=True)  21.9 us
    ppermute x6, starting transfers between devices, swap(): far = lax.ppermute(far_out, axis, outer)  13.6 us
    ppermute x6, starting transfers between devices, swap(): near = lax.ppermute(near_out, axis, inner)  11.9 us
    ppermute x6, waiting for transfers between devices, swap(): far = lax.ppermute(far_out, axis, outer)  1.93 us
    unnamed x16, local copies, waits for them, and re-layouts  1.69 us
  transfers between devices with their start and end apart: 12, of which 2 were waited for; matrix products, arithmetic and copies ran while one was open for 1% of the time, Pallas kernels for 24%

profile of v2, /device:TPU:1, one launch (start us, length us, event | category | flops | bytes accessed | tf_op | source)
XLA Modules:
  0.0 78.3 jit_solution(7906314999008341622)
XLA Ops:
  0.6 1.7 %copy-done = f32[3,8,32,768]{3,2,1,0:T(8,128)S(1)} copy-done((f32[3,8,32,768]{3,2,1,0:T(8,128)S(1)}, f32[3,8,32,768]{3,2,1,0:T(8,128)}, u32[]{:S(2)}) %copy-start) | copy-done | bytes 2359320
  2.4 1.5 %collective-permute-start = (f32[3,8,768]{2,1,0:T(8,128)S(1)}, f32[3,8,768]{2,1,0:T(8,128)S(1)}, u32[]{:S(2)}, u32[]{:S(2)}) collective-permute-start(f32[3,8,768]{2,1,0:T(8,128)S(1)} %get-tuple-element.40), channel_id=1, source_target_pairs={{0,1},{1,0},{2,3},{3,2},{4,5},{5,4},{6,7},{7,6},{8,9},{9,8},{10,11... | collective-permute-start | bytes 221192 | tf_op jit(solution)/shard_map/ppermute | solution.py:513
  3.9 3.7 %collective-permute-start.1 = (f32[3,8,768]{2,1,0:T(8,128)S(1)}, f32[3,8,768]{2,1,0:T(8,128)S(1)}, u32[]{:S(2)}, u32[]{:S(2)}) collective-permute-start(f32[3,8,768]{2,1,0:T(8,128)S(1)} %get-tuple-element.41), channel_id=1, source_target_pairs={{1,2},{2,1},{3,4},{4,3},{5,6},{6,5},{9,10},{10,9},{11,12},{12,11},... | collective-permute-start | bytes 221192 | tf_op jit(solution)/shard_map/ppermute | solution.py:512
  7.6 0.1 copy.13
  7.8 0.1 multiply_subtract_fusion.refs_2_.refs_4_.refs_6_
  7.9 0.1 copy.14
  8.1 1.7 %collective-permute-done.1.yfar_ref.refs_3_ = f32[3,8,768]{2,1,0:T(8,128)S(1)} collective-permute-done((f32[3,8,768]{2,1,0:T(8,128)S(1)}, f32[3,8,768]{2,1,0:T(8,128)S(1)}, u32[]{:S(2)}, u32[]{:S(2)}) %collective-permute-start.1) | collective-permute-done | bytes 73760 | tf_op jit(solution)/shard_map/ppermute | solution.py:512
  9.8 0.1 faces.3
  10.0 1.4 %collective-permute-start.2 = (f32[3,32,768]{2,1,0:T(8,128)S(1)}, f32[3,32,768]{2,1,0:T(8,128)S(1)}, u32[]{:S(2)}, u32[]{:S(2)}) collective-permute-start(f32[3,32,768]{2,1,0:T(8,128)S(1)} %get-tuple-element.42), channel_id=1, source_target_pairs={{0,8},{8,0},{16,24},{24,16},{32,40},{40,32},{48,56},{56,48},{64,72... | collective-permute-start | bytes 884744 | tf_op jit(solution)/shard_map/ppermute | solution.py:513
  11.4 0.7 collective-permute-start.3
  12.2 0.1 mul.70.refs_4_.refs_6_
  12.3 3.7 %middle.2 = (f32[3,8,16,768]{3,2,1,0:T(8,128)S(1)}, f32[3,8,16,768]{3,2,1,0:T(8,128)S(1)}, f32[8,128]{1,0:T(8,128)S(1)}) custom-call(f32[3,8,32,768]{3,2,1,0:T(8,128)S(1)} %copy-done.1, f32[3,8,32,768]{3,2,1,0:T(8,128)S(1)} %copy-done.1, f32[8,32,128]{2,1,0:T(8,128)S(1)} %multiply_subtract_fusion.refs_2_.refs_4_.refs_6_, ...), custom_call_target="tpu_custom_call" | custom-call | flops 20000000 | bytes 12500000 | tf_op jit(solution)/shard_map/middle/pallas_call | solution.py:560
  16.0 3.7 %edges.2 = (f32[3,8,16,768]{3,2,1,0:T(8,128)S(1)}, f32[3,8,16,768]{3,2,1,0:T(8,128)S(1)}, f32[8,128]{1,0:T(8,128)S(1)}) custom-call(f32[3,8,32,768]{3,2,1,0:T(8,128)S(1)} %copy-done.1, f32[3,8,32,768]{3,2,1,0:T(8,128)S(1)} %copy-done.1, f32[3,8,768]{2,1,0:T(8,128)S(1)} %collective-permute-done.ynear_ref.refs_2_, ...), custom_call_target="tpu_custom_call" | custom-call | flops 20000000 | bytes 12500000 | tf_op jit(solution)/shard_map/edges/pallas_call | solution.py:560
  19.8 1.9 %update_edges.2 = (f32[3,8,16,768]{3,2,1,0:T(8,128)S(1)}, f32[3,2,16,768]{3,2,1,0:T(8,128)S(1)}, f32[4,8,128]{2,1,0:T(8,128)S(1)}, f32[3,8,768]{2,1,0:T(8,128)S(1)}, f32[3,8,768]{2,1,0:T(8,128)S(1)}) custom-call(f32[3,8,16,768]{3,2,1,0:T(8,128)S(1)} %get-tuple-element.44.refs_0_.refs_8_, f32[3,8,16,768]{3,2,1,0:T(8,128)S(1)} %get-tuple-element.45.refs_1_, ...), custom_call_target="tpu_custom_call" | custom-call | flops 8000000 | bytes 5000000 | tf_op jit(solution)/shard_map/update_edges/pallas_call | solution.py:560
  21.7 0.1 collective-permute-start.4
  21.8 3.6 %collective-permute-start.5 = (f32[3,8,768]{2,1,0:T(8,128)S(1)}, f32[3,8,768]{2,1,0:T(8,128)S(1)}, u32[]{:S(2)}, u32[]{:S(2)}) collective-permute-start(f32[3,8,768]{2,1,0:T(8,128)S(1)} %get-tuple-element.54), channel_id=1, source_target_pairs={{1,2},{2,1},{3,4},{4,3},{5,6},{6,5},{9,10},{10,9},{11,12},{12,11},... | collective-permute-start | bytes 221192 | tf_op jit(solution)/shard_map/ppermute | solution.py:512
  25.4 1.8 %update_middle.2 = (f32[3,8,16,768]{3,2,1,0:T(8,128)S(1)}, f32[3,2,16,768]{3,2,1,0:T(8,128)S(1)}, f32[4,8,128]{2,1,0:T(8,128)S(1)}) custom-call(f32[3,8,16,768]{3,2,1,0:T(8,128)S(1)} %get-tuple-element.38.refs_0_.refs_7_, f32[3,8,16,768]{3,2,1,0:T(8,128)S(1)} %get-tuple-element.39.refs_1_, f32[3,32,768]{2,1,0:T(8,128)S(1)} %collective-permute-done.2.refs_2_, ...), custom_call_target="tpu_custom_call" | custom-call | flops 8000000 | bytes 5000000 | tf_op jit(solution)/shard_map/update_middle/pallas_call | solution.py:560
  27.2 0.2 collective-permute-done.5.yfar_ref.refs_3_
  27.4 0.1 faces.4
  27.6 3.8 %collective-permute-start.6 = (f32[3,32,768]{2,1,0:T(8,128)S(1)}, f32[3,32,768]{2,1,0:T(8,128)S(1)}, u32[]{:S(2)}, u32[]{:S(2)}) collective-permute-start(f32[3,32,768]{2,1,0:T(8,128)S(1)} %get-tuple-element.55), channel_id=1, source_target_pairs={{0,8},{8,0},{16,24},{24,16},{32,40},{40,32},{48,56},{56,48},{64,72... | collective-permute-start | bytes 884744 | tf_op jit(solution)/shard_map/ppermute | solution.py:513
  31.4 0.7 collective-permute-start.7
  32.1 3.7 %middle.3 = (f32[3,8,16,768]{3,2,1,0:T(8,128)S(1)}, f32[3,8,16,768]{3,2,1,0:T(8,128)S(1)}, f32[8,128]{1,0:T(8,128)S(1)}) custom-call(f32[3,8,16,768]{3,2,1,0:T(8,128)S(1)} %get-tuple-element.49.refs_0_.vmid_ref, f32[3,8,16,768]{3,2,1,0:T(8,128)S(1)} %get-tuple-element.50.refs_1_.vedge_ref, f32[8,32,128]{2,1,0:T(8,128)S(1)} %multiply_subtract_fusion.refs_2_.refs_4_.refs_6_, ...), custom_call_target="tpu_custom_call" | custom-call | flops 20000000 | bytes 12500000 | tf_op jit(solution)/shard_map/middle/pallas_call | solution.py:560
  35.8 3.7 %edges.3 = (f32[3,8,16,768]{3,2,1,0:T(8,128)S(1)}, f32[3,8,16,768]{3,2,1,0:T(8,128)S(1)}, f32[8,128]{1,0:T(8,128)S(1)}) custom-call(f32[3,8,16,768]{3,2,1,0:T(8,128)S(1)} %get-tuple-element.49.refs_0_.vmid_ref, f32[3,8,16,768]{3,2,1,0:T(8,128)S(1)} %get-tuple-element.50.refs_1_.vedge_ref, f32[3,8,768]{2,1,0:T(8,128)S(1)} %collective-permute-done.4.ynear_ref.refs_2_, ...), custom_call_target="tpu_custom_call" | custom-call | flops 20000000 | bytes 12500000 | tf_op jit(solution)/shard_map/edges/pallas_call | solution.py:560
  39.5 1.9 %update_edges.3 = (f32[3,8,16,768]{3,2,1,0:T(8,128)S(1)}, f32[3,2,16,768]{3,2,1,0:T(8,128)S(1)}, f32[4,8,128]{2,1,0:T(8,128)S(1)}, f32[3,8,768]{2,1,0:T(8,128)S(1)}, f32[3,8,768]{2,1,0:T(8,128)S(1)}) custom-call(f32[3,8,16,768]{3,2,1,0:T(8,128)S(1)} %get-tuple-element.57.refs_0_.refs_12_, f32[3,8,16,768]{3,2,1,0:T(8,128)S(1)} %get-tuple-element.58.refs_1_, ...), custom_call_target="tpu_custom_call" | custom-call | flops 8000000 | bytes 5000000 | tf_op jit(solution)/shard_map/update_edges/pallas_call | solution.py:560
  41.4 0.1 collective-permute-start.8
  41.5 4.3 %collective-permute-start.9 = (f32[3,8,768]{2,1,0:T(8,128)S(1)}, f32[3,8,768]{2,1,0:T(8,128)S(1)}, u32[]{:S(2)}, u32[]{:S(2)}) collective-permute-start(f32[3,8,768]{2,1,0:T(8,128)S(1)} %get-tuple-element.66), channel_id=1, source_target_pairs={{1,2},{2,1},{3,4},{4,3},{5,6},{6,5},{9,10},{10,9},{11,12},{12,11},... | collective-permute-start | bytes 221192 | tf_op jit(solution)/shard_map/ppermute | solution.py:512
  45.8 2.0 %update_middle.3 = (f32[3,8,16,768]{3,2,1,0:T(8,128)S(1)}, f32[3,2,16,768]{3,2,1,0:T(8,128)S(1)}, f32[128,128]{1,0:T(8,128)S(1)}) custom-call(f32[3,8,16,768]{3,2,1,0:T(8,128)S(1)} %get-tuple-element.51.refs_0_.refs_11_, f32[3,8,16,768]{3,2,1,0:T(8,128)S(1)} %get-tuple-element.52.refs_1_, f32[3,32,768]{2,1,0:T(8,128)S(1)} %collective-permute-done.6.refs_2_, ...), custom_call_target="tpu_custom_call" | custom-call | flops 8000000 | bytes 5000000 | tf_op jit(solution)/shard_map/update_middle/pallas_call | solution.py:560
  47.8 0.1 faces.5
  47.9 5.0 %collective-permute-start.10 = (f32[3,32,768]{2,1,0:T(8,128)S(1)}, f32[3,32,768]{2,1,0:T(8,128)S(1)}, u32[]{:S(2)}, u32[]{:S(2)}) collective-permute-start(f32[3,32,768]{2,1,0:T(8,128)S(1)} %get-tuple-element.67), channel_id=1, source_target_pairs={{0,8},{8,0},{16,24},{24,16},{32,40},{40,32},{48,56},{56,48},{64,72... | collective-permute-start | bytes 884744 | tf_op jit(solution)/shard_map/ppermute | solution.py:513
  52.9 0.7 collective-permute-start.11
  53.6 21.9 %all_to_all.11 = f32[128,1,128]{2,1,0:T(1,128)S(1)} all-to-all(f32[128,1,128]{2,1,0:T(1,128)S(1)} %bitcast.11), channel_id=1, replica_groups=mesh['gx'=16,'gy'=8] {'gx','gy'}, dimensions={0} | all-to-all | bytes 131072 | tf_op jit(solution)/shard_map/all_to_all | solution.py:636
  75.5 2.7 %finish.1 = (f32[3,8,32,768]{3,2,1,0:T(8,128)}, f32[3,8,32,768]{3,2,1,0:T(8,128)}) custom-call(f32[3,8,16,768]{3,2,1,0:T(8,128)S(1)} %get-tuple-element.63.vmid_ref.refs_0_, f32[3,8,16,768]{3,2,1,0:T(8,128)S(1)} %get-tuple-element.64.vedge_ref.refs_1_, f32[3,8,768]{2,1,0:T(8,128)S(1)} %collective-permute-done.8.ynear_ref.refs_2_, ...), custom_call_target="tpu_custom_call" | custom-call | flops 16000000 | bytes 10000000 | tf_op jit(solution)/shard_map/finish/pallas_call | solution.py:560
  (38 shorter events, 0.3 us)
Async XLA Ops:
  0.6 1.7 %copy-start = (f32[3,8,32,768]{3,2,1,0:T(8,128)S(1)}, f32[3,8,32,768]{3,2,1,0:T(8,128)}, u32[]{:S(2)}) copy-start(f32[3,8,32,768]{3,2,1,0:T(8,128)} %refs_1_.3) | copy-start | bytes 7077892
  2.3 5.3 %copy-start.6 = (s32[1,4,96]{2,1,0:T(4,128)S(1)}, s32[1,4,96]{2,1,0:T(4,128)}, u32[]{:S(2)}) copy-start(s32[1,4,96]{2,1,0:T(4,128)} %param.8) | copy-start | bytes 4612
  2.3 5.3 %copy-start.5 = (s32[8,32]{1,0:T(8,128)S(1)}, s32[8,32]{1,0:T(8,128)}, u32[]{:S(2)}) copy-start(s32[8,32]{1,0:T(8,128)} %param.9) | copy-start | bytes 3076
  2.3 7.5 %copy-start.1 = (f32[3,8,32,768]{3,2,1,0:T(8,128)S(1)}, f32[3,8,32,768]{3,2,1,0:T(8,128)}, u32[]{:S(2)}) copy-start(f32[3,8,32,768]{3,2,1,0:T(8,128)} %refs_1_.3) | copy-start | bytes 7077892
  2.4 5.8 %collective-permute-start = (f32[3,8,768]{2,1,0:T(8,128)S(1)}, f32[3,8,768]{2,1,0:T(8,128)S(1)}, u32[]{:S(2)}, u32[]{:S(2)}) collective-permute-start(f32[3,8,768]{2,1,0:T(8,128)S(1)} %get-tuple-element.40), channel_id=1, source_target_pairs={{0,1},{1,0},{2,3},{3,2},{4,5},{5,4},{6,7},{7,6},{8,9},{9,8},{10,11... | collective-permute-start | bytes 221192 | tf_op jit(solution)/shard_map/ppermute | solution.py:513
  3.9 6.0 %collective-permute-start.1 = (f32[3,8,768]{2,1,0:T(8,128)S(1)}, f32[3,8,768]{2,1,0:T(8,128)S(1)}, u32[]{:S(2)}, u32[]{:S(2)}) collective-permute-start(f32[3,8,768]{2,1,0:T(8,128)S(1)} %get-tuple-element.41), channel_id=1, source_target_pairs={{1,2},{2,1},{3,4},{4,3},{5,6},{6,5},{9,10},{10,9},{11,12},{12,11},... | collective-permute-start | bytes 221192 | tf_op jit(solution)/shard_map/ppermute | solution.py:512
  8.1 4.0 %copy-start.4 = (f32[768]{0:T(1024)S(1)}, f32[768]{0:T(1024)}, u32[]{:S(2)}) copy-start(f32[768]{0:T(1024)} %constant.80.clone) | copy-start | bytes 9220
  8.1 4.0 %copy-start.7 = (f32[32]{0:T(128)S(1)}, f32[32]{0:T(128)}, u32[]{:S(2)}) copy-start(f32[32]{0:T(128)} %constant.79.clone) | copy-start | bytes 388
  8.1 4.2 %copy-start.2 = (bf16[2,256,256]{2,1,0:T(8,128)(2,1)S(1)}, bf16[2,256,256]{2,1,0:T(8,128)(2,1)}, u32[]{:S(2)}) copy-start(bf16[2,256,256]{2,1,0:T(8,128)(2,1)} %constant.81.clone.refs_6_.refs_8_) | copy-start | bytes 786436
  8.1 4.2 %copy-start.3 = (f32[2,8,8,128]{3,2,1,0:T(8,128)S(1)}, f32[2,8,8,128]{3,2,1,0:T(8,128)}, u32[]{:S(2)}) copy-start(f32[2,8,8,128]{3,2,1,0:T(8,128)} %constant.82.clone.refs_7_.refs_9_) | copy-start | bytes 196612
  10.0 9.8 %collective-permute-start.2 = (f32[3,32,768]{2,1,0:T(8,128)S(1)}, f32[3,32,768]{2,1,0:T(8,128)S(1)}, u32[]{:S(2)}, u32[]{:S(2)}) collective-permute-start(f32[3,32,768]{2,1,0:T(8,128)S(1)} %get-tuple-element.42), channel_id=1, source_target_pairs={{0,8},{8,0},{16,24},{24,16},{32,40},{40,32},{48,56},{56,48},{64,72... | collective-permute-start | bytes 884744 | tf_op jit(solution)/shard_map/ppermute | solution.py:513
  11.4 8.3 %collective-permute-start.3 = (f32[3,32,768]{2,1,0:T(8,128)S(1)}, f32[3,32,768]{2,1,0:T(8,128)S(1)}, u32[]{:S(2)}, u32[]{:S(2)}) collective-permute-start(f32[3,32,768]{2,1,0:T(8,128)S(1)} %get-tuple-element.43), channel_id=1, source_target_pairs={{8,16},{16,8},{24,32},{32,24},{40,48},{48,40},{56,64},{64,56},{72,... | collective-permute-start | bytes 884744 | tf_op jit(solution)/shard_map/ppermute | solution.py:512
  21.7 5.6 %collective-permute-start.4 = (f32[3,8,768]{2,1,0:T(8,128)S(1)}, f32[3,8,768]{2,1,0:T(8,128)S(1)}, u32[]{:S(2)}, u32[]{:S(2)}) collective-permute-start(f32[3,8,768]{2,1,0:T(8,128)S(1)} %get-tuple-element.53), channel_id=1, source_target_pairs={{0,1},{1,0},{2,3},{3,2},{4,5},{5,4},{6,7},{7,6},{8,9},{9,8},{10,11... | collective-permute-start | bytes 221192 | tf_op jit(solution)/shard_map/ppermute | solution.py:513
  21.8 5.7 %collective-permute-start.5 = (f32[3,8,768]{2,1,0:T(8,128)S(1)}, f32[3,8,768]{2,1,0:T(8,128)S(1)}, u32[]{:S(2)}, u32[]{:S(2)}) collective-permute-start(f32[3,8,768]{2,1,0:T(8,128)S(1)} %get-tuple-element.54), channel_id=1, source_target_pairs={{1,2},{2,1},{3,4},{4,3},{5,6},{6,5},{9,10},{10,9},{11,12},{12,11},... | collective-permute-start | bytes 221192 | tf_op jit(solution)/shard_map/ppermute | solution.py:512
  27.6 11.9 %collective-permute-start.6 = (f32[3,32,768]{2,1,0:T(8,128)S(1)}, f32[3,32,768]{2,1,0:T(8,128)S(1)}, u32[]{:S(2)}, u32[]{:S(2)}) collective-permute-start(f32[3,32,768]{2,1,0:T(8,128)S(1)} %get-tuple-element.55), channel_id=1, source_target_pairs={{0,8},{8,0},{16,24},{24,16},{32,40},{40,32},{48,56},{56,48},{64,72... | collective-permute-start | bytes 884744 | tf_op jit(solution)/shard_map/ppermute | solution.py:513
  31.4 8.1 %collective-permute-start.7 = (f32[3,32,768]{2,1,0:T(8,128)S(1)}, f32[3,32,768]{2,1,0:T(8,128)S(1)}, u32[]{:S(2)}, u32[]{:S(2)}) collective-permute-start(f32[3,32,768]{2,1,0:T(8,128)S(1)} %get-tuple-element.56), channel_id=1, source_target_pairs={{8,16},{16,8},{24,32},{32,24},{40,48},{48,40},{56,64},{64,56},{72,... | collective-permute-start | bytes 884744 | tf_op jit(solution)/shard_map/ppermute | solution.py:512
  41.4 6.4 %collective-permute-start.8 = (f32[3,8,768]{2,1,0:T(8,128)S(1)}, f32[3,8,768]{2,1,0:T(8,128)S(1)}, u32[]{:S(2)}, u32[]{:S(2)}) collective-permute-start(f32[3,8,768]{2,1,0:T(8,128)S(1)} %get-tuple-element.65), channel_id=1, source_target_pairs={{0,1},{1,0},{2,3},{3,2},{4,5},{5,4},{6,7},{7,6},{8,9},{9,8},{10,11... | collective-permute-start | bytes 221192 | tf_op jit(solution)/shard_map/ppermute | solution.py:513
  41.5 6.3 %collective-permute-start.9 = (f32[3,8,768]{2,1,0:T(8,128)S(1)}, f32[3,8,768]{2,1,0:T(8,128)S(1)}, u32[]{:S(2)}, u32[]{:S(2)}) collective-permute-start(f32[3,8,768]{2,1,0:T(8,128)S(1)} %get-tuple-element.66), channel_id=1, source_target_pairs={{1,2},{2,1},{3,4},{4,3},{5,6},{6,5},{9,10},{10,9},{11,12},{12,11},... | collective-permute-start | bytes 221192 | tf_op jit(solution)/shard_map/ppermute | solution.py:512
  47.9 27.6 %collective-permute-start.10 = (f32[3,32,768]{2,1,0:T(8,128)S(1)}, f32[3,32,768]{2,1,0:T(8,128)S(1)}, u32[]{:S(2)}, u32[]{:S(2)}) collective-permute-start(f32[3,32,768]{2,1,0:T(8,128)S(1)} %get-tuple-element.67), channel_id=1, source_target_pairs={{0,8},{8,0},{16,24},{24,16},{32,40},{40,32},{48,56},{56,48},{64,72... | collective-permute-start | bytes 884744 | tf_op jit(solution)/shard_map/ppermute | solution.py:513
  52.9 22.6 %collective-permute-start.11 = (f32[3,32,768]{2,1,0:T(8,128)S(1)}, f32[3,32,768]{2,1,0:T(8,128)S(1)}, u32[]{:S(2)}, u32[]{:S(2)}) collective-permute-start(f32[3,32,768]{2,1,0:T(8,128)S(1)} %get-tuple-element.68), channel_id=1, source_target_pairs={{8,16},{16,8},{24,32},{32,24},{40,48},{48,40},{56,64},{64,56},{72,... | collective-permute-start | bytes 884744 | tf_op jit(solution)/shard_map/ppermute | solution.py:512

commit v3 on v2

--- a/solution.py
+++ b/solution.py
@@ -25,7 +25,7 @@
     0.5917001814331423,
     0.8717401485096066,
 )
-VMEM_LIMIT = 16 * 1024 * 1024
+VMEM_LIMIT = 10 * 1024 * 1024
 
 
 def legendre_value(poly_order, point):
@@ -149,10 +149,19 @@
     return pick(upper, near_ref[comp, row, :], far_ref[comp, row, :])
 
 
-def column_sum(y_col_ref, which, row_of):
+def x_side(upper, near_ref, far_ref, comp, elem, n_elem, end):
+    rows = side_rows(comp, elem, n_elem)
+    return pick(upper, near_ref[rows, :], far_ref[rows, :])[end]
+
+
+def columns(y_col_ref, which):
+    return [y_col_ref[which, j] for j in range(NODES)]
+
+
+def column_sum(cols, row_of):
     total = None
     for j in range(NODES):
-        part = y_col_ref[which, j] * jnp.broadcast_to(row_of(j), (NODES, LANES))
+        part = cols[j] * jnp.broadcast_to(row_of(j), (NODES, LANES))
         total = part if total is None else total + part
     return total
 
@@ -173,7 +182,7 @@
         refs = refs[2:]
     free_ref, elem_ref, half_ref, halfz_ref, zmat_ref, ycol_ref = refs[:6]
     u_ref, k_ref, square_ref = refs[6:9]
-    grad_ref, stress_ref, side_ref = refs[9:]
+    grad_ref, stress_ref, side_ref, along_ref = refs[9:]
     comps, planes, size_y, size_z = u_ref.shape
     n_tile = size_z // LANES
     y_upper = is_upper("gy")
@@ -208,6 +217,12 @@
         lanes = pl.ds(pl.multiple_of(tile * LANES, LANES), LANES)
         base = place * NODES
         sub = slice(base, base + NODES)
+        cols = columns(ycol_ref, 0)
+        for c in range(3):
+            for plane in range(NODES):
+                along_ref[c, plane] = column_sum(
+                    cols, lambda j: u_ref[c, plane, base + j : base + j + 1, lanes]
+                )
         even, odd = [], []
         for comp in range(3):
             vals = [u_ref[comp, i, sub, lanes] for i in range(NODES)]
@@ -222,12 +237,7 @@
             side_x = []
             for plane, sign in ((pair, 1), (ORDER - pair, -1)):
                 gx = [first[c] + second[c] if sign > 0 else first[c] - second[c] for c in range(3)]
-                gy = [
-                    column_sum(
-                        ycol_ref, 0, lambda j: u_ref[c, plane, base + j : base + j + 1, lanes]
-                    )
-                    for c in range(3)
-                ]
+                gy = [along_ref[c, plane] for c in range(3)]
                 gz = [grad_ref[c, plane, sub, lanes] for c in range(3)]
                 shear = scale * float(LAME_SHEAR * WEIGHTS[plane])
                 twice = scale * float(2.0 * LAME_SHEAR * WEIGHTS[plane])
@@ -251,12 +261,13 @@
                     add_y = float(ODD[pair][i]) * se
                     xsum[c][i] = add_x if pair == 0 else xsum[c][i] + add_x
                     xdif[c][i] = add_y if pair == 0 else xdif[c][i] + add_y
+        cols = columns(ycol_ref, 1)
         for c in range(3):
             for plane in range(NODES):
                 i = min(plane, ORDER - plane)
                 total = xsum[c][i] + xdif[c][i] if plane < HALF else xsum[c][i] - xdif[c][i]
                 k_ref[c, plane, sub, lanes] = total + column_sum(
-                    ycol_ref, 1, lambda b: side_ref[c, plane, b : b + 1, :]
+                    cols, lambda b: side_ref[c, plane, b : b + 1, :]
                 )
 
     @pl.loop(0, n_tile)
@@ -309,7 +320,7 @@
         for end, plane in enumerate(ENDS):
             part = None
             for comp in range(comps):
-                strip = pick(x_upper, xnear_ref[comp, rows, :], xfar_ref[comp, rows, :])[end]
+                strip = x_side(x_upper, xnear_ref, xfar_ref, comp, elem, n_elem, end)
                 strip = release(sum_z(strip), free_ref[plane, rows, :])
                 add_ref[comp, end, own, :] = strip
                 strip = strip + u_ref[comp, plane, own, :]
@@ -329,10 +340,11 @@
             base = place * NODES
             sub = slice(base, base + NODES)
             scale = elem_ref[elem * NODES : (elem + 1) * NODES, lanes]
+            cols = columns(ycol_ref, 0)
             for end, plane in enumerate(ENDS):
                 gy = [
                     column_sum(
-                        ycol_ref, 0, lambda j: add_ref[c, end, base + j : base + j + 1, lanes]
+                        cols, lambda j: add_ref[c, end, base + j : base + j + 1, lanes]
                     )
                     for c in range(3)
                 ]
@@ -351,9 +363,11 @@
                     side_ref[c, end, :, :] = value
                 for c, value in enumerate((axx, axy, axz)):
                     keep_ref[c, end, sub, lanes] = value
+            cols = columns(ycol_ref, 1)
+            for end in range(2):
                 for c in range(5):
                     keep_ref[3 + c, end, sub, lanes] = column_sum(
-                        ycol_ref, 1, lambda b: side_ref[c, end, b : b + 1, :]
+                        cols, lambda b: side_ref[c, end, b : b + 1, :]
                     )
 
     for tile in range(n_tile):
@@ -430,6 +444,16 @@
             )
 
 
+def scale_kernel(flags_ref, widen_ref, weight_ref, scale_ref):
+    solid = (flags_ref[...] == 1).astype(jnp.bfloat16)
+    solid = jnp.dot(solid, widen_ref[...], preferred_element_type=jnp.float32)
+    modulus = jnp.where(solid > 0.5, SOLID_MODULUS, VOID_MODULUS).astype(jnp.float32)
+    for elem in range(flags_ref.shape[0]):
+        scale_ref[elem * NODES : (elem + 1) * NODES, :] = (
+            modulus[elem : elem + 1, :] * weight_ref[...]
+        )
+
+
 def rows_kernel(v_ref, near_ref, far_ref):
     size_y = v_ref.shape[2]
     put_rows(
@@ -440,27 +464,44 @@
     )
 
 
-def faces_kernel(vmid_ref, vedge_ref, ynear_ref, yfar_ref, near_ref, far_ref):
-    comps, size_y, _ = near_ref.shape
-    n_elem = size_y // NODES
+def side_rows(comp, elem, n_elem):
+    start = comp * (n_elem * ORDER + 1) + elem * ORDER
+    return slice(start, start + NODES)
+
+
+def faces_kernel(*refs, n_elem):
+    vmid_ref, vedge_ref, ynear_ref, yfar_ref = refs[:4]
+    near_ref, far_ref = refs[-2:]
+    comps = vmid_ref.shape[0]
     x_upper, y_upper = is_upper("gx"), is_upper("gy")
     v_refs = vmid_ref, vedge_ref
     for comp in range(comps):
         sides = [y_sides(y_upper, ynear_ref, yfar_ref, comp, plane) for plane in ENDS]
         for elem in range(n_elem):
-            rows = slice(elem * NODES, (elem + 1) * NODES)
+            rows = side_rows(comp, elem, n_elem)
             lo, hi = [
                 row_sum_y(v_refs, *side, comp, plane, elem, n_elem)
                 for plane, side in zip(ENDS, sides)
             ]
-            near_ref[comp, rows, :], far_ref[comp, rows, :] = pick(x_upper, lo, hi)
+            near_ref[rows, :], far_ref[rows, :] = pick(x_upper, lo, hi)
+
+
+def assemble_kernel(kmid_ref, kedge_ref, free_ref, w_ref, done_ref, *, elems, n_elem):
+    for place, elem in enumerate(elems):
+        own = slice(place * NODES, (place + 1) * NODES)
+        sub = slice(elem * NODES, (elem + 1) * NODES)
+        for plane in range(w_ref.shape[1]):
+            for comp in range(w_ref.shape[0]):
+                rows = row_sum_y((kmid_ref, kedge_ref), None, None, comp, plane, elem, n_elem)
+                w_ref[comp, plane, own, :] = release(sum_z(rows), free_ref[plane, sub, :])
+    done_ref[...] = w_ref[0, 0, 0:NODES, :LANES]
 
 
 def finish_kernel(*refs):
-    k_refs = refs[:2]
-    ynear_ref, yfar_ref, xnear_ref, xfar_ref, free_ref = refs[2:7]
-    r_refs, r_faces, q_refs, q_faces = refs[7:9], refs[9:11], refs[11:13], refs[13:15]
-    sums_ref, adj_out, res_out, adj_ref, res_ref, sem_ref = refs[15:]
+    *k_refs, w_ref = refs[:3]
+    ynear_ref, yfar_ref, xnear_ref, xfar_ref, free_ref = refs[3:8]
+    r_refs, r_faces, q_refs, q_faces = refs[8:10], refs[10:12], refs[12:14], refs[14:16]
+    sums_ref, adj_out, res_out, adj_ref, res_ref, sem_ref = refs[16:]
     planes, comps, size_y, _ = adj_ref.shape
     n_elem = size_y // NODES
     x_upper, y_upper = is_upper("gx"), is_upper("gy")
@@ -478,23 +519,28 @@
     cross = first * second
     copies = []
     for plane in range(planes):
-        for elem in range(n_elem):
-            sub = slice(elem * NODES, (elem + 1) * NODES)
-            end = ENDS.index(plane) if plane in ENDS else None
-            place = plane if end is None else end
-            r_ref, row = locate(r_refs if end is None else r_faces, elem, n_elem)
-            q_ref, row = locate(q_refs if end is None else q_faces, elem, n_elem)
-            own = slice(row, row + NODES)
-            for comp in range(comps):
-                lo = hi = None
+        end = ENDS.index(plane) if plane in ENDS else None
+        place = plane if end is None else end
+        for comp in range(comps):
+            for elem in range(n_elem):
+                sub = slice(elem * NODES, (elem + 1) * NODES)
+                r_ref, row = locate(r_refs if end is None else r_faces, elem, n_elem)
+                q_ref, row = locate(q_refs if end is None else q_faces, elem, n_elem)
+                own = slice(row, row + NODES)
+                strip = None
+                if end is not None:
+                    strip = x_side(x_upper, xnear_ref, xfar_ref, comp, elem, n_elem, end)
                 if elem in (0, n_elem - 1):
                     lo, hi = y_sides(y_upper, ynear_ref, yfar_ref, comp, plane)
-                strip = row_sum_y(k_refs, lo, hi, comp, plane, elem, n_elem)
-                if end is not None:
-                    strip = strip + pick(x_upper, xnear_ref[comp, sub, :], xfar_ref[comp, sub, :])[end]
+                    rows = row_sum_y(k_refs, lo, hi, comp, plane, elem, n_elem)
+                    strip = rows if strip is None else strip + rows
+                if strip is not None:
+                    strip = release(sum_z(strip), free_ref[plane, sub, :])
+                if elem not in (0, n_elem - 1):
+                    rows = w_ref[comp, plane, own, :]
+                    strip = rows if strip is None else strip + rows
                 loads = r_ref[comp, place, own, :]
                 image = q_ref[comp, place, own, :]
-                strip = release(sum_z(strip), free_ref[plane, sub, :])
                 adj_ref[plane, comp, sub, :] = lead * loads - cross * image
                 res_ref[plane, comp, sub, :] = loads - lead * image + cross * strip
         for which, (ref, out) in enumerate(((adj_ref, adj_out), (res_ref, res_out))):
@@ -520,14 +566,22 @@
     devices = lax.axis_size("gx") * lax.axis_size("gy")
     f32 = jnp.float32
     y_side = jax.ShapeDtypeStruct((comps, size_x, size_z), f32)
-    x_side = jax.ShapeDtypeStruct((comps, size_y, size_z), f32)
+    side_len = comps * (size_y // NODES * ORDER + 1)
+    side = jax.ShapeDtypeStruct((side_len + -side_len % NODES, size_z), f32)
     whole = pl.BlockSpec(memory_space=pltpu.VMEM)
 
-    modulus = jnp.where(flags[0] == 1, SOLID_MODULUS, VOID_MODULUS).astype(f32)
-    modulus = jnp.repeat(jnp.repeat(modulus, NODES, axis=0), NODES, axis=1)
-    weight_y = jnp.asarray(np.tile(WEIGHTS, size_y // NODES), f32)
-    weight_z = jnp.asarray(np.tile(WEIGHTS, size_z // NODES), f32)
-    elem_scale = modulus * weight_y[:, None] * weight_z[None, :]
+    n_elem, n_deep = flags.shape[1:]
+    widen = jnp.asarray(np.kron(np.eye(n_deep), np.ones((1, NODES))), jnp.bfloat16)
+    weight_yz = jnp.asarray(WEIGHTS[:, None] * np.tile(WEIGHTS, n_deep)[None, :], f32)
+    elem_scale = pl.pallas_call(
+        scale_kernel,
+        in_specs=[whole] * 3,
+        out_specs=whole,
+        out_shape=jax.ShapeDtypeStruct((size_y, size_z), f32),
+        compiler_params=pltpu.CompilerParams(vmem_limit_bytes=VMEM_LIMIT),
+        cost_estimate=pl.CostEstimate(flops=1000, bytes_accessed=100000, transcendentals=0),
+        name="scale",
+    )(flags[0], widen, weight_yz)
     free = 1.0 - fixed.astype(f32)[:, :, None] * (jnp.arange(LANES) == 0).astype(f32)
     half_xy = (
         shared_halves(size_x, lax.axis_index("gx") * size_x, size_x * lax.axis_size("gx"), NODES)[
@@ -547,7 +601,6 @@
         f32,
     )
 
-    n_elem = size_y // NODES
     mid, edge = parts(n_elem)
     tables = (free, elem_scale, half_xy, half_z, z_mat, y_col)
 
@@ -580,6 +633,7 @@
             (
                 pltpu.VMEM(some, f32),
                 pltpu.VMEM(some, f32),
+                pltpu.VMEM((comps, size_x, NODES, LANES), f32),
                 pltpu.VMEM((comps, size_x, NODES, LANES), f32),
             ),
             us=5.0,
@@ -611,14 +665,23 @@
             us=2.0,
         )
 
-    def halos(v, y_rows):
-        y_halo = swap(*y_rows, "gy")
-        sides = call(faces_kernel, "faces", (*v, *y_halo), (x_side, x_side), us=0.3)
-        return y_halo, swap(*sides, "gx")
+    def y_halos(y_rows):
+        return swap(*y_rows, "gy")
+
+    def x_halos(v, y_halo, after):
+        sides = call(
+            functools.partial(faces_kernel, n_elem=n_elem),
+            "faces",
+            (*v, *y_halo, *after),
+            (side, side),
+            us=0.3,
+        )
+        return swap(*sides, "gx")
 
     def step(v, y_rows, carry, slot):
-        y_halo, x_halo = halos(v, y_rows)
+        y_halo = y_halos(y_rows)
         u_mid, k_mid, sq_mid = main(v, (), mid, "middle")
+        x_halo = x_halos(v, y_halo, ())
         u_edge, k_edge, sq_edge = main(v, y_halo, edge, "edges")
         k_edge, f_edge, carry, *y_rows = update(
             u_edge, k_edge, x_halo, (sq_mid, sq_edge), carry, edge, slot, "update_edges"
@@ -632,13 +695,21 @@
     carry = jnp.zeros((4, NODES, LANES), f32)
     k_loads, loads, y_rows, carry = step((rhs_loads, rhs_loads), y_rows, carry, 0)
     k_image, image, y_rows, sums = step(k_loads, y_rows, carry, 1)
-    y_halo, x_halo = halos(k_image, y_rows)
+    y_halo = y_halos(y_rows)
+    w_mid, done = call(
+        functools.partial(assemble_kernel, elems=mid, n_elem=n_elem),
+        "assemble",
+        (*k_image, free),
+        (shape(comps, size_x, len(mid) * NODES, size_z), shape(NODES, LANES)),
+        us=1.0,
+    )
+    x_halo = x_halos(k_image, y_halo, (done,))
     sums = lax.all_to_all(sums, axes, 0, 0, tiled=True)
     return tuple(
         call(
             finish_kernel,
             "finish",
-            (*k_image, *y_halo, *x_halo, free, *loads, *image, sums),
+            (*k_image, w_mid, *y_halo, *x_halo, free, *loads, *image, sums),
             (shape(*rhs_loads.shape),) * 2,
             (
                 pltpu.VMEM((size_x, comps, size_y, size_z), f32),

time: 78.6 us -> 77.7 us (0.989)
  blocking collectives: 21.9 us -> 20.9 us
    all_to_all x1, blocking collectives: 21.9 us -> 20.9 us  [local(): sums = lax.all_to_all(sums, axes, 0, 0, tiled=True)]
    pallas_call x13 -> x14, Pallas kernels: 25.5 us -> 25.9 us  [call(): pl.pallas_call(kernel, in_specs=[whole] * len(args), out_specs=[out_spec]...]
  transfers between devices with their start and end apart: 12 -> 12, of which waited for: 2 -> 2; matrix products, arithmetic and copies ran while one was open for 1% -> 0% of each run, Pallas kernels for 24% -> 25%
where the time goes in v3:
time: 77.7 us; the launch traced here: 77.4 us
  Pallas kernels  26.1 us (34%)
  starting transfers between devices  24.9 us (32%)
  blocking collectives  20.9 us (27%)
  waiting for transfers between devices  2.34 us (3%)
  local copies, waits for them, and re-layouts  1.79 us (2%)
  between operations  1.17 us (2%)
    pallas_call x14, Pallas kernels, call(): pl.pallas_call(kernel, in_specs=[whole] * len(args), out_specs=[out_spec]...  25.9 us
    all_to_all x1, blocking collectives, local(): sums = lax.all_to_all(sums, axes, 0, 0, tiled=True)  20.9 us
    ppermute x6, starting transfers between devices, swap(): far = lax.ppermute(far_out, axis, outer)  13.6 us
    ppermute x6, starting transfers between devices, swap(): near = lax.ppermute(near_out, axis, inner)  11.4 us
    ppermute x6, waiting for transfers between devices, swap(): far = lax.ppermute(far_out, axis, outer)  2.32 us
    unnamed x16, local copies, waits for them, and re-layouts  1.7 us
  transfers between devices with their start and end apart: 12, of which 2 were waited for; matrix products, arithmetic and copies ran while one was open for 0% of the time, Pallas kernels for 25%

profile of v3, /device:TPU:1, one launch (start us, length us, event | category | flops | bytes accessed | tf_op | source)
XLA Modules:
  0.0 77.4 jit_solution(5771241478946791395)
XLA Ops:
  0.6 1.7 %copy-done = f32[3,8,32,768]{3,2,1,0:T(8,128)S(1)} copy-done((f32[3,8,32,768]{3,2,1,0:T(8,128)S(1)}, f32[3,8,32,768]{3,2,1,0:T(8,128)}, u32[]{:S(2)}) %copy-start) | copy-done | bytes 2359320
  2.4 1.5 %collective-permute-start = (f32[3,8,768]{2,1,0:T(8,128)S(1)}, f32[3,8,768]{2,1,0:T(8,128)S(1)}, u32[]{:S(2)}, u32[]{:S(2)}) collective-permute-start(f32[3,8,768]{2,1,0:T(8,128)S(1)} %get-tuple-element.42), channel_id=1, source_target_pairs={{0,1},{1,0},{2,3},{3,2},{4,5},{5,4},{6,7},{7,6},{8,9},{9,8},{10,11... | collective-permute-start | bytes 221192 | tf_op jit(solution)/shard_map/ppermute | solution.py:559
  3.9 3.7 %collective-permute-start.1 = (f32[3,8,768]{2,1,0:T(8,128)S(1)}, f32[3,8,768]{2,1,0:T(8,128)S(1)}, u32[]{:S(2)}, u32[]{:S(2)}) collective-permute-start(f32[3,8,768]{2,1,0:T(8,128)S(1)} %get-tuple-element.43), channel_id=1, source_target_pairs={{1,2},{2,1},{3,4},{4,3},{5,6},{6,5},{9,10},{10,9},{11,12},{12,11},... | collective-permute-start | bytes 221192 | tf_op jit(solution)/shard_map/ppermute | solution.py:558
  7.7 2.1 %collective-permute-done.1.refs_3_ = f32[3,8,768]{2,1,0:T(8,128)S(1)} collective-permute-done((f32[3,8,768]{2,1,0:T(8,128)S(1)}, f32[3,8,768]{2,1,0:T(8,128)S(1)}, u32[]{:S(2)}, u32[]{:S(2)}) %collective-permute-start.1) | collective-permute-done | bytes 73760 | tf_op jit(solution)/shard_map/ppermute | solution.py:558
  9.8 0.2 faces.3
  10.0 1.4 %collective-permute-start.2 = (f32[88,768]{1,0:T(8,128)S(1)}, f32[88,768]{1,0:T(8,128)S(1)}, u32[]{:S(2)}, u32[]{:S(2)}) collective-permute-start(f32[88,768]{1,0:T(8,128)S(1)} %get-tuple-element.44), channel_id=1, source_target_pairs={{0,8},{8,0},{16,24},{24,16},{32,40},{40,32},{48,56},{56,48},{64,72... | collective-permute-start | bytes 811016 | tf_op jit(solution)/shard_map/ppermute | solution.py:559
  11.5 0.7 collective-permute-start.3
  12.2 0.1 scale.1.refs_3_.refs_5_
  12.3 0.1 multiply_subtract_fusion.refs_2_.refs_4_.free_ref.refs_7_
  12.5 0.1 mul.50.refs_4_.refs_6_
  12.6 3.6 %middle.2 = (f32[3,8,16,768]{3,2,1,0:T(8,128)S(1)}, f32[3,8,16,768]{3,2,1,0:T(8,128)S(1)}, f32[8,128]{1,0:T(8,128)S(1)}) custom-call(f32[3,8,32,768]{3,2,1,0:T(8,128)S(1)} %copy-done.1, f32[3,8,32,768]{3,2,1,0:T(8,128)S(1)} %copy-done.1, f32[8,32,128]{2,1,0:T(8,128)S(1)} %multiply_subtract_fusion.refs_2_.refs_4_.free_ref.refs_7_, ...), custom_call_target="tpu_custom_call" | custom-call | flops 20000000 | bytes 12500000 | tf_op jit(solution)/shard_map/middle/pallas_call | solution.py:613
  16.2 3.6 %edges.2 = (f32[3,8,16,768]{3,2,1,0:T(8,128)S(1)}, f32[3,8,16,768]{3,2,1,0:T(8,128)S(1)}, f32[8,128]{1,0:T(8,128)S(1)}) custom-call(f32[3,8,32,768]{3,2,1,0:T(8,128)S(1)} %copy-done.1, f32[3,8,32,768]{3,2,1,0:T(8,128)S(1)} %copy-done.1, f32[3,8,768]{2,1,0:T(8,128)S(1)} %collective-permute-done.refs_2_, f32[3,8,768]{2,1,0:T(8,128)S(1)} %collective-permute-done.1.refs_3_, ...), custom_call_target="tpu_custom_call" | custom-call | flops 20000000 | bytes 12500000 | tf_op jit(solution)/shard_map/edges/pallas_call | solution.py:613
  19.8 1.9 %update_edges.2 = (f32[3,8,16,768]{3,2,1,0:T(8,128)S(1)}, f32[3,2,16,768]{3,2,1,0:T(8,128)S(1)}, f32[4,8,128]{2,1,0:T(8,128)S(1)}, f32[3,8,768]{2,1,0:T(8,128)S(1)}, f32[3,8,768]{2,1,0:T(8,128)S(1)}) custom-call(f32[3,8,16,768]{3,2,1,0:T(8,128)S(1)} %get-tuple-element.46.refs_0_.refs_9_, f32[3,8,16,768]{3,2,1,0:T(8,128)S(1)} %get-tuple-element.47.refs_1_, ...), custom_call_target="tpu_custom_call" | custom-call | flops 8000000 | bytes 5000000 | tf_op jit(solution)/shard_map/update_edges/pallas_call | solution.py:613
  21.7 0.1 collective-permute-start.4
  21.8 3.6 %collective-permute-start.5 = (f32[3,8,768]{2,1,0:T(8,128)S(1)}, f32[3,8,768]{2,1,0:T(8,128)S(1)}, u32[]{:S(2)}, u32[]{:S(2)}) collective-permute-start(f32[3,8,768]{2,1,0:T(8,128)S(1)} %get-tuple-element.56), channel_id=1, source_target_pairs={{1,2},{2,1},{3,4},{4,3},{5,6},{6,5},{9,10},{10,9},{11,12},{12,11},... | collective-permute-start | bytes 221192 | tf_op jit(solution)/shard_map/ppermute | solution.py:558
  25.5 1.8 %update_middle.2 = (f32[3,8,16,768]{3,2,1,0:T(8,128)S(1)}, f32[3,2,16,768]{3,2,1,0:T(8,128)S(1)}, f32[4,8,128]{2,1,0:T(8,128)S(1)}) custom-call(f32[3,8,16,768]{3,2,1,0:T(8,128)S(1)} %get-tuple-element.40.refs_0_.refs_8_, f32[3,8,16,768]{3,2,1,0:T(8,128)S(1)} %get-tuple-element.41.refs_1_, f32[88,768]{1,0:T(8,128)S(1)} %collective-permute-done.2.refs_2_, ...), custom_call_target="tpu_custom_call" | custom-call | flops 8000000 | bytes 5000000 | tf_op jit(solution)/shard_map/update_middle/pallas_call | solution.py:613
  27.3 0.2 collective-permute-done.5.refs_3_
  27.5 0.2 faces.4
  27.7 3.8 %collective-permute-start.6 = (f32[88,768]{1,0:T(8,128)S(1)}, f32[88,768]{1,0:T(8,128)S(1)}, u32[]{:S(2)}, u32[]{:S(2)}) collective-permute-start(f32[88,768]{1,0:T(8,128)S(1)} %get-tuple-element.57), channel_id=1, source_target_pairs={{0,8},{8,0},{16,24},{24,16},{32,40},{40,32},{48,56},{56,48},{64,72... | collective-permute-start | bytes 811016 | tf_op jit(solution)/shard_map/ppermute | solution.py:559
  31.5 0.7 collective-permute-start.7
  32.2 3.6 %middle.3 = (f32[3,8,16,768]{3,2,1,0:T(8,128)S(1)}, f32[3,8,16,768]{3,2,1,0:T(8,128)S(1)}, f32[8,128]{1,0:T(8,128)S(1)}) custom-call(f32[3,8,16,768]{3,2,1,0:T(8,128)S(1)} %get-tuple-element.51.refs_0_, f32[3,8,16,768]{3,2,1,0:T(8,128)S(1)} %get-tuple-element.52.refs_1_, f32[8,32,128]{2,1,0:T(8,128)S(1)} %multiply_subtract_fusion.refs_2_.refs_4_.free_ref.refs_7_, ...), custom_call_target="tpu_custom_call" | custom-call | flops 20000000 | bytes 12500000 | tf_op jit(solution)/shard_map/middle/pallas_call | solution.py:613
  35.8 3.6 %edges.3 = (f32[3,8,16,768]{3,2,1,0:T(8,128)S(1)}, f32[3,8,16,768]{3,2,1,0:T(8,128)S(1)}, f32[8,128]{1,0:T(8,128)S(1)}) custom-call(f32[3,8,16,768]{3,2,1,0:T(8,128)S(1)} %get-tuple-element.51.refs_0_, f32[3,8,16,768]{3,2,1,0:T(8,128)S(1)} %get-tuple-element.52.refs_1_, f32[3,8,768]{2,1,0:T(8,128)S(1)} %collective-permute-done.4.refs_2_, ...), custom_call_target="tpu_custom_call" | custom-call | flops 20000000 | bytes 12500000 | tf_op jit(solution)/shard_map/edges/pallas_call | solution.py:613
  39.5 1.9 %update_edges.3 = (f32[3,8,16,768]{3,2,1,0:T(8,128)S(1)}, f32[3,2,16,768]{3,2,1,0:T(8,128)S(1)}, f32[4,8,128]{2,1,0:T(8,128)S(1)}, f32[3,8,768]{2,1,0:T(8,128)S(1)}, f32[3,8,768]{2,1,0:T(8,128)S(1)}) custom-call(f32[3,8,16,768]{3,2,1,0:T(8,128)S(1)} %get-tuple-element.59.refs_0_.refs_13_, f32[3,8,16,768]{3,2,1,0:T(8,128)S(1)} %get-tuple-element.60.refs_1_, ...), custom_call_target="tpu_custom_call" | custom-call | flops 8000000 | bytes 5000000 | tf_op jit(solution)/shard_map/update_edges/pallas_call | solution.py:613
  41.4 0.1 collective-permute-start.8
  41.5 4.3 %collective-permute-start.9 = (f32[3,8,768]{2,1,0:T(8,128)S(1)}, f32[3,8,768]{2,1,0:T(8,128)S(1)}, u32[]{:S(2)}, u32[]{:S(2)}) collective-permute-start(f32[3,8,768]{2,1,0:T(8,128)S(1)} %get-tuple-element.69), channel_id=1, source_target_pairs={{1,2},{2,1},{3,4},{4,3},{5,6},{6,5},{9,10},{10,9},{11,12},{12,11},... | collective-permute-start | bytes 221192 | tf_op jit(solution)/shard_map/ppermute | solution.py:558
  45.7 2.0 %update_middle.3 = (f32[3,8,16,768]{3,2,1,0:T(8,128)S(1)}, f32[3,2,16,768]{3,2,1,0:T(8,128)S(1)}, f32[128,128]{1,0:T(8,128)S(1)}) custom-call(f32[3,8,16,768]{3,2,1,0:T(8,128)S(1)} %get-tuple-element.53.refs_0_.refs_12_, f32[3,8,16,768]{3,2,1,0:T(8,128)S(1)} %get-tuple-element.54.refs_1_, f32[88,768]{1,0:T(8,128)S(1)} %collective-permute-done.6.refs_2_, ...), custom_call_target="tpu_custom_call" | custom-call | flops 8000000 | bytes 5000000 | tf_op jit(solution)/shard_map/update_middle/pallas_call | solution.py:613
  47.7 0.7 assemble.1
  48.4 0.2 faces.5
  48.6 4.4 %collective-permute-start.10 = (f32[88,768]{1,0:T(8,128)S(1)}, f32[88,768]{1,0:T(8,128)S(1)}, u32[]{:S(2)}, u32[]{:S(2)}) collective-permute-start(f32[88,768]{1,0:T(8,128)S(1)} %get-tuple-element.71), channel_id=1, source_target_pairs={{0,8},{8,0},{16,24},{24,16},{32,40},{40,32},{48,56},{56,48},{64,72... | collective-permute-start | bytes 811016 | tf_op jit(solution)/shard_map/ppermute | solution.py:559
  53.0 0.7 collective-permute-start.11
  53.7 20.9 %all_to_all.11 = f32[128,1,128]{2,1,0:T(1,128)S(1)} all-to-all(f32[128,1,128]{2,1,0:T(1,128)S(1)} %bitcast.6), channel_id=1, replica_groups=mesh['gx'=16,'gy'=8] {'gx','gy'}, dimensions={0} | all-to-all | bytes 131072 | tf_op jit(solution)/shard_map/all_to_all | solution.py:707
  74.6 2.6 %finish.1 = (f32[3,8,32,768]{3,2,1,0:T(8,128)}, f32[3,8,32,768]{3,2,1,0:T(8,128)}) custom-call(f32[3,8,16,768]{3,2,1,0:T(8,128)S(1)} %get-tuple-element.65.kmid_ref.refs_0_, f32[3,8,16,768]{3,2,1,0:T(8,128)S(1)} %get-tuple-element.66.kedge_ref.refs_1_, f32[3,8,16,768]{3,2,1,0:T(8,128)S(1)} %get-tuple-element.67.refs_2_, ...), custom_call_target="tpu_custom_call" | custom-call | flops 16000000 | bytes 10000000 | tf_op jit(solution)/shard_map/finish/pallas_call | solution.py:613
  (34 shorter events, 0.2 us)
Async XLA Ops:
  0.6 1.7 %copy-start = (f32[3,8,32,768]{3,2,1,0:T(8,128)S(1)}, f32[3,8,32,768]{3,2,1,0:T(8,128)}, u32[]{:S(2)}) copy-start(f32[3,8,32,768]{3,2,1,0:T(8,128)} %refs_1_.5) | copy-start | bytes 7077892
  2.3 7.5 %copy-start.1 = (f32[3,8,32,768]{3,2,1,0:T(8,128)S(1)}, f32[3,8,32,768]{3,2,1,0:T(8,128)}, u32[]{:S(2)}) copy-start(f32[3,8,32,768]{3,2,1,0:T(8,128)} %refs_1_.5) | copy-start | bytes 7077892
  2.4 5.3 %collective-permute-start = (f32[3,8,768]{2,1,0:T(8,128)S(1)}, f32[3,8,768]{2,1,0:T(8,128)S(1)}, u32[]{:S(2)}, u32[]{:S(2)}) collective-permute-start(f32[3,8,768]{2,1,0:T(8,128)S(1)} %get-tuple-element.42), channel_id=1, source_target_pairs={{0,1},{1,0},{2,3},{3,2},{4,5},{5,4},{6,7},{7,6},{8,9},{9,8},{10,11... | collective-permute-start | bytes 221192 | tf_op jit(solution)/shard_map/ppermute | solution.py:559
  3.9 6.0 %collective-permute-start.1 = (f32[3,8,768]{2,1,0:T(8,128)S(1)}, f32[3,8,768]{2,1,0:T(8,128)S(1)}, u32[]{:S(2)}, u32[]{:S(2)}) collective-permute-start(f32[3,8,768]{2,1,0:T(8,128)S(1)} %get-tuple-element.43), channel_id=1, source_target_pairs={{1,2},{2,1},{3,4},{4,3},{5,6},{6,5},{9,10},{10,9},{11,12},{12,11},... | collective-permute-start | bytes 221192 | tf_op jit(solution)/shard_map/ppermute | solution.py:558
  7.6 4.5 %copy-start.4 = (bf16[96,768]{1,0:T(8,128)(2,1)S(1)}, bf16[96,768]{1,0:T(8,128)(2,1)}, u32[]{:S(2)}) copy-start(bf16[96,768]{1,0:T(8,128)(2,1)} %constant.73.clone.widen_ref) | copy-start | bytes 442372
  7.6 4.5 %copy-start.5 = (f32[8,768]{1,0:T(8,128)S(1)}, f32[8,768]{1,0:T(8,128)}, u32[]{:S(2)}) copy-start(f32[8,768]{1,0:T(8,128)} %constant.74.clone.weight_ref) | copy-start | bytes 73732
  7.6 4.5 %copy-start.6 = (s32[1,4,96]{2,1,0:T(4,128)S(1)}, s32[1,4,96]{2,1,0:T(4,128)}, u32[]{:S(2)}) copy-start(s32[1,4,96]{2,1,0:T(4,128)} %param.8) | copy-start | bytes 4612
  7.7 4.7 %copy-start.7 = (s32[8,32]{1,0:T(8,128)S(1)}, s32[8,32]{1,0:T(8,128)}, u32[]{:S(2)}) copy-start(s32[8,32]{1,0:T(8,128)} %param.9) | copy-start | bytes 3076
  7.7 4.9 %copy-start.2 = (bf16[2,256,256]{2,1,0:T(8,128)(2,1)S(1)}, bf16[2,256,256]{2,1,0:T(8,128)(2,1)}, u32[]{:S(2)}) copy-start(bf16[2,256,256]{2,1,0:T(8,128)(2,1)} %constant.75.clone.refs_6_.refs_8_) | copy-start | bytes 786436
  7.7 4.9 %copy-start.3 = (f32[2,8,8,128]{3,2,1,0:T(8,128)S(1)}, f32[2,8,8,128]{3,2,1,0:T(8,128)}, u32[]{:S(2)}) copy-start(f32[2,8,8,128]{3,2,1,0:T(8,128)} %constant.76.clone.refs_7_.refs_9_) | copy-start | bytes 196612
  10.0 9.8 %collective-permute-start.2 = (f32[88,768]{1,0:T(8,128)S(1)}, f32[88,768]{1,0:T(8,128)S(1)}, u32[]{:S(2)}, u32[]{:S(2)}) collective-permute-start(f32[88,768]{1,0:T(8,128)S(1)} %get-tuple-element.44), channel_id=1, source_target_pairs={{0,8},{8,0},{16,24},{24,16},{32,40},{40,32},{48,56},{56,48},{64,72... | collective-permute-start | bytes 811016 | tf_op jit(solution)/shard_map/ppermute | solution.py:559
  11.5 8.4 %collective-permute-start.3 = (f32[88,768]{1,0:T(8,128)S(1)}, f32[88,768]{1,0:T(8,128)S(1)}, u32[]{:S(2)}, u32[]{:S(2)}) collective-permute-start(f32[88,768]{1,0:T(8,128)S(1)} %get-tuple-element.45), channel_id=1, source_target_pairs={{8,16},{16,8},{24,32},{32,24},{40,48},{48,40},{56,64},{64,56},{72,... | collective-permute-start | bytes 811016 | tf_op jit(solution)/shard_map/ppermute | solution.py:558
  21.7 5.6 %collective-permute-start.4 = (f32[3,8,768]{2,1,0:T(8,128)S(1)}, f32[3,8,768]{2,1,0:T(8,128)S(1)}, u32[]{:S(2)}, u32[]{:S(2)}) collective-permute-start(f32[3,8,768]{2,1,0:T(8,128)S(1)} %get-tuple-element.55), channel_id=1, source_target_pairs={{0,1},{1,0},{2,3},{3,2},{4,5},{5,4},{6,7},{7,6},{8,9},{9,8},{10,11... | collective-permute-start | bytes 221192 | tf_op jit(solution)/shard_map/ppermute | solution.py:559
  21.8 5.7 %collective-permute-start.5 = (f32[3,8,768]{2,1,0:T(8,128)S(1)}, f32[3,8,768]{2,1,0:T(8,128)S(1)}, u32[]{:S(2)}, u32[]{:S(2)}) collective-permute-start(f32[3,8,768]{2,1,0:T(8,128)S(1)} %get-tuple-element.56), channel_id=1, source_target_pairs={{1,2},{2,1},{3,4},{4,3},{5,6},{6,5},{9,10},{10,9},{11,12},{12,11},... | collective-permute-start | bytes 221192 | tf_op jit(solution)/shard_map/ppermute | solution.py:558
  27.7 11.7 %collective-permute-start.6 = (f32[88,768]{1,0:T(8,128)S(1)}, f32[88,768]{1,0:T(8,128)S(1)}, u32[]{:S(2)}, u32[]{:S(2)}) collective-permute-start(f32[88,768]{1,0:T(8,128)S(1)} %get-tuple-element.57), channel_id=1, source_target_pairs={{0,8},{8,0},{16,24},{24,16},{32,40},{40,32},{48,56},{56,48},{64,72... | collective-permute-start | bytes 811016 | tf_op jit(solution)/shard_map/ppermute | solution.py:559
  31.5 7.9 %collective-permute-start.7 = (f32[88,768]{1,0:T(8,128)S(1)}, f32[88,768]{1,0:T(8,128)S(1)}, u32[]{:S(2)}, u32[]{:S(2)}) collective-permute-start(f32[88,768]{1,0:T(8,128)S(1)} %get-tuple-element.58), channel_id=1, source_target_pairs={{8,16},{16,8},{24,32},{32,24},{40,48},{48,40},{56,64},{64,56},{72,... | collective-permute-start | bytes 811016 | tf_op jit(solution)/shard_map/ppermute | solution.py:558
  41.4 7.0 %collective-permute-start.8 = (f32[3,8,768]{2,1,0:T(8,128)S(1)}, f32[3,8,768]{2,1,0:T(8,128)S(1)}, u32[]{:S(2)}, u32[]{:S(2)}) collective-permute-start(f32[3,8,768]{2,1,0:T(8,128)S(1)} %get-tuple-element.68), channel_id=1, source_target_pairs={{0,1},{1,0},{2,3},{3,2},{4,5},{5,4},{6,7},{7,6},{8,9},{9,8},{10,11... | collective-permute-start | bytes 221192 | tf_op jit(solution)/shard_map/ppermute | solution.py:559
  41.5 6.9 %collective-permute-start.9 = (f32[3,8,768]{2,1,0:T(8,128)S(1)}, f32[3,8,768]{2,1,0:T(8,128)S(1)}, u32[]{:S(2)}, u32[]{:S(2)}) collective-permute-start(f32[3,8,768]{2,1,0:T(8,128)S(1)} %get-tuple-element.69), channel_id=1, source_target_pairs={{1,2},{2,1},{3,4},{4,3},{5,6},{6,5},{9,10},{10,9},{11,12},{12,11},... | collective-permute-start | bytes 221192 | tf_op jit(solution)/shard_map/ppermute | solution.py:558
  48.6 26.0 %collective-permute-start.10 = (f32[88,768]{1,0:T(8,128)S(1)}, f32[88,768]{1,0:T(8,128)S(1)}, u32[]{:S(2)}, u32[]{:S(2)}) collective-permute-start(f32[88,768]{1,0:T(8,128)S(1)} %get-tuple-element.71), channel_id=1, source_target_pairs={{0,8},{8,0},{16,24},{24,16},{32,40},{40,32},{48,56},{56,48},{64,72... | collective-permute-start | bytes 811016 | tf_op jit(solution)/shard_map/ppermute | solution.py:559
  53.0 21.6 %collective-permute-start.11 = (f32[88,768]{1,0:T(8,128)S(1)}, f32[88,768]{1,0:T(8,128)S(1)}, u32[]{:S(2)}, u32[]{:S(2)}) collective-permute-start(f32[88,768]{1,0:T(8,128)S(1)} %get-tuple-element.72), channel_id=1, source_target_pairs={{8,16},{16,8},{24,32},{32,24},{40,48},{48,40},{56,64},{64,56},{72,... | collective-permute-start | bytes 811016 | tf_op jit(solution)/shard_map/ppermute | solution.py:558

commit v4 on v3

--- a/solution.py
+++ b/solution.py
@@ -301,32 +301,31 @@
 def update_kernel(*refs, elems, n_elem, slot, last):
     u_ref, kin_ref, xnear_ref, xfar_ref = refs[:4]
     free_ref, elem_ref, half_ref, halfz_ref, zmat_ref, ycol_ref = refs[4:10]
-    squares_refs, refs = (refs[10:12], refs[12:]) if 0 in elems else ((), refs[10:])
-    carry_ref, k_ref, face_ref, sums_ref = refs[:4]
-    refs = refs[4:]
-    if 0 in elems:
+    outer = 0 in elems
+    squares_refs, refs = refs[10:12], refs[12:]
+    if not outer:
+        uo_ref, ko_ref, fo_ref, carry_ref = refs[:4]
+        refs = refs[4:]
+    k_ref, face_ref = refs[:2]
+    refs = refs[2:]
+    if not outer:
+        sums_ref, *refs = refs
+    if outer:
         near_ref, far_ref = refs[:2]
         refs = refs[2:]
     add_ref, grad_ref, keep_ref, zin_ref, zout_ref, side_ref = refs
     comps, planes, size_y, size_z = k_ref.shape
     n_tile = size_z // LANES
     x_upper = is_upper("gx")
-    square = jnp.zeros((NODES, LANES), jnp.float32)
-    for ref in squares_refs:
-        square = square + ref[...]
     for place, elem in enumerate(elems):
         rows = slice(elem * NODES, (elem + 1) * NODES)
         own = slice(place * NODES, (place + 1) * NODES)
         for end, plane in enumerate(ENDS):
-            part = None
             for comp in range(comps):
                 strip = x_side(x_upper, xnear_ref, xfar_ref, comp, elem, n_elem, end)
                 strip = release(sum_z(strip), free_ref[plane, rows, :])
                 add_ref[comp, end, own, :] = strip
-                strip = strip + u_ref[comp, plane, own, :]
-                face_ref[comp, end, own, :] = strip
-                part = strip * strip if part is None else part + strip * strip
-            square = square + fold(part * halfz_ref[0:1, :]) * half_ref[plane, rows, :]
+                face_ref[comp, end, own, :] = strip + u_ref[comp, plane, own, :]
 
     for tile in range(n_tile):
         lanes = slice(tile * LANES, (tile + 1) * LANES)
@@ -377,6 +376,14 @@
 
     def tile_energy(tile, energy):
         lanes = pl.ds(pl.multiple_of(tile * LANES, LANES), LANES)
+        if not outer:
+            for plane in range(planes):
+                for c in range(comps):
+                    vector = uo_ref[c, plane, :, lanes]
+                    if plane in ENDS:
+                        vector = fo_ref[c, ENDS.index(plane), :, lanes]
+                    product = vector * ko_ref[c, plane, :, lanes]
+                    energy = energy + product[:NODES] + product[NODES:]
         for place, elem in enumerate(elems):
             sub = slice(place * NODES, (place + 1) * NODES)
             scale = elem_ref[elem * NODES : (elem + 1) * NODES, lanes]
@@ -404,21 +411,34 @@
                         if plane in ENDS:
                             end = ENDS.index(plane)
                             value = value + (kept[5 + c][end] + zout[2 + c][end])
-                            vector = face_ref[c, end, sub, lanes]
-                        else:
+                            vector = None if outer else face_ref[c, end, sub, lanes]
+                        elif not outer:
                             vector = u_ref[c, plane, sub, lanes]
                         k_ref[c, plane, sub, lanes] = value
-                        energy = energy + value * vector
+                        if not outer:
+                            energy = energy + value * vector
         return energy
 
     energy = lax.fori_loop(0, n_tile, tile_energy, jnp.zeros((NODES, LANES), jnp.float32))
-    if 0 in elems:
+    if outer:
         put_rows(
             lambda comp, plane: k_ref[comp, plane, 0:1, :],
             lambda comp, plane: k_ref[comp, plane, size_y - 1 : size_y, :],
             near_ref,
             far_ref,
         )
+        return
+    square = squares_refs[0][...] + squares_refs[1][...]
+    for group, ref in ((elems, face_ref), ((0, n_elem - 1), fo_ref)):
+        for place, elem in enumerate(group):
+            own = slice(place * NODES, (place + 1) * NODES)
+            rows = slice(elem * NODES, (elem + 1) * NODES)
+            for end, plane in enumerate(ENDS):
+                part = None
+                for comp in range(comps):
+                    strip = ref[comp, end, own, :]
+                    part = strip * strip if part is None else part + strip * strip
+                square = square + fold(part * halfz_ref[0:1, :]) * half_ref[plane, rows, :]
     moments = [carry_ref[i] for i in range(4)]
     moments[2 * slot] = moments[2 * slot] + square
     moments[2 * slot + 1] = moments[2 * slot + 1] + energy
@@ -639,20 +659,18 @@
             us=5.0,
         )
 
-    def update(u, k, x_halo, squares, carry, elems, slot, name):
+    def update(u, k, x_halo, squares, others, elems, slot, name):
         rows = len(elems) * NODES
         last = slot == 1 and 0 not in elems
-        out = [
-            shape(comps, size_x, rows, size_z),
-            shape(comps, 2, rows, size_z),
-            shape(devices, LANES) if last else shape(4, NODES, LANES),
-        ]
+        out = [shape(comps, size_x, rows, size_z), shape(comps, 2, rows, size_z)]
         if 0 in elems:
             out += [y_side, y_side]
+        else:
+            out += [shape(devices, LANES) if last else shape(4, NODES, LANES)]
         return call(
             functools.partial(update_kernel, elems=elems, n_elem=n_elem, slot=slot, last=last),
             name,
-            (u, k, *x_halo, *tables, *squares, carry),
+            (u, k, *x_halo, *tables, *squares, *others),
             out,
             (
                 pltpu.VMEM((comps, 2, rows, size_z), f32),
@@ -683,11 +701,13 @@
         u_mid, k_mid, sq_mid = main(v, (), mid, "middle")
         x_halo = x_halos(v, y_halo, ())
         u_edge, k_edge, sq_edge = main(v, y_halo, edge, "edges")
-        k_edge, f_edge, carry, *y_rows = update(
-            u_edge, k_edge, x_halo, (sq_mid, sq_edge), carry, edge, slot, "update_edges"
-        )
+        squares = sq_mid, sq_edge
+        k_edge, f_edge, *y_rows = update(
+            u_edge, k_edge, x_halo, squares, (), edge, slot, "update_edges"
+        )
+        outer = u_edge, k_edge, f_edge, carry
         k_mid, f_mid, carry = update(
-            u_mid, k_mid, x_halo, (), carry, mid, slot, "update_middle"
+            u_mid, k_mid, x_halo, squares, outer, mid, slot, "update_middle"
         )
         return (k_mid, k_edge), (u_mid, u_edge, f_mid, f_edge), y_rows, carry
 

time: 77.7 us -> 77.3 us (level)
  transfers between devices with their start and end apart: 12 -> 12, of which waited for: 2 -> 1; matrix products, arithmetic and copies ran while one was open for 0% -> 0% of each run, Pallas kernels for 25% -> 25%
where the time goes in v4:
time: 77.3 us; the launch traced here: 77 us
  Pallas kernels  26.2 us (34%)
  starting transfers between devices  24.9 us (32%)
  blocking collectives  20.7 us (27%)
  waiting for transfers between devices  2.16 us (3%)
  local copies, waits for them, and re-layouts  1.79 us (2%)
  between operations  1.18 us (2%)
    pallas_call x14, Pallas kernels, call(): pl.pallas_call(kernel, in_specs=[whole] * len(args), out_specs=[out_spec]...  26 us
    all_to_all x1, blocking collectives, local(): sums = lax.all_to_all(sums, axes, 0, 0, tiled=True)  20.7 us
    ppermute x6, starting transfers between devices, swap(): far = lax.ppermute(far_out, axis, outer)  13.5 us
    ppermute x6, starting transfers between devices, swap(): near = lax.ppermute(near_out, axis, inner)  11.4 us
    ppermute x6, waiting for transfers between devices, swap(): far = lax.ppermute(far_out, axis, outer)  2.15 us
    unnamed x16, local copies, waits for them, and re-layouts  1.7 us
  transfers between devices with their start and end apart: 12, of which 1 were waited for; matrix products, arithmetic and copies ran while one was open for 0% of the time, Pallas kernels for 25%

profile of v4, /device:TPU:1, one launch (start us, length us, event | category | flops | bytes accessed | tf_op | source)
XLA Modules:
  0.0 77.0 jit_solution(1185632166750403363)
XLA Ops:
  0.6 1.7 %copy-done = f32[3,8,32,768]{3,2,1,0:T(8,128)S(1)} copy-done((f32[3,8,32,768]{3,2,1,0:T(8,128)S(1)}, f32[3,8,32,768]{3,2,1,0:T(8,128)}, u32[]{:S(2)}) %copy-start) | copy-done | bytes 2359320
  2.4 1.5 %collective-permute-start = (f32[3,8,768]{2,1,0:T(8,128)S(1)}, f32[3,8,768]{2,1,0:T(8,128)S(1)}, u32[]{:S(2)}, u32[]{:S(2)}) collective-permute-start(f32[3,8,768]{2,1,0:T(8,128)S(1)} %get-tuple-element.40), channel_id=1, source_target_pairs={{0,1},{1,0},{2,3},{3,2},{4,5},{5,4},{6,7},{7,6},{8,9},{9,8},{10,11... | collective-permute-start | bytes 221192 | tf_op jit(solution)/shard_map/ppermute | solution.py:579
  3.9 3.7 %collective-permute-start.1 = (f32[3,8,768]{2,1,0:T(8,128)S(1)}, f32[3,8,768]{2,1,0:T(8,128)S(1)}, u32[]{:S(2)}, u32[]{:S(2)}) collective-permute-start(f32[3,8,768]{2,1,0:T(8,128)S(1)} %get-tuple-element.41), channel_id=1, source_target_pairs={{1,2},{2,1},{3,4},{4,3},{5,6},{6,5},{9,10},{10,9},{11,12},{12,11},... | collective-permute-start | bytes 221192 | tf_op jit(solution)/shard_map/ppermute | solution.py:578
  7.6 0.1 broadcast_multiply_fusion
  7.7 2.1 %collective-permute-done.1.refs_3_ = f32[3,8,768]{2,1,0:T(8,128)S(1)} collective-permute-done((f32[3,8,768]{2,1,0:T(8,128)S(1)}, f32[3,8,768]{2,1,0:T(8,128)S(1)}, u32[]{:S(2)}, u32[]{:S(2)}) %collective-permute-start.1) | collective-permute-done | bytes 73760 | tf_op jit(solution)/shard_map/ppermute | solution.py:578
  9.8 0.2 faces.3
  10.0 1.4 %collective-permute-start.2 = (f32[88,768]{1,0:T(8,128)S(1)}, f32[88,768]{1,0:T(8,128)S(1)}, u32[]{:S(2)}, u32[]{:S(2)}) collective-permute-start(f32[88,768]{1,0:T(8,128)S(1)} %get-tuple-element.42), channel_id=1, source_target_pairs={{0,8},{8,0},{16,24},{24,16},{32,40},{40,32},{48,56},{56,48},{64,72... | collective-permute-start | bytes 811016 | tf_op jit(solution)/shard_map/ppermute | solution.py:579
  11.5 0.7 collective-permute-start.3
  12.2 0.1 scale.1.refs_3_.refs_5_
  12.3 0.1 multiply_subtract_fusion.refs_2_.refs_4_.free_ref.refs_7_
  12.5 0.1 mul.50.refs_4_.refs_6_
  12.6 3.6 %middle.2 = (f32[3,8,16,768]{3,2,1,0:T(8,128)S(1)}, f32[3,8,16,768]{3,2,1,0:T(8,128)S(1)}, f32[8,128]{1,0:T(8,128)S(1)}) custom-call(f32[3,8,32,768]{3,2,1,0:T(8,128)S(1)} %copy-done.1, f32[3,8,32,768]{3,2,1,0:T(8,128)S(1)} %copy-done.1, f32[8,32,128]{2,1,0:T(8,128)S(1)} %multiply_subtract_fusion.refs_2_.refs_4_.free_ref.refs_7_, ...), custom_call_target="tpu_custom_call" | custom-call | flops 20000000 | bytes 12500000 | tf_op jit(solution)/shard_map/middle/pallas_call | solution.py:633
  16.2 3.6 %edges.2 = (f32[3,8,16,768]{3,2,1,0:T(8,128)S(1)}, f32[3,8,16,768]{3,2,1,0:T(8,128)S(1)}, f32[8,128]{1,0:T(8,128)S(1)}) custom-call(f32[3,8,32,768]{3,2,1,0:T(8,128)S(1)} %copy-done.1, f32[3,8,32,768]{3,2,1,0:T(8,128)S(1)} %copy-done.1, f32[3,8,768]{2,1,0:T(8,128)S(1)} %collective-permute-done.refs_2_, f32[3,8,768]{2,1,0:T(8,128)S(1)} %collective-permute-done.1.refs_3_, ...), custom_call_target="tpu_custom_call" | custom-call | flops 20000000 | bytes 12500000 | tf_op jit(solution)/shard_map/edges/pallas_call | solution.py:633
  19.8 1.7 %update_edges.2 = (f32[3,8,16,768]{3,2,1,0:T(8,128)S(1)}, f32[3,2,16,768]{3,2,1,0:T(8,128)S(1)}, f32[3,8,768]{2,1,0:T(8,128)S(1)}, f32[3,8,768]{2,1,0:T(8,128)S(1)}) custom-call(f32[3,8,16,768]{3,2,1,0:T(8,128)S(1)} %get-tuple-element.46.refs_0_.refs_12_.refs_9_, f32[3,8,16,768]{3,2,1,0:T(8,128)S(1)} %get-tuple-element.47.refs_1_, ...), custom_call_target="tpu_custom_call" | custom-call | flops 8000000 | bytes 5000000 | tf_op jit(solution)/shard_map/update_edges/pallas_call | solution.py:633
  21.6 0.1 collective-permute-start.4
  21.7 3.6 %collective-permute-start.5 = (f32[3,8,768]{2,1,0:T(8,128)S(1)}, f32[3,8,768]{2,1,0:T(8,128)S(1)}, u32[]{:S(2)}, u32[]{:S(2)}) collective-permute-start(f32[3,8,768]{2,1,0:T(8,128)S(1)} %get-tuple-element.54), channel_id=1, source_target_pairs={{1,2},{2,1},{3,4},{4,3},{5,6},{6,5},{9,10},{10,9},{11,12},{12,11},... | collective-permute-start | bytes 221192 | tf_op jit(solution)/shard_map/ppermute | solution.py:578
  25.3 2.0 %update_middle.2 = (f32[3,8,16,768]{3,2,1,0:T(8,128)S(1)}, f32[3,2,16,768]{3,2,1,0:T(8,128)S(1)}, f32[4,8,128]{2,1,0:T(8,128)S(1)}) custom-call(f32[3,8,16,768]{3,2,1,0:T(8,128)S(1)} %get-tuple-element.38.refs_0_.refs_8_, f32[3,8,16,768]{3,2,1,0:T(8,128)S(1)} %get-tuple-element.39.refs_1_, f32[88,768]{1,0:T(8,128)S(1)} %collective-permute-done.2.refs_2_, ...), custom_call_target="tpu_custom_call" | custom-call | flops 8000000 | bytes 5000000 | tf_op jit(solution)/shard_map/update_middle/pallas_call | solution.py:633
  27.4 0.2 faces.4
  27.6 3.8 %collective-permute-start.6 = (f32[88,768]{1,0:T(8,128)S(1)}, f32[88,768]{1,0:T(8,128)S(1)}, u32[]{:S(2)}, u32[]{:S(2)}) collective-permute-start(f32[88,768]{1,0:T(8,128)S(1)} %get-tuple-element.55), channel_id=1, source_target_pairs={{0,8},{8,0},{16,24},{24,16},{32,40},{40,32},{48,56},{56,48},{64,72... | collective-permute-start | bytes 811016 | tf_op jit(solution)/shard_map/ppermute | solution.py:579
  31.4 0.7 collective-permute-start.7
  32.1 3.6 %middle.3 = (f32[3,8,16,768]{3,2,1,0:T(8,128)S(1)}, f32[3,8,16,768]{3,2,1,0:T(8,128)S(1)}, f32[8,128]{1,0:T(8,128)S(1)}) custom-call(f32[3,8,16,768]{3,2,1,0:T(8,128)S(1)} %get-tuple-element.50.refs_0_, f32[3,8,16,768]{3,2,1,0:T(8,128)S(1)} %get-tuple-element.48.refs_13_.refs_1_, f32[8,32,128]{2,1,0:T(8,128)S(1)} %multiply_subtract_fusion.refs_2_.refs_4_.free_ref.refs_7_, ...), custom_call_target="tpu_custom_call" | custom-call | flops 20000000 | bytes 12500000 | tf_op jit(solution)/shard_map/middle/pallas_call | solution.py:633
  35.7 3.6 %edges.3 = (f32[3,8,16,768]{3,2,1,0:T(8,128)S(1)}, f32[3,8,16,768]{3,2,1,0:T(8,128)S(1)}, f32[8,128]{1,0:T(8,128)S(1)}) custom-call(f32[3,8,16,768]{3,2,1,0:T(8,128)S(1)} %get-tuple-element.50.refs_0_, f32[3,8,16,768]{3,2,1,0:T(8,128)S(1)} %get-tuple-element.48.refs_13_.refs_1_, f32[3,8,768]{2,1,0:T(8,128)S(1)} %collective-permute-done.4.refs_2_, ...), custom_call_target="tpu_custom_call" | custom-call | flops 20000000 | bytes 12500000 | tf_op jit(solution)/shard_map/edges/pallas_call | solution.py:633
  39.3 1.7 %update_edges.3 = (f32[3,8,16,768]{3,2,1,0:T(8,128)S(1)}, f32[3,2,16,768]{3,2,1,0:T(8,128)S(1)}, f32[3,8,768]{2,1,0:T(8,128)S(1)}, f32[3,8,768]{2,1,0:T(8,128)S(1)}) custom-call(f32[3,8,16,768]{3,2,1,0:T(8,128)S(1)} %get-tuple-element.59.refs_0_.refs_12_.refs_13_, f32[3,8,16,768]{3,2,1,0:T(8,128)S(1)} %get-tuple-element.60.refs_1_, ...), custom_call_target="tpu_custom_call" | custom-call | flops 8000000 | bytes 5000000 | tf_op jit(solution)/shard_map/update_edges/pallas_call | solution.py:633
  41.1 0.1 collective-permute-start.8
  41.2 4.2 %collective-permute-start.9 = (f32[3,8,768]{2,1,0:T(8,128)S(1)}, f32[3,8,768]{2,1,0:T(8,128)S(1)}, u32[]{:S(2)}, u32[]{:S(2)}) collective-permute-start(f32[3,8,768]{2,1,0:T(8,128)S(1)} %get-tuple-element.67), channel_id=1, source_target_pairs={{1,2},{2,1},{3,4},{4,3},{5,6},{6,5},{9,10},{10,9},{11,12},{12,11},... | collective-permute-start | bytes 221192 | tf_op jit(solution)/shard_map/ppermute | solution.py:578
  45.4 2.2 %update_middle.3 = (f32[3,8,16,768]{3,2,1,0:T(8,128)S(1)}, f32[3,2,16,768]{3,2,1,0:T(8,128)S(1)}, f32[128,128]{1,0:T(8,128)S(1)}) custom-call(f32[3,8,16,768]{3,2,1,0:T(8,128)S(1)} %get-tuple-element.51.refs_0_.refs_12_, f32[3,8,16,768]{3,2,1,0:T(8,128)S(1)} %get-tuple-element.52.refs_1_, f32[88,768]{1,0:T(8,128)S(1)} %collective-permute-done.6.refs_2_, ...), custom_call_target="tpu_custom_call" | custom-call | flops 8000000 | bytes 5000000 | tf_op jit(solution)/shard_map/update_middle/pallas_call | solution.py:633
  47.6 0.7 assemble.1
  48.3 0.2 faces.5
  48.5 4.4 %collective-permute-start.10 = (f32[88,768]{1,0:T(8,128)S(1)}, f32[88,768]{1,0:T(8,128)S(1)}, u32[]{:S(2)}, u32[]{:S(2)}) collective-permute-start(f32[88,768]{1,0:T(8,128)S(1)} %get-tuple-element.69), channel_id=1, source_target_pairs={{0,8},{8,0},{16,24},{24,16},{32,40},{40,32},{48,56},{56,48},{64,72... | collective-permute-start | bytes 811016 | tf_op jit(solution)/shard_map/ppermute | solution.py:579
  52.9 0.7 collective-permute-start.11
  53.6 20.7 %all_to_all.11 = f32[128,1,128]{2,1,0:T(1,128)S(1)} all-to-all(f32[128,1,128]{2,1,0:T(1,128)S(1)} %bitcast.6), channel_id=1, replica_groups=mesh['gx'=16,'gy'=8] {'gx','gy'}, dimensions={0} | all-to-all | bytes 131072 | tf_op jit(solution)/shard_map/all_to_all | solution.py:727
  74.3 2.6 %finish.1 = (f32[3,8,32,768]{3,2,1,0:T(8,128)}, f32[3,8,32,768]{3,2,1,0:T(8,128)}) custom-call(f32[3,8,16,768]{3,2,1,0:T(8,128)S(1)} %get-tuple-element.64.kmid_ref.refs_0_, f32[3,8,16,768]{3,2,1,0:T(8,128)S(1)} %get-tuple-element.61.refs_13_.kedge_ref.refs_1_, f32[3,8,16,768]{3,2,1,0:T(8,128)S(1)} %get-tuple-element.65.refs_2_, ...), custom_call_target="tpu_custom_call" | custom-call | flops 16000000 | bytes 10000000 | tf_op jit(solution)/shard_map/finish/pallas_call | solution.py:633
  (34 shorter events, 0.2 us)
Async XLA Ops:
  0.6 1.7 %copy-start = (f32[3,8,32,768]{3,2,1,0:T(8,128)S(1)}, f32[3,8,32,768]{3,2,1,0:T(8,128)}, u32[]{:S(2)}) copy-start(f32[3,8,32,768]{3,2,1,0:T(8,128)} %refs_1_.5) | copy-start | bytes 7077892
  2.3 7.5 %copy-start.1 = (f32[3,8,32,768]{3,2,1,0:T(8,128)S(1)}, f32[3,8,32,768]{3,2,1,0:T(8,128)}, u32[]{:S(2)}) copy-start(f32[3,8,32,768]{3,2,1,0:T(8,128)} %refs_1_.5) | copy-start | bytes 7077892
  2.4 5.3 %collective-permute-start = (f32[3,8,768]{2,1,0:T(8,128)S(1)}, f32[3,8,768]{2,1,0:T(8,128)S(1)}, u32[]{:S(2)}, u32[]{:S(2)}) collective-permute-start(f32[3,8,768]{2,1,0:T(8,128)S(1)} %get-tuple-element.40), channel_id=1, source_target_pairs={{0,1},{1,0},{2,3},{3,2},{4,5},{5,4},{6,7},{7,6},{8,9},{9,8},{10,11... | collective-permute-start | bytes 221192 | tf_op jit(solution)/shard_map/ppermute | solution.py:579
  3.9 6.0 %collective-permute-start.1 = (f32[3,8,768]{2,1,0:T(8,128)S(1)}, f32[3,8,768]{2,1,0:T(8,128)S(1)}, u32[]{:S(2)}, u32[]{:S(2)}) collective-permute-start(f32[3,8,768]{2,1,0:T(8,128)S(1)} %get-tuple-element.41), channel_id=1, source_target_pairs={{1,2},{2,1},{3,4},{4,3},{5,6},{6,5},{9,10},{10,9},{11,12},{12,11},... | collective-permute-start | bytes 221192 | tf_op jit(solution)/shard_map/ppermute | solution.py:578
  7.6 4.5 %copy-start.4 = (bf16[96,768]{1,0:T(8,128)(2,1)S(1)}, bf16[96,768]{1,0:T(8,128)(2,1)}, u32[]{:S(2)}) copy-start(bf16[96,768]{1,0:T(8,128)(2,1)} %constant.73.clone.widen_ref) | copy-start | bytes 442372
  7.6 4.5 %copy-start.5 = (f32[8,768]{1,0:T(8,128)S(1)}, f32[8,768]{1,0:T(8,128)}, u32[]{:S(2)}) copy-start(f32[8,768]{1,0:T(8,128)} %constant.74.clone.weight_ref) | copy-start | bytes 73732
  7.6 4.5 %copy-start.6 = (s32[1,4,96]{2,1,0:T(4,128)S(1)}, s32[1,4,96]{2,1,0:T(4,128)}, u32[]{:S(2)}) copy-start(s32[1,4,96]{2,1,0:T(4,128)} %param.8) | copy-start | bytes 4612
  7.7 4.7 %copy-start.7 = (s32[8,32]{1,0:T(8,128)S(1)}, s32[8,32]{1,0:T(8,128)}, u32[]{:S(2)}) copy-start(s32[8,32]{1,0:T(8,128)} %param.9) | copy-start | bytes 3076
  7.7 4.9 %copy-start.2 = (bf16[2,256,256]{2,1,0:T(8,128)(2,1)S(1)}, bf16[2,256,256]{2,1,0:T(8,128)(2,1)}, u32[]{:S(2)}) copy-start(bf16[2,256,256]{2,1,0:T(8,128)(2,1)} %constant.75.clone.refs_6_.refs_8_) | copy-start | bytes 786436
  7.7 4.9 %copy-start.3 = (f32[2,8,8,128]{3,2,1,0:T(8,128)S(1)}, f32[2,8,8,128]{3,2,1,0:T(8,128)}, u32[]{:S(2)}) copy-start(f32[2,8,8,128]{3,2,1,0:T(8,128)} %constant.76.clone.refs_7_.refs_9_) | copy-start | bytes 196612
  10.0 9.8 %collective-permute-start.2 = (f32[88,768]{1,0:T(8,128)S(1)}, f32[88,768]{1,0:T(8,128)S(1)}, u32[]{:S(2)}, u32[]{:S(2)}) collective-permute-start(f32[88,768]{1,0:T(8,128)S(1)} %get-tuple-element.42), channel_id=1, source_target_pairs={{0,8},{8,0},{16,24},{24,16},{32,40},{40,32},{48,56},{56,48},{64,72... | collective-permute-start | bytes 811016 | tf_op jit(solution)/shard_map/ppermute | solution.py:579
  11.5 8.4 %collective-permute-start.3 = (f32[88,768]{1,0:T(8,128)S(1)}, f32[88,768]{1,0:T(8,128)S(1)}, u32[]{:S(2)}, u32[]{:S(2)}) collective-permute-start(f32[88,768]{1,0:T(8,128)S(1)} %get-tuple-element.43), channel_id=1, source_target_pairs={{8,16},{16,8},{24,32},{32,24},{40,48},{48,40},{56,64},{64,56},{72,... | collective-permute-start | bytes 811016 | tf_op jit(solution)/shard_map/ppermute | solution.py:578
  21.6 5.8 %collective-permute-start.4 = (f32[3,8,768]{2,1,0:T(8,128)S(1)}, f32[3,8,768]{2,1,0:T(8,128)S(1)}, u32[]{:S(2)}, u32[]{:S(2)}) collective-permute-start(f32[3,8,768]{2,1,0:T(8,128)S(1)} %get-tuple-element.53), channel_id=1, source_target_pairs={{0,1},{1,0},{2,3},{3,2},{4,5},{5,4},{6,7},{7,6},{8,9},{9,8},{10,11... | collective-permute-start | bytes 221192 | tf_op jit(solution)/shard_map/ppermute | solution.py:579
  21.7 5.7 %collective-permute-start.5 = (f32[3,8,768]{2,1,0:T(8,128)S(1)}, f32[3,8,768]{2,1,0:T(8,128)S(1)}, u32[]{:S(2)}, u32[]{:S(2)}) collective-permute-start(f32[3,8,768]{2,1,0:T(8,128)S(1)} %get-tuple-element.54), channel_id=1, source_target_pairs={{1,2},{2,1},{3,4},{4,3},{5,6},{6,5},{9,10},{10,9},{11,12},{12,11},... | collective-permute-start | bytes 221192 | tf_op jit(solution)/shard_map/ppermute | solution.py:578
  27.6 11.8 %collective-permute-start.6 = (f32[88,768]{1,0:T(8,128)S(1)}, f32[88,768]{1,0:T(8,128)S(1)}, u32[]{:S(2)}, u32[]{:S(2)}) collective-permute-start(f32[88,768]{1,0:T(8,128)S(1)} %get-tuple-element.55), channel_id=1, source_target_pairs={{0,8},{8,0},{16,24},{24,16},{32,40},{40,32},{48,56},{56,48},{64,72... | collective-permute-start | bytes 811016 | tf_op jit(solution)/shard_map/ppermute | solution.py:579
  31.4 7.9 %collective-permute-start.7 = (f32[88,768]{1,0:T(8,128)S(1)}, f32[88,768]{1,0:T(8,128)S(1)}, u32[]{:S(2)}, u32[]{:S(2)}) collective-permute-start(f32[88,768]{1,0:T(8,128)S(1)} %get-tuple-element.56), channel_id=1, source_target_pairs={{8,16},{16,8},{24,32},{32,24},{40,48},{48,40},{56,64},{64,56},{72,... | collective-permute-start | bytes 811016 | tf_op jit(solution)/shard_map/ppermute | solution.py:578
  41.1 7.2 %collective-permute-start.8 = (f32[3,8,768]{2,1,0:T(8,128)S(1)}, f32[3,8,768]{2,1,0:T(8,128)S(1)}, u32[]{:S(2)}, u32[]{:S(2)}) collective-permute-start(f32[3,8,768]{2,1,0:T(8,128)S(1)} %get-tuple-element.66), channel_id=1, source_target_pairs={{0,1},{1,0},{2,3},{3,2},{4,5},{5,4},{6,7},{7,6},{8,9},{9,8},{10,11... | collective-permute-start | bytes 221192 | tf_op jit(solution)/shard_map/ppermute | solution.py:579
  41.2 7.1 %collective-permute-start.9 = (f32[3,8,768]{2,1,0:T(8,128)S(1)}, f32[3,8,768]{2,1,0:T(8,128)S(1)}, u32[]{:S(2)}, u32[]{:S(2)}) collective-permute-start(f32[3,8,768]{2,1,0:T(8,128)S(1)} %get-tuple-element.67), channel_id=1, source_target_pairs={{1,2},{2,1},{3,4},{4,3},{5,6},{6,5},{9,10},{10,9},{11,12},{12,11},... | collective-permute-start | bytes 221192 | tf_op jit(solution)/shard_map/ppermute | solution.py:578
  48.5 25.8 %collective-permute-start.10 = (f32[88,768]{1,0:T(8,128)S(1)}, f32[88,768]{1,0:T(8,128)S(1)}, u32[]{:S(2)}, u32[]{:S(2)}) collective-permute-start(f32[88,768]{1,0:T(8,128)S(1)} %get-tuple-element.69), channel_id=1, source_target_pairs={{0,8},{8,0},{16,24},{24,16},{32,40},{40,32},{48,56},{56,48},{64,72... | collective-permute-start | bytes 811016 | tf_op jit(solution)/shard_map/ppermute | solution.py:579
  52.9 21.4 %collective-permute-start.11 = (f32[88,768]{1,0:T(8,128)S(1)}, f32[88,768]{1,0:T(8,128)S(1)}, u32[]{:S(2)}, u32[]{:S(2)}) collective-permute-start(f32[88,768]{1,0:T(8,128)S(1)} %get-tuple-element.70), channel_id=1, source_target_pairs={{8,16},{16,8},{24,32},{32,24},{40,48},{48,40},{56,64},{64,56},{72,... | collective-permute-start | bytes 811016 | tf_op jit(solution)/shard_map/ppermute | solution.py:578

commit v5 on v4

--- a/solution.py
+++ b/solution.py
@@ -331,10 +331,6 @@
         lanes = slice(tile * LANES, (tile + 1) * LANES)
         flat = add_ref[:, :, :, lanes].reshape(comps * 2 * size_y, LANES)
         grad_ref[:, :, :, lanes] = along_z(flat, zmat_ref[0]).reshape(comps, 2, size_y, LANES)
-
-    @pl.loop(0, n_tile)
-    def _(tile):
-        lanes = pl.ds(pl.multiple_of(tile * LANES, LANES), LANES)
         for place, elem in enumerate(elems):
             base = place * NODES
             sub = slice(base, base + NODES)
@@ -368,14 +364,11 @@
                     keep_ref[3 + c, end, sub, lanes] = column_sum(
                         cols, lambda b: side_ref[c, end, b : b + 1, :]
                     )
-
-    for tile in range(n_tile):
-        lanes = slice(tile * LANES, (tile + 1) * LANES)
         flat = zin_ref[:, :, :, lanes].reshape(5 * 2 * size_y, LANES)
         zout_ref[:, :, :, lanes] = along_z(flat, zmat_ref[1]).reshape(5, 2, size_y, LANES)
 
     def tile_energy(tile, energy):
-        lanes = pl.ds(pl.multiple_of(tile * LANES, LANES), LANES)
+        lanes = slice(tile * LANES, (tile + 1) * LANES)
         if not outer:
             for plane in range(planes):
                 for c in range(comps):
@@ -419,7 +412,9 @@
                             energy = energy + value * vector
         return energy
 
-    energy = lax.fori_loop(0, n_tile, tile_energy, jnp.zeros((NODES, LANES), jnp.float32))
+    energy = jnp.zeros((NODES, LANES), jnp.float32)
+    for tile in range(n_tile):
+        energy = tile_energy(tile, energy)
     if outer:
         put_rows(
             lambda comp, plane: k_ref[comp, plane, 0:1, :],

time: 77.3 us -> 76.9 us (level)
  Pallas kernels: 26.2 us -> 25.3 us
    pallas_call x14, Pallas kernels: 26 us -> 25.2 us  [call(): pl.pallas_call(kernel, in_specs=[whole] * len(args), out_specs=[out_spec]...]
  transfers between devices with their start and end apart: 12 -> 12, of which waited for: 1 -> 2; matrix products, arithmetic and copies ran while one was open for 0% -> 0% of each run, Pallas kernels for 25% -> 25%
where the time goes in v5:
time: 76.9 us; the launch traced here: 76.6 us
  Pallas kernels  25.3 us (33%)
  starting transfers between devices  24.9 us (32%)
  blocking collectives  20.8 us (27%)
  waiting for transfers between devices  2.4 us (3%)
  local copies, waits for them, and re-layouts  1.79 us (2%)
  between operations  1.15 us (1%)
    pallas_call x14, Pallas kernels, call(): pl.pallas_call(kernel, in_specs=[whole] * len(args), out_specs=[out_spec]...  25.2 us
    all_to_all x1, blocking collectives, local(): sums = lax.all_to_all(sums, axes, 0, 0, tiled=True)  20.8 us
    ppermute x6, starting transfers between devices, swap(): far = lax.ppermute(far_out, axis, outer)  13.6 us
    ppermute x6, starting transfers between devices, swap(): near = lax.ppermute(near_out, axis, inner)  11.4 us
    ppermute x6, waiting for transfers between devices, swap(): far = lax.ppermute(far_out, axis, outer)  2.38 us
    unnamed x16, local copies, waits for them, and re-layouts  1.7 us
  transfers between devices with their start and end apart: 12, of which 2 were waited for; matrix products, arithmetic and copies ran while one was open for 0% of the time, Pallas kernels for 25%

profile of v5, /device:TPU:1, one launch (start us, length us, event | category | flops | bytes accessed | tf_op | source)
XLA Modules:
  0.0 76.6 jit_solution(9719683679539408777)
XLA Ops:
  0.6 1.7 %copy-done = f32[3,8,32,768]{3,2,1,0:T(8,128)S(1)} copy-done((f32[3,8,32,768]{3,2,1,0:T(8,128)S(1)}, f32[3,8,32,768]{3,2,1,0:T(8,128)}, u32[]{:S(2)}) %copy-start) | copy-done | bytes 2359320
  2.4 1.5 %collective-permute-start = (f32[3,8,768]{2,1,0:T(8,128)S(1)}, f32[3,8,768]{2,1,0:T(8,128)S(1)}, u32[]{:S(2)}, u32[]{:S(2)}) collective-permute-start(f32[3,8,768]{2,1,0:T(8,128)S(1)} %get-tuple-element.40), channel_id=1, source_target_pairs={{0,1},{1,0},{2,3},{3,2},{4,5},{5,4},{6,7},{7,6},{8,9},{9,8},{10,11... | collective-permute-start | bytes 221192 | tf_op jit(solution)/shard_map/ppermute | solution.py:574
  3.9 3.7 %collective-permute-start.1 = (f32[3,8,768]{2,1,0:T(8,128)S(1)}, f32[3,8,768]{2,1,0:T(8,128)S(1)}, u32[]{:S(2)}, u32[]{:S(2)}) collective-permute-start(f32[3,8,768]{2,1,0:T(8,128)S(1)} %get-tuple-element.41), channel_id=1, source_target_pairs={{1,2},{2,1},{3,4},{4,3},{5,6},{6,5},{9,10},{10,9},{11,12},{12,11},... | collective-permute-start | bytes 221192 | tf_op jit(solution)/shard_map/ppermute | solution.py:573
  7.7 2.1 %collective-permute-done.1.refs_3_ = f32[3,8,768]{2,1,0:T(8,128)S(1)} collective-permute-done((f32[3,8,768]{2,1,0:T(8,128)S(1)}, f32[3,8,768]{2,1,0:T(8,128)S(1)}, u32[]{:S(2)}, u32[]{:S(2)}) %collective-permute-start.1) | collective-permute-done | bytes 73760 | tf_op jit(solution)/shard_map/ppermute | solution.py:573
  9.8 0.2 faces.3
  10.0 1.4 %collective-permute-start.2 = (f32[88,768]{1,0:T(8,128)S(1)}, f32[88,768]{1,0:T(8,128)S(1)}, u32[]{:S(2)}, u32[]{:S(2)}) collective-permute-start(f32[88,768]{1,0:T(8,128)S(1)} %get-tuple-element.42), channel_id=1, source_target_pairs={{0,8},{8,0},{16,24},{24,16},{32,40},{40,32},{48,56},{56,48},{64,72... | collective-permute-start | bytes 811016 | tf_op jit(solution)/shard_map/ppermute | solution.py:574
  11.5 0.7 collective-permute-start.3
  12.2 0.1 scale.1.refs_3_.refs_5_
  12.3 0.1 multiply_subtract_fusion.refs_2_.refs_4_.free_ref.refs_7_
  12.5 0.1 mul.50.refs_4_.refs_6_
  12.6 3.6 %middle.2 = (f32[3,8,16,768]{3,2,1,0:T(8,128)S(1)}, f32[3,8,16,768]{3,2,1,0:T(8,128)S(1)}, f32[8,128]{1,0:T(8,128)S(1)}) custom-call(f32[3,8,32,768]{3,2,1,0:T(8,128)S(1)} %copy-done.1, f32[3,8,32,768]{3,2,1,0:T(8,128)S(1)} %copy-done.1, f32[8,32,128]{2,1,0:T(8,128)S(1)} %multiply_subtract_fusion.refs_2_.refs_4_.free_ref.refs_7_, ...), custom_call_target="tpu_custom_call" | custom-call | flops 20000000 | bytes 12500000 | tf_op jit(solution)/shard_map/middle/pallas_call | solution.py:628
  16.2 3.6 %edges.2 = (f32[3,8,16,768]{3,2,1,0:T(8,128)S(1)}, f32[3,8,16,768]{3,2,1,0:T(8,128)S(1)}, f32[8,128]{1,0:T(8,128)S(1)}) custom-call(f32[3,8,32,768]{3,2,1,0:T(8,128)S(1)} %copy-done.1, f32[3,8,32,768]{3,2,1,0:T(8,128)S(1)} %copy-done.1, f32[3,8,768]{2,1,0:T(8,128)S(1)} %collective-permute-done.refs_2_, f32[3,8,768]{2,1,0:T(8,128)S(1)} %collective-permute-done.1.refs_3_, ...), custom_call_target="tpu_custom_call" | custom-call | flops 20000000 | bytes 12500000 | tf_op jit(solution)/shard_map/edges/pallas_call | solution.py:628
  19.8 1.5 %update_edges.2 = (f32[3,8,16,768]{3,2,1,0:T(8,128)S(1)}, f32[3,2,16,768]{3,2,1,0:T(8,128)S(1)}, f32[3,8,768]{2,1,0:T(8,128)S(1)}, f32[3,8,768]{2,1,0:T(8,128)S(1)}) custom-call(f32[3,8,16,768]{3,2,1,0:T(8,128)S(1)} %get-tuple-element.46.refs_0_.refs_12_.refs_9_, f32[3,8,16,768]{3,2,1,0:T(8,128)S(1)} %get-tuple-element.47.refs_1_, ...), custom_call_target="tpu_custom_call" | custom-call | flops 8000000 | bytes 5000000 | tf_op jit(solution)/shard_map/update_edges/pallas_call | solution.py:628
  21.4 0.1 collective-permute-start.4
  21.5 3.6 %collective-permute-start.5 = (f32[3,8,768]{2,1,0:T(8,128)S(1)}, f32[3,8,768]{2,1,0:T(8,128)S(1)}, u32[]{:S(2)}, u32[]{:S(2)}) collective-permute-start(f32[3,8,768]{2,1,0:T(8,128)S(1)} %get-tuple-element.54), channel_id=1, source_target_pairs={{1,2},{2,1},{3,4},{4,3},{5,6},{6,5},{9,10},{10,9},{11,12},{12,11},... | collective-permute-start | bytes 221192 | tf_op jit(solution)/shard_map/ppermute | solution.py:573
  25.1 1.8 %update_middle.2 = (f32[3,8,16,768]{3,2,1,0:T(8,128)S(1)}, f32[3,2,16,768]{3,2,1,0:T(8,128)S(1)}, f32[4,8,128]{2,1,0:T(8,128)S(1)}) custom-call(f32[3,8,16,768]{3,2,1,0:T(8,128)S(1)} %get-tuple-element.38.refs_0_.refs_8_, f32[3,8,16,768]{3,2,1,0:T(8,128)S(1)} %get-tuple-element.39.refs_1_, f32[88,768]{1,0:T(8,128)S(1)} %collective-permute-done.2.refs_2_, ...), custom_call_target="tpu_custom_call" | custom-call | flops 8000000 | bytes 5000000 | tf_op jit(solution)/shard_map/update_middle/pallas_call | solution.py:628
  26.9 0.2 collective-permute-done.5.refs_3_
  27.1 0.2 faces.4
  27.3 3.8 %collective-permute-start.6 = (f32[88,768]{1,0:T(8,128)S(1)}, f32[88,768]{1,0:T(8,128)S(1)}, u32[]{:S(2)}, u32[]{:S(2)}) collective-permute-start(f32[88,768]{1,0:T(8,128)S(1)} %get-tuple-element.55), channel_id=1, source_target_pairs={{0,8},{8,0},{16,24},{24,16},{32,40},{40,32},{48,56},{56,48},{64,72... | collective-permute-start | bytes 811016 | tf_op jit(solution)/shard_map/ppermute | solution.py:574
  31.1 0.8 %collective-permute-start.7 = (f32[88,768]{1,0:T(8,128)S(1)}, f32[88,768]{1,0:T(8,128)S(1)}, u32[]{:S(2)}, u32[]{:S(2)}) collective-permute-start(f32[88,768]{1,0:T(8,128)S(1)} %get-tuple-element.56), channel_id=1, source_target_pairs={{8,16},{16,8},{24,32},{32,24},{40,48},{48,40},{56,64},{64,56},{72,... | collective-permute-start | bytes 811016 | tf_op jit(solution)/shard_map/ppermute | solution.py:573
  32.0 3.6 %middle.3 = (f32[3,8,16,768]{3,2,1,0:T(8,128)S(1)}, f32[3,8,16,768]{3,2,1,0:T(8,128)S(1)}, f32[8,128]{1,0:T(8,128)S(1)}) custom-call(f32[3,8,16,768]{3,2,1,0:T(8,128)S(1)} %get-tuple-element.50.refs_0_, f32[3,8,16,768]{3,2,1,0:T(8,128)S(1)} %get-tuple-element.48.refs_13_.refs_1_, f32[8,32,128]{2,1,0:T(8,128)S(1)} %multiply_subtract_fusion.refs_2_.refs_4_.free_ref.refs_7_, ...), custom_call_target="tpu_custom_call" | custom-call | flops 20000000 | bytes 12500000 | tf_op jit(solution)/shard_map/middle/pallas_call | solution.py:628
  35.6 3.6 %edges.3 = (f32[3,8,16,768]{3,2,1,0:T(8,128)S(1)}, f32[3,8,16,768]{3,2,1,0:T(8,128)S(1)}, f32[8,128]{1,0:T(8,128)S(1)}) custom-call(f32[3,8,16,768]{3,2,1,0:T(8,128)S(1)} %get-tuple-element.50.refs_0_, f32[3,8,16,768]{3,2,1,0:T(8,128)S(1)} %get-tuple-element.48.refs_13_.refs_1_, f32[3,8,768]{2,1,0:T(8,128)S(1)} %collective-permute-done.4.refs_2_, ...), custom_call_target="tpu_custom_call" | custom-call | flops 20000000 | bytes 12500000 | tf_op jit(solution)/shard_map/edges/pallas_call | solution.py:628
  39.2 1.5 %update_edges.3 = (f32[3,8,16,768]{3,2,1,0:T(8,128)S(1)}, f32[3,2,16,768]{3,2,1,0:T(8,128)S(1)}, f32[3,8,768]{2,1,0:T(8,128)S(1)}, f32[3,8,768]{2,1,0:T(8,128)S(1)}) custom-call(f32[3,8,16,768]{3,2,1,0:T(8,128)S(1)} %get-tuple-element.59.refs_0_.refs_12_.refs_13_, f32[3,8,16,768]{3,2,1,0:T(8,128)S(1)} %get-tuple-element.60.refs_1_, ...), custom_call_target="tpu_custom_call" | custom-call | flops 8000000 | bytes 5000000 | tf_op jit(solution)/shard_map/update_edges/pallas_call | solution.py:628
  40.8 0.1 collective-permute-start.8
  40.9 4.1 %collective-permute-start.9 = (f32[3,8,768]{2,1,0:T(8,128)S(1)}, f32[3,8,768]{2,1,0:T(8,128)S(1)}, u32[]{:S(2)}, u32[]{:S(2)}) collective-permute-start(f32[3,8,768]{2,1,0:T(8,128)S(1)} %get-tuple-element.67), channel_id=1, source_target_pairs={{1,2},{2,1},{3,4},{4,3},{5,6},{6,5},{9,10},{10,9},{11,12},{12,11},... | collective-permute-start | bytes 221192 | tf_op jit(solution)/shard_map/ppermute | solution.py:573
  45.0 2.0 %update_middle.3 = (f32[3,8,16,768]{3,2,1,0:T(8,128)S(1)}, f32[3,2,16,768]{3,2,1,0:T(8,128)S(1)}, f32[128,128]{1,0:T(8,128)S(1)}) custom-call(f32[3,8,16,768]{3,2,1,0:T(8,128)S(1)} %get-tuple-element.51.refs_0_.refs_12_, f32[3,8,16,768]{3,2,1,0:T(8,128)S(1)} %get-tuple-element.52.refs_1_, f32[88,768]{1,0:T(8,128)S(1)} %collective-permute-done.6.refs_2_, ...), custom_call_target="tpu_custom_call" | custom-call | flops 8000000 | bytes 5000000 | tf_op jit(solution)/shard_map/update_middle/pallas_call | solution.py:628
  47.0 0.7 assemble.1
  47.7 0.2 faces.5
  47.9 4.4 %collective-permute-start.10 = (f32[88,768]{1,0:T(8,128)S(1)}, f32[88,768]{1,0:T(8,128)S(1)}, u32[]{:S(2)}, u32[]{:S(2)}) collective-permute-start(f32[88,768]{1,0:T(8,128)S(1)} %get-tuple-element.69), channel_id=1, source_target_pairs={{0,8},{8,0},{16,24},{24,16},{32,40},{40,32},{48,56},{56,48},{64,72... | collective-permute-start | bytes 811016 | tf_op jit(solution)/shard_map/ppermute | solution.py:574
  52.3 0.7 collective-permute-start.11
  53.0 20.8 %all_to_all.11 = f32[128,1,128]{2,1,0:T(1,128)S(1)} all-to-all(f32[128,1,128]{2,1,0:T(1,128)S(1)} %bitcast.6), channel_id=1, replica_groups=mesh['gx'=16,'gy'=8] {'gx','gy'}, dimensions={0} | all-to-all | bytes 131072 | tf_op jit(solution)/shard_map/all_to_all | solution.py:722
  73.9 2.6 %finish.1 = (f32[3,8,32,768]{3,2,1,0:T(8,128)}, f32[3,8,32,768]{3,2,1,0:T(8,128)}) custom-call(f32[3,8,16,768]{3,2,1,0:T(8,128)S(1)} %get-tuple-element.64.kmid_ref.refs_0_, f32[3,8,16,768]{3,2,1,0:T(8,128)S(1)} %get-tuple-element.61.refs_13_.kedge_ref.refs_1_, f32[3,8,16,768]{3,2,1,0:T(8,128)S(1)} %get-tuple-element.65.refs_2_, ...), custom_call_target="tpu_custom_call" | custom-call | flops 16000000 | bytes 10000000 | tf_op jit(solution)/shard_map/finish/pallas_call | solution.py:628
  (34 shorter events, 0.2 us)
Async XLA Ops:
  0.6 1.7 %copy-start = (f32[3,8,32,768]{3,2,1,0:T(8,128)S(1)}, f32[3,8,32,768]{3,2,1,0:T(8,128)}, u32[]{:S(2)}) copy-start(f32[3,8,32,768]{3,2,1,0:T(8,128)} %refs_1_.5) | copy-start | bytes 7077892
  2.3 7.5 %copy-start.1 = (f32[3,8,32,768]{3,2,1,0:T(8,128)S(1)}, f32[3,8,32,768]{3,2,1,0:T(8,128)}, u32[]{:S(2)}) copy-start(f32[3,8,32,768]{3,2,1,0:T(8,128)} %refs_1_.5) | copy-start | bytes 7077892
  2.4 5.3 %collective-permute-start = (f32[3,8,768]{2,1,0:T(8,128)S(1)}, f32[3,8,768]{2,1,0:T(8,128)S(1)}, u32[]{:S(2)}, u32[]{:S(2)}) collective-permute-start(f32[3,8,768]{2,1,0:T(8,128)S(1)} %get-tuple-element.40), channel_id=1, source_target_pairs={{0,1},{1,0},{2,3},{3,2},{4,5},{5,4},{6,7},{7,6},{8,9},{9,8},{10,11... | collective-permute-start | bytes 221192 | tf_op jit(solution)/shard_map/ppermute | solution.py:574
  3.9 6.0 %collective-permute-start.1 = (f32[3,8,768]{2,1,0:T(8,128)S(1)}, f32[3,8,768]{2,1,0:T(8,128)S(1)}, u32[]{:S(2)}, u32[]{:S(2)}) collective-permute-start(f32[3,8,768]{2,1,0:T(8,128)S(1)} %get-tuple-element.41), channel_id=1, source_target_pairs={{1,2},{2,1},{3,4},{4,3},{5,6},{6,5},{9,10},{10,9},{11,12},{12,11},... | collective-permute-start | bytes 221192 | tf_op jit(solution)/shard_map/ppermute | solution.py:573
  7.6 4.5 %copy-start.4 = (bf16[96,768]{1,0:T(8,128)(2,1)S(1)}, bf16[96,768]{1,0:T(8,128)(2,1)}, u32[]{:S(2)}) copy-start(bf16[96,768]{1,0:T(8,128)(2,1)} %constant.73.clone.widen_ref) | copy-start | bytes 442372
  7.6 4.5 %copy-start.5 = (f32[8,768]{1,0:T(8,128)S(1)}, f32[8,768]{1,0:T(8,128)}, u32[]{:S(2)}) copy-start(f32[8,768]{1,0:T(8,128)} %constant.74.clone.weight_ref) | copy-start | bytes 73732
  7.6 4.5 %copy-start.6 = (s32[1,4,96]{2,1,0:T(4,128)S(1)}, s32[1,4,96]{2,1,0:T(4,128)}, u32[]{:S(2)}) copy-start(s32[1,4,96]{2,1,0:T(4,128)} %param.8) | copy-start | bytes 4612
  7.7 4.7 %copy-start.7 = (s32[8,32]{1,0:T(8,128)S(1)}, s32[8,32]{1,0:T(8,128)}, u32[]{:S(2)}) copy-start(s32[8,32]{1,0:T(8,128)} %param.9) | copy-start | bytes 3076
  7.7 4.9 %copy-start.2 = (bf16[2,256,256]{2,1,0:T(8,128)(2,1)S(1)}, bf16[2,256,256]{2,1,0:T(8,128)(2,1)}, u32[]{:S(2)}) copy-start(bf16[2,256,256]{2,1,0:T(8,128)(2,1)} %constant.75.clone.refs_6_.refs_8_) | copy-start | bytes 786436
  7.7 4.9 %copy-start.3 = (f32[2,8,8,128]{3,2,1,0:T(8,128)S(1)}, f32[2,8,8,128]{3,2,1,0:T(8,128)}, u32[]{:S(2)}) copy-start(f32[2,8,8,128]{3,2,1,0:T(8,128)} %constant.76.clone.refs_7_.refs_9_) | copy-start | bytes 196612
  10.0 9.8 %collective-permute-start.2 = (f32[88,768]{1,0:T(8,128)S(1)}, f32[88,768]{1,0:T(8,128)S(1)}, u32[]{:S(2)}, u32[]{:S(2)}) collective-permute-start(f32[88,768]{1,0:T(8,128)S(1)} %get-tuple-element.42), channel_id=1, source_target_pairs={{0,8},{8,0},{16,24},{24,16},{32,40},{40,32},{48,56},{56,48},{64,72... | collective-permute-start | bytes 811016 | tf_op jit(solution)/shard_map/ppermute | solution.py:574
  11.5 8.4 %collective-permute-start.3 = (f32[88,768]{1,0:T(8,128)S(1)}, f32[88,768]{1,0:T(8,128)S(1)}, u32[]{:S(2)}, u32[]{:S(2)}) collective-permute-start(f32[88,768]{1,0:T(8,128)S(1)} %get-tuple-element.43), channel_id=1, source_target_pairs={{8,16},{16,8},{24,32},{32,24},{40,48},{48,40},{56,64},{64,56},{72,... | collective-permute-start | bytes 811016 | tf_op jit(solution)/shard_map/ppermute | solution.py:573
  21.4 5.5 %collective-permute-start.4 = (f32[3,8,768]{2,1,0:T(8,128)S(1)}, f32[3,8,768]{2,1,0:T(8,128)S(1)}, u32[]{:S(2)}, u32[]{:S(2)}) collective-permute-start(f32[3,8,768]{2,1,0:T(8,128)S(1)} %get-tuple-element.53), channel_id=1, source_target_pairs={{0,1},{1,0},{2,3},{3,2},{4,5},{5,4},{6,7},{7,6},{8,9},{9,8},{10,11... | collective-permute-start | bytes 221192 | tf_op jit(solution)/shard_map/ppermute | solution.py:574
  21.5 5.7 %collective-permute-start.5 = (f32[3,8,768]{2,1,0:T(8,128)S(1)}, f32[3,8,768]{2,1,0:T(8,128)S(1)}, u32[]{:S(2)}, u32[]{:S(2)}) collective-permute-start(f32[3,8,768]{2,1,0:T(8,128)S(1)} %get-tuple-element.54), channel_id=1, source_target_pairs={{1,2},{2,1},{3,4},{4,3},{5,6},{6,5},{9,10},{10,9},{11,12},{12,11},... | collective-permute-start | bytes 221192 | tf_op jit(solution)/shard_map/ppermute | solution.py:573
  27.3 11.9 %collective-permute-start.6 = (f32[88,768]{1,0:T(8,128)S(1)}, f32[88,768]{1,0:T(8,128)S(1)}, u32[]{:S(2)}, u32[]{:S(2)}) collective-permute-start(f32[88,768]{1,0:T(8,128)S(1)} %get-tuple-element.55), channel_id=1, source_target_pairs={{0,8},{8,0},{16,24},{24,16},{32,40},{40,32},{48,56},{56,48},{64,72... | collective-permute-start | bytes 811016 | tf_op jit(solution)/shard_map/ppermute | solution.py:574
  31.1 8.1 %collective-permute-start.7 = (f32[88,768]{1,0:T(8,128)S(1)}, f32[88,768]{1,0:T(8,128)S(1)}, u32[]{:S(2)}, u32[]{:S(2)}) collective-permute-start(f32[88,768]{1,0:T(8,128)S(1)} %get-tuple-element.56), channel_id=1, source_target_pairs={{8,16},{16,8},{24,32},{32,24},{40,48},{48,40},{56,64},{64,56},{72,... | collective-permute-start | bytes 811016 | tf_op jit(solution)/shard_map/ppermute | solution.py:573
  40.8 6.9 %collective-permute-start.8 = (f32[3,8,768]{2,1,0:T(8,128)S(1)}, f32[3,8,768]{2,1,0:T(8,128)S(1)}, u32[]{:S(2)}, u32[]{:S(2)}) collective-permute-start(f32[3,8,768]{2,1,0:T(8,128)S(1)} %get-tuple-element.66), channel_id=1, source_target_pairs={{0,1},{1,0},{2,3},{3,2},{4,5},{5,4},{6,7},{7,6},{8,9},{9,8},{10,11... | collective-permute-start | bytes 221192 | tf_op jit(solution)/shard_map/ppermute | solution.py:574
  40.9 6.8 %collective-permute-start.9 = (f32[3,8,768]{2,1,0:T(8,128)S(1)}, f32[3,8,768]{2,1,0:T(8,128)S(1)}, u32[]{:S(2)}, u32[]{:S(2)}) collective-permute-start(f32[3,8,768]{2,1,0:T(8,128)S(1)} %get-tuple-element.67), channel_id=1, source_target_pairs={{1,2},{2,1},{3,4},{4,3},{5,6},{6,5},{9,10},{10,9},{11,12},{12,11},... | collective-permute-start | bytes 221192 | tf_op jit(solution)/shard_map/ppermute | solution.py:573
  47.9 26.0 %collective-permute-start.10 = (f32[88,768]{1,0:T(8,128)S(1)}, f32[88,768]{1,0:T(8,128)S(1)}, u32[]{:S(2)}, u32[]{:S(2)}) collective-permute-start(f32[88,768]{1,0:T(8,128)S(1)} %get-tuple-element.69), channel_id=1, source_target_pairs={{0,8},{8,0},{16,24},{24,16},{32,40},{40,32},{48,56},{56,48},{64,72... | collective-permute-start | bytes 811016 | tf_op jit(solution)/shard_map/ppermute | solution.py:574
  52.3 21.5 %collective-permute-start.11 = (f32[88,768]{1,0:T(8,128)S(1)}, f32[88,768]{1,0:T(8,128)S(1)}, u32[]{:S(2)}, u32[]{:S(2)}) collective-permute-start(f32[88,768]{1,0:T(8,128)S(1)} %get-tuple-element.70), channel_id=1, source_target_pairs={{8,16},{16,8},{24,32},{32,24},{40,48},{48,40},{56,64},{64,56},{72,... | collective-permute-start | bytes 811016 | tf_op jit(solution)/shard_map/ppermute | solution.py:573
